TPU v7x, 32 devices: a whole 2x2x4 slice. The times are simulated.
32 devices in a mesh: frames: 4 (over y, x), height: 8 (over z, core).
Axes of the slice: x: 2, y: 2, z: 4, core: 2. Of those that a mesh axis runs over, the one named last changes fastest.
Arguments:
- latent: bfloat16 [4, 16, 160, 384], P('frames', 'height'), may hold values from -15 to 15
- first_gain: float32 [384], replicated, may hold values from 0.1 to 1.9
- first_shift: float32 [384], replicated, may hold values from -4 to 4
- query_weight: bfloat16 [384, 384], replicated
- key_weight: bfloat16 [384, 384], replicated
- value_weight: bfloat16 [384, 384], replicated, may hold values from -0.3125 to 0.3125
- out_weight: bfloat16 [384, 384], replicated, may hold values from -0.3125 to 0.3125
- out_bias: float32 [384], replicated, may hold values from -6 to 6
- second_gain: float32 [384], replicated, may hold values from 0.1 to 1.9
- second_shift: float32 [384], replicated, may hold values from -4 to 4
- up_weight: bfloat16 [3, 3, 3, 384, 384], replicated, may hold values from -0.15625 to 0.15625
- up_bias: float32 [384], replicated, may hold values from -6 to 6
Outputs:
- upsampled: bfloat16 [8, 32, 320, 384], P('frames', 'height')
All inputs are finite; a program needn't handle non-finite values.
Results may differ from a plain program's by a relative error of at most 0.013.
Values may be sent and summed in bfloat16 or wider, within the bound.
No kernel may reach another device: no remote copies, remote signals or barrier semaphores. Data moves between devices by JAX's collectives and lax.ppermute only.
A program may use at most 128 MiB of HBM per device.

v0:
```python
import jax
import jax.numpy as jnp
from jax import lax
from jax.sharding import PartitionSpec as P

GROUPS = 32


EPS = 1e-05


def passed_along(value, axis, steps):
    count = lax.axis_size(axis)
    initial, last = (max(0, -steps), min(count, count - steps))
    return lax.ppermute(value, axis, [(source, source + steps) for source in range(initial, last)])


def group_norm(value, gain, shift):
    floats = value.astype(jnp.float32)
    width = floats.shape[-1]
    per_group = width // GROUPS
    count = (
        floats.shape[0]
        * floats.shape[1]
        * floats.shape[2]
        * per_group
        * lax.axis_size("frames")
        * lax.axis_size("height")
    )

    def grouped(array):
        return jnp.sum(array, axis=(0, 1, 2)).reshape(GROUPS, per_group).sum(axis=-1)

    mean = lax.psum(grouped(floats), ("frames", "height")) / count
    centered = floats - jnp.repeat(mean, per_group)
    spread = lax.psum(grouped(centered * centered), ("frames", "height")) / count
    factor = gain * jnp.repeat(lax.rsqrt(spread + EPS), per_group)
    return centered * factor + shift


def upsample_taps(current, earlier, weight, bias):
    rows = current.shape[0] - 1
    cols = current.shape[1] - 1
    width = current.shape[2]
    time_taps = (((0, current), (2, earlier)), ((1, current),))
    space_taps = (((1, 0),), ((2, 0), (0, 1)))
    frame_list = []
    for odd_time in range(2):
        row_list = []
        for odd_row in range(2):
            col_list = []
            for odd_col in range(2):
                summed = jnp.zeros((rows * cols, width), jnp.float32)
                for time_tap, source in time_taps[odd_time]:
                    for row_tap, row_step in space_taps[odd_row]:
                        for col_tap, col_step in space_taps[odd_col]:
                            window = source[
                                row_step : row_step + rows, col_step : col_step + cols
                            ].reshape(-1, width)
                            summed = summed + jnp.dot(
                                window,
                                weight[time_tap, row_tap, col_tap],
                                preferred_element_type=jnp.float32,
                            )
                col_list.append((summed + bias).reshape(rows, cols, width))
            row_list.append(jnp.stack(col_list, axis=2).reshape(rows, 2 * cols, width))
        frame_list.append(jnp.stack(row_list, axis=1).reshape(2 * rows, 2 * cols, width))
    return jnp.stack(frame_list, axis=0)


def local(
    latent,
    first_gain,
    first_shift,
    query_weight,
    key_weight,
    value_weight,
    out_weight,
    out_bias,
    second_gain,
    second_shift,
    up_weight,
    up_bias,
):
    frames, rows, cols, width = latent.shape
    normed = group_norm(latent, first_gain, first_shift).astype(jnp.bfloat16)
    factor = width ** (-0.5)

    def project(block, weight):
        return jnp.dot(block.reshape(-1, width), weight, preferred_element_type=jnp.float32).astype(
            jnp.bfloat16
        )

    queries = project(normed, query_weight).reshape(frames, rows * cols, width)
    keys = project(normed, key_weight).reshape(frames, rows, cols, width)
    values = project(normed, value_weight).reshape(frames, rows, cols, width)
    absorb_keys = lax.all_gather(keys, "height", axis=1, tiled=True).reshape(frames, -1, width)
    absorb_values = lax.all_gather(values, "height", axis=1, tiled=True).reshape(frames, -1, width)
    highest = jnp.full((frames, rows * cols), -1e30, jnp.float32)
    scores = (
        jnp.einsum("fqc,fkc->fqk", queries, absorb_keys, preferred_element_type=jnp.float32)
        * factor
    )
    new_high = jnp.maximum(highest, jnp.max(scores, axis=-1))
    weights = jnp.exp(scores - new_high[..., None])
    totals = jnp.sum(weights, axis=-1)
    summed = jnp.einsum(
        "fqk,fkc->fqc",
        weights.astype(jnp.bfloat16),
        absorb_values,
        preferred_element_type=jnp.float32,
    )
    state = (new_high, totals, summed)
    highest, totals, summed = state
    attended = (summed / totals[..., None]).astype(jnp.bfloat16)
    branch = (
        jnp.dot(
            attended.reshape(-1, width), out_weight, preferred_element_type=jnp.float32
        ).reshape(latent.shape)
        + out_bias
    )
    mixed = (latent.astype(jnp.float32) + branch).astype(jnp.bfloat16)
    activated = jax.nn.silu(group_norm(mixed, second_gain, second_shift)).astype(jnp.bfloat16)
    cached = passed_along(activated, "frames", 1)
    earlier = jnp.concatenate([cached, activated[: frames - 1]], axis=0)
    paired = jnp.stack([activated, earlier], axis=0)
    below = passed_along(paired[:, :, :1], "height", -1)
    extended = jnp.concatenate([paired, below], axis=2)
    extended = jnp.pad(extended, ((0, 0), (0, 0), (0, 0), (0, 1), (0, 0)))
    outputs = [
        upsample_taps(extended[0, 0], extended[1, 0], up_weight, up_bias).astype(jnp.bfloat16)
    ]
    return jnp.stack(outputs, axis=0).reshape(2 * frames, 2 * rows, 2 * cols, width)


def solution(mesh):
    placed = (
        P("frames", "height", None, None),
        P(),
        P(),
        P(),
        P(),
        P(),
        P(),
        P(),
        P(),
        P(),
        P(),
        P(),
    )
    return jax.shard_map(
        local,
        mesh=mesh,
        in_specs=placed,
        out_specs=P("frames", "height", None, None),
        check_vma=False,
    )
```

profile of v0, /device:TPU:0, one launch (start us, length us, event | category | flops | bytes accessed | tf_op | source)
XLA Modules:
  0.0 282.6 jit_solution(7802551236630283915)
XLA Ops:
  6.5 1.1 convert_reduce_fusion
  7.8 42.0 %psum.28 = f32[32]{0:T(128)S(1)} all-reduce(f32[32]{0:T(128)S(1)} %reduce_sum.82), channel_id=1, replica_groups=mesh['frames'=4,'height'=8] {'frames','height'}, use_global_device_ids=true, to_apply=%region_2.0 | all-reduce | flops 32 | bytes 256 | tf_op jit(solution)/shard_map/psum | solution.py:34
  50.0 1.0 fusion.37
  51.3 40.2 %psum.29 = f32[32]{0:T(128)S(1)} all-reduce(f32[32]{0:T(128)S(1)} %reduce_sum.84), channel_id=1, replica_groups=mesh['frames'=4,'height'=8] {'frames','height'}, use_global_device_ids=true, to_apply=%region_5.0 | all-reduce | flops 32 | bytes 256 | tf_op jit(solution)/shard_map/psum | solution.py:36
  91.7 0.7 mul.40
  92.3 1.0 fusion.39
  93.4 2.0 convolution_convert_fusion.1
  95.4 2.0 convolution_convert_fusion
  97.4 26.7 %all-gather.3.cloned.1.call-done = bf16[1,16,160,384]{3,2,0,1:T(8,128)(2,1)} async-done(((bf16[1,2,160,384]{3,2,0,1:T(8,128)(2,1)}), bf16[1,16,160,384]{3,2,0,1:T(8,128)(2,1)}) %all-gather.3.cloned.1.call-update) | async-done | bytes 1966096 | tf_op jit(solution)/shard_map/all_gather | solution.py:97
  124.2 4.5 %fusion.104 = (f32[320]{0:T(512)S(1)}, f32[320,2560]{1,0:T(8,128)}) fusion(bf16[2560,384]{1,0:T(8,128)(2,1)} %bitcast.206, bf16[320,384]{1,0:T(8,128)(2,1)S(1)} %bitcast.195, bf16[384,384]{1,0:T(8,128)(2,1)S(1)} %copy-done), kind=kOutput, calls=%fused_computation.145 | convolution fusion | flops 725278400 | bytes 5784832 | tf_op jit(solution)/shard_map/fqc,fkc->fqk/dot_general | solution.py:101
  128.7 2.6 fusion
  131.3 22.1 %all-gather.5.cloned.1.call-done = bf16[1,16,160,384]{3,2,0,1:T(8,128)(2,1)} async-done(((bf16[1,2,160,384]{3,2,0,1:T(8,128)(2,1)}), bf16[1,16,160,384]{3,2,0,1:T(8,128)(2,1)}) %all-gather.5.cloned.1.call-update) | async-done | bytes 1966096 | tf_op jit(solution)/shard_map/all_gather | solution.py:98
  153.4 3.6 %fusion.30 = bf16[320,384]{1,0:T(8,128)(2,1)S(1)} fusion(bf16[2560,384]{1,0:T(8,128)(2,1)} %bitcast.221, f32[320,2560]{1,0:T(8,128)} %get-tuple-element.16, f32[320]{0:T(512)S(1)} %broadcast_maximum_fusion, f32[320]{0:T(512)S(1)} %fusion), kind=kOutput, calls=%fused_computation.55 | convolution fusion | flops 631029760 | bytes 5491200 | tf_op jit(solution)/shard_map/fqk,fkc->fqc/dot_general | solution.py:107
  157.6 40.2 %psum.30 = f32[32]{0:T(128)S(1)} all-reduce(f32[32]{0:T(128)S(1)} %reduce_sum.87), channel_id=1, replica_groups=mesh['frames'=4,'height'=8] {'frames','height'}, use_global_device_ids=true, to_apply=%region_10.0 | all-reduce | flops 32 | bytes 256 | tf_op jit(solution)/shard_map/psum | solution.py:34
  198.3 39.1 %psum.31 = f32[32]{0:T(128)S(1)} all-reduce(f32[32]{0:T(128)S(1)} %reduce_sum.89), channel_id=1, replica_groups=mesh['frames'=4,'height'=8] {'frames','height'}, use_global_device_ids=true, to_apply=%region_13.0 | all-reduce | flops 32 | bytes 256 | tf_op jit(solution)/shard_map/psum | solution.py:36
  237.8 4.5 %collective-permute-start = (bf16[1,2,160,384]{3,2,1,0:T(8,128)(2,1)S(1)}, bf16[1,2,160,384]{3,2,1,0:T(8,128)(2,1)S(1)}, u32[]{:S(2)}, u32[]{:S(2)}) collective-permute-start(bf16[1,2,160,384]{3,2,1,0:T(8,128)(2,1)S(1)} %multiply_convert_fusion), channel_id=1, source_target_pairs={{0,8},{8,16},{16,24},{1,9},{9,17},{17,25},{2,10},{10,18},{18,26},{... | collective-permute-start | bytes 737288 | tf_op jit(solution)/shard_map/ppermute | solution.py:15
  242.4 4.2 %collective-permute-done = bf16[1,2,160,384]{3,2,1,0:T(8,128)(2,1)S(1)} collective-permute-done((bf16[1,2,160,384]{3,2,1,0:T(8,128)(2,1)S(1)}, bf16[1,2,160,384]{3,2,1,0:T(8,128)(2,1)S(1)}, u32[]{:S(2)}, u32[]{:S(2)}) %collective-permute-start) | collective-permute-done | bytes 245792 | tf_op jit(solution)/shard_map/ppermute | solution.py:15
  246.7 1.5 collective-permute-start.1
  248.2 1.9 collective-permute-done.1
  250.6 1.5 fusion.69
  252.0 1.3 fusion.72
  253.3 1.3 fusion.64
  254.6 1.3 fusion.59
  255.9 1.3 fusion.49
  257.2 1.3 fusion.46
  258.5 1.3 fusion.43
  265.8 0.7 pad_maximum_fusion.3
  267.1 1.4 pad_maximum_fusion.1
  271.2 0.7 pad_maximum_fusion.5
  271.8 0.9 pad_maximum_fusion.6
  272.7 1.4 pad_maximum_fusion.2
  274.2 1.5 pad_maximum_fusion
  (84 shorter events, 12.1 us)
Async XLA Ops:
  6.5 117.6 %copy-start = (bf16[384,384]{1,0:T(8,128)(2,1)S(1)}, bf16[384,384]{1,0:T(8,128)(2,1)}, u32[]{:S(2)}) copy-start(bf16[384,384]{1,0:T(8,128)(2,1)} %param.15) | copy-start | bytes 884740
  6.5 117.6 %all-gather.3.cloned.1.call-start = ((), (), s32[]{:S(2)}) async-start(), calls=%async_computation | async-start | bytes 2211840 | tf_op jit(solution)/shard_map/all_gather | solution.py:97
  95.4 58.0 %all-gather.5.cloned.1.call-start = ((), (), s32[]{:S(2)}) async-start(), calls=%async_computation.1 | async-start | bytes 2211840 | tf_op jit(solution)/shard_map/all_gather | solution.py:98
  128.7 28.3 %copy-start.1 = (bf16[1,2,160,384]{3,2,1,0:T(8,128)(2,1)S(1)}, bf16[1,2,160,384]{3,2,1,0:T(8,128)(2,1)}, u32[]{:S(2)}) copy-start(bf16[1,2,160,384]{3,2,1,0:T(8,128)(2,1)} %param.12) | copy-start | bytes 737284
  128.7 28.3 %copy-start.2 = (bf16[384,384]{1,0:T(8,128)(2,1)S(1)}, bf16[384,384]{1,0:T(8,128)(2,1)}, u32[]{:S(2)}) copy-start(bf16[384,384]{1,0:T(8,128)(2,1)} %param.18) | copy-start | bytes 884740
  128.7 28.3 %copy-start.5 = (f32[384]{0:T(512)S(1)}, f32[384]{0:T(512)}, u32[]{:S(2)}) copy-start(f32[384]{0:T(512)} %param.19) | copy-start | bytes 4612
  128.7 108.9 %copy-start.6 = (f32[384]{0:T(512)S(1)}, f32[384]{0:T(512)}, u32[]{:S(2)}) copy-start(f32[384]{0:T(512)} %param.20) | copy-start | bytes 4612
  128.7 108.9 %copy-start.4 = (f32[384]{0:T(512)S(1)}, f32[384]{0:T(512)}, u32[]{:S(2)}) copy-start(f32[384]{0:T(512)} %param.21) | copy-start | bytes 4612
  237.8 22.1 %slice-start = ((s8[7962624]{0:T(1024)(128)(4,1)}), s8[4194304]{0:T(1024)(128)(4,1)S(1)}, s32[]{:S(2)}) async-start(s8[7962624]{0:T(1024)(128)(4,1)} %bitcast.177), calls=%async_computation.2 | async-start | bytes 8388608
  237.8 22.1 %copy-start.3 = (f32[384]{0:T(512)S(1)}, f32[384]{0:T(512)}, u32[]{:S(2)}) copy-start(f32[384]{0:T(512)} %param.23) | copy-start | bytes 4612
  237.8 8.8 %collective-permute-start = (bf16[1,2,160,384]{3,2,1,0:T(8,128)(2,1)S(1)}, bf16[1,2,160,384]{3,2,1,0:T(8,128)(2,1)S(1)}, u32[]{:S(2)}, u32[]{:S(2)}) collective-permute-start(bf16[1,2,160,384]{3,2,1,0:T(8,128)(2,1)S(1)} %multiply_convert_fusion), channel_id=1, source_target_pairs={{0,8},{8,16},{16,24},{1,9},{9,17},{17,25},{2,10},{10,18},{18,26},{... | collective-permute-start | bytes 737288 | tf_op jit(solution)/shard_map/ppermute | solution.py:15
  246.7 3.4 %collective-permute-start.1 = (bf16[2,1,1,160,384]{4,3,2,1,0:T(8,128)(2,1)S(1)}, bf16[2,1,1,160,384]{4,3,2,1,0:T(8,128)(2,1)S(1)}, u32[]{:S(2)}, u32[]{:S(2)}) collective-permute-start(bf16[2,1,1,160,384]{4,3,2,1,0:T(8,128)(2,1)S(1)} %pad_maximum_fusion.7), channel_id=1, source_target_pairs={{1,0},{2,1},{3,2},{4,3},{5,4},{6,5},{7,6},{9,8},{10,9},{11,10},{12... | collective-permute-start | bytes 737288 | tf_op jit(solution)/shard_map/ppermute | solution.py:15
  250.3 9.6 %slice-start.1 = ((s8[7962624]{0:T(1024)(128)(4,1)}), s8[3768320]{0:T(1024)(128)(4,1)S(1)}, s32[]{:S(2)}) async-start(s8[7962624]{0:T(1024)(128)(4,1)} %bitcast.177), calls=%async_computation.3 | async-start | bytes 7536640
Sparse Core Ops, SparseCore 0:
  95.5 28.6 all-gather.2
  125.8 27.5 all-gather.4
where the time goes:
time: 288 us; the launch traced here: 283 us
  blocking collectives  162 us (56%)
  waiting for transfers between devices  55 us (19%)
  matrix products  28.4 us (10%)
  other arithmetic  14.5 us (5%)
  between operations  13.9 us (5%)
  starting transfers between devices  5.97 us (2%)
  local copies, waits for them, and re-layouts  3.35 us (1%)
    psum x2, blocking collectives, group_norm(): mean = lax.psum(grouped(floats), ('frames', 'height')) / count  82.2 us
    psum x2, blocking collectives, group_norm(): lax.psum(grouped(centered * centered), ('frames', 'height')) / count  79.3 us
    all_gather x1, waiting for transfers between devices, local(): lax.all_gather(keys, 'height', axis=1, tiled=True)  26.7 us
    all_gather x1, waiting for transfers between devices, local(): lax.all_gather(values, 'height', axis=1, tiled=True)  22.1 us
    dot_general x27, matrix products, upsample_taps(): jnp.dot(window, weight[time_tap, row_tap, col_tap], preferred_element_typ...  15.9 us
    ppermute x2, waiting for transfers between devices, passed_along(): lax.ppermute(value, axis, [(source, source + steps) for source in range(i...  6.14 us
    ppermute x2, starting transfers between devices, passed_along(): lax.ppermute(value, axis, [(source, source + steps) for source in range(i...  5.93 us
  transfers between devices with their start and end apart: 4, of which 4 were waited for; matrix products, arithmetic and copies ran while one was open for 3% of the time, Pallas kernels for 0%

commit v1 on v0

v1 whole, which is shorter than its diff:
```python
import functools
import math

import jax
import jax.numpy as jnp
import numpy as np
from jax import lax
from jax.experimental import pallas as pl
from jax.experimental.pallas import tpu as pltpu
from jax.sharding import PartitionSpec as P

GROUPS = 32
EPS = 1e-05
F32 = jnp.float32
BF16 = jnp.bfloat16
VMEM_LIMIT = 48 * 1024 * 1024


def swapped(value, axis, mask):
    count = lax.axis_size(axis)
    return lax.ppermute(value, axis, [(i, i ^ mask) for i in range(count)])


def group_matrix(width):
    group = np.arange(width) // (width // GROUPS)
    return jnp.asarray(group[:, None] == group[None, :], BF16)


def group_sum(vector, same_group):
    high = vector.astype(BF16).astype(F32)
    rest = vector - high
    middle = rest.astype(BF16).astype(F32)
    low = rest - middle
    row = lax.broadcasted_iota(jnp.int32, (8, vector.shape[1]), 0)
    parts = jnp.where(row == 0, high, jnp.where(row == 1, middle, jnp.where(row == 2, low, 0.0)))
    summed = jnp.dot(parts.astype(BF16), same_group, preferred_element_type=F32)
    return jnp.sum(summed, axis=0, keepdims=True)


def mean_and_spread(values, same_group):
    count = values.shape[0] * (values.shape[1] // GROUPS)
    mean = group_sum(jnp.sum(values, axis=0, keepdims=True), same_group) * (1.0 / count)
    centered = values - mean
    return mean, group_sum(jnp.sum(centered * centered, axis=0, keepdims=True), same_group)


def stats_kernel(x_ref, same_ref, out_ref):
    mean, spread = mean_and_spread(x_ref[...].astype(F32), same_ref[...])
    out_ref[0:1, :] = mean
    out_ref[1:2, :] = spread


def local_stats(block, same_group):
    positions, width = block.shape
    return pl.pallas_call(
        stats_kernel,
        out_shape=jax.ShapeDtypeStruct((2, width), F32),
        name="local_stats",
    )(block, same_group)


def merged(stats, other, count):
    gap = stats[0] - other[0]
    return jnp.stack(
        [0.5 * (stats[0] + other[0]), stats[1] + other[1] + gap * gap * (0.5 * count)]
    )


def attention_kernel(slabs, count, below_ref, stats_ref, gain_ref, shift_ref, qk_ref, vo_ref, bias_ref, same_ref, *refs):
    blocks = refs[:slabs]
    mixed_ref, out_stats_ref, keys, sems = refs[slabs:]
    positions, width = blocks[0].shape
    cols = positions // 2
    copies = [
        pltpu.make_async_copy(
            blocks[i], keys.at[pl.ds(i * positions, positions), :], sems.at[i]
        )
        for i in range(slabs)
    ]
    for copy in copies:
        copy.start()
    mean = stats_ref[0:1, :]
    factor = gain_ref[...] * lax.rsqrt(stats_ref[1:2, :] * (1.0 / count) + EPS)
    offset = shift_ref[...] - mean * factor
    scale = width ** (-0.5) * math.log2(math.e)
    for copy in copies:
        copy.wait()
    below = pl.multiple_of(below_ref[0] * positions, positions)
    for row in range(3):
        if row < 2:
            own = keys[row * cols : (row + 1) * cols, :].astype(F32)
        else:
            own = keys[pl.ds(below, cols), :].astype(F32)
        normed = ((own - mean) * factor + shift_ref[...]).astype(BF16)
        turned = jnp.dot(normed, qk_ref[...], preferred_element_type=F32) * scale
        constant = jnp.sum(turned * offset, axis=1, keepdims=True)
        queries = (turned * factor).astype(BF16)
        scores = lax.dot_general(
            queries, keys[...], (((1,), (1,)), ((), ())), preferred_element_type=F32
        )
        highest = jnp.max(scores, axis=1, keepdims=True) + constant
        probs = jnp.exp2(scores + (constant - highest)).astype(BF16)
        total = jnp.sum(probs.astype(F32), axis=1, keepdims=True)
        summed = jnp.dot(probs, keys[...], preferred_element_type=F32)
        attended = ((summed / total - mean) * factor + shift_ref[...]).astype(BF16)
        branch = jnp.dot(attended, vo_ref[...], preferred_element_type=F32) + bias_ref[...]
        mixed_ref[row * cols : (row + 1) * cols, :] = (own + branch).astype(BF16)
    mean, spread = mean_and_spread(mixed_ref[0:positions, :].astype(F32), same_ref[...])
    out_stats_ref[0:1, :] = mean
    out_stats_ref[1:2, :] = spread


def attention(blocks, below, stats, count, gain, shift, qk, vo, bias, same_group):
    slabs = len(blocks)
    positions, width = blocks[0].shape
    vmem = pl.BlockSpec(memory_space=pltpu.VMEM)
    return pl.pallas_call(
        functools.partial(attention_kernel, slabs, count),
        out_shape=(
            jax.ShapeDtypeStruct((positions // 2 * 3, width), BF16),
            jax.ShapeDtypeStruct((2, width), F32),
        ),
        in_specs=[pl.BlockSpec(memory_space=pltpu.SMEM)]
        + [vmem] * 7
        + [pl.BlockSpec(memory_space=pl.ANY)] * slabs,
        out_specs=(vmem, vmem),
        scratch_shapes=[
            pltpu.VMEM((slabs * positions, width), BF16),
            pltpu.SemaphoreType.DMA((slabs,)),
        ],
        compiler_params=pltpu.CompilerParams(vmem_limit_bytes=VMEM_LIMIT),
        name="attention",
    )(below, stats, gain, shift, qk, vo, bias, same_group, *blocks)


SPACE_TAPS = (((1, 0),), ((2, 0), (0, 1)))


def upsample_kernel(count, valid_ref, current_ref, earlier_ref, stats_ref, gain_ref, shift_ref, bias_ref, weight_hbm, out_hbm, active, weight, wide, out, weight_sems, out_sems):
    positions, width = current_ref.shape
    cols = positions // 3
    order = []
    for odd_row in range(2):
        for odd_time in range(2):
            for odd_col in range(2):
                taps = []
                for time_tap, source in (((0, 0), (2, 1)), ((1, 0),))[odd_time]:
                    for row_tap, row_step in SPACE_TAPS[odd_row]:
                        for col_tap, col_step in SPACE_TAPS[odd_col]:
                            index = (time_tap * 3 + row_tap) * 3 + col_tap
                            taps.append((index, source * 2 + col_step, row_step))
                order.append((odd_time, odd_row, odd_col, taps))
    weight_copies = {}
    for *_, taps in order:
        for index, *_ in taps:
            weight_copies[index] = pltpu.make_async_copy(
                weight_hbm.at[index], weight.at[index], weight_sems.at[index]
            )
            weight_copies[index].start()
    mean = stats_ref[0:1, :]
    factor = gain_ref[...] * lax.rsqrt(stats_ref[1:2, :] * (1.0 / count) + EPS)
    col = lax.broadcasted_iota(jnp.int32, (cols, width), 0)
    for source, ref in enumerate((current_ref, earlier_ref)):
        for row in range(3):
            value = (ref[row * cols : (row + 1) * cols, :].astype(F32) - mean) * factor + shift_ref[...]
            value = value / (1.0 + jnp.exp(-value))
            kept = (valid_ref[0] if row == 2 else 1) * (valid_ref[1] if source else 1)
            value = jnp.where(kept > 0, value, 0.0)
            place = slice(row * cols, (row + 1) * cols)
            active[2 * source, place, :] = value.astype(BF16)
            moved = jnp.where(col == cols - 1, 0.0, pltpu.roll(value, cols - 1, 0))
            active[2 * source + 1, place, :] = moved.astype(BF16)
    out_copies = []
    for odd_time, odd_row, odd_col, taps in order:
        for index, *_ in taps:
            weight_copies[index].wait()
        windows = [
            active[which, row_step * cols : (row_step + 2) * cols, :] for _, which, row_step in taps
        ]
        stacked = [weight[index] for index, *_ in taps]
        summed = jnp.dot(
            jnp.concatenate(windows, axis=1),
            jnp.concatenate(stacked, axis=0),
            preferred_element_type=F32,
        )
        summed = summed + bias_ref[...]
        for row in range(2):
            for lane in range(width // 128):
                wide[row, lane, pl.ds(odd_col, cols, stride=2), :] = summed[
                    row * cols : (row + 1) * cols, lane * 128 : (lane + 1) * 128
                ]
        if odd_col == 1:
            for row in range(2):
                for lane in range(width // 128):
                    out[odd_time, 2 * row + odd_row, :, lane * 128 : (lane + 1) * 128] = wide[
                        row, lane
                    ].astype(BF16)
                copy = pltpu.make_async_copy(
                    out.at[odd_time, 2 * row + odd_row],
                    out_hbm.at[odd_time, 2 * row + odd_row],
                    out_sems.at[odd_time, 2 * row + odd_row],
                )
                copy.start()
                out_copies.append(copy)
    for copy in out_copies:
        copy.wait()


def upsample(valid, current, earlier, stats, count, gain, shift, bias, weight):
    positions, width = current.shape
    cols = positions // 3
    vmem = pl.BlockSpec(memory_space=pltpu.VMEM)
    taps = weight.shape[0]
    return pl.pallas_call(
        functools.partial(upsample_kernel, count),
        out_shape=jax.ShapeDtypeStruct((2, 4, 2 * cols, width), BF16),
        in_specs=[pl.BlockSpec(memory_space=pltpu.SMEM)]
        + [vmem] * 6
        + [pl.BlockSpec(memory_space=pl.ANY)],
        out_specs=pl.BlockSpec(memory_space=pl.ANY),
        scratch_shapes=[
            pltpu.VMEM((4, positions, width), BF16),
            pltpu.VMEM((taps, width, width), BF16),
            pltpu.VMEM((2, width // 128, 2 * cols, 128), F32),
            pltpu.VMEM((2, 4, 2 * cols, width), BF16),
            pltpu.SemaphoreType.DMA((taps,)),
            pltpu.SemaphoreType.DMA((2, 4)),
        ],
        compiler_params=pltpu.CompilerParams(vmem_limit_bytes=VMEM_LIMIT),
        name="upsample",
    )(valid, current, earlier, stats, gain, shift, bias, weight)


def local(
    latent,
    first_gain,
    first_shift,
    query_weight,
    key_weight,
    value_weight,
    out_weight,
    out_bias,
    second_gain,
    second_shift,
    up_weight,
    up_bias,
):
    frames, rows, cols, width = latent.shape
    positions = rows * cols
    height, groups = lax.axis_size("height"), lax.axis_size("frames")
    slab, group = lax.axis_index("height"), lax.axis_index("frames")
    entries = positions * (width // GROUPS)
    count = entries * height * groups
    same_group = group_matrix(width)
    block = latent.reshape(positions, width)

    def summed_over_mesh(stats):
        held = entries
        for axis, size in (("height", height), ("frames", groups)):
            mask = 1
            while mask < size:
                stats = merged(stats, swapped(stats, axis, mask), held)
                held, mask = 2 * held, 2 * mask
        return stats

    slots = {0: block}
    masks = sorted(range(2, height, 2), key=lambda m: (bin(m).count("1"), -m))
    for mask in masks:
        lowest = mask & -mask
        slots[mask] = swapped(slots[mask ^ lowest], "height", lowest)
    for mask in [0] + masks:
        slots[mask | 1] = swapped(slots[mask], "height", 1)
    below = jnp.where(slab + 1 < height, slab ^ (slab + 1), 0).astype(jnp.int32).reshape(1)

    first = summed_over_mesh(local_stats(block, same_group))
    qk = lax.dot_general(
        query_weight, key_weight, (((1,), (1,)), ((), ())), preferred_element_type=F32
    ).astype(BF16)
    vo = jnp.dot(value_weight, out_weight, preferred_element_type=F32).astype(BF16)
    row = lambda vector: vector.reshape(1, width)
    mixed, second = attention(
        [slots[m] for m in range(height)],
        below,
        first,
        count,
        row(first_gain),
        row(first_shift),
        qk,
        vo,
        row(out_bias),
        same_group,
    )
    earlier = lax.ppermute(mixed, "frames", [(i, i + 1) for i in range(groups - 1)])
    second = summed_over_mesh(second)
    valid = jnp.stack([slab + 1 < height, group > 0]).astype(jnp.int32)
    result = upsample(
        valid,
        mixed,
        earlier,
        second,
        count,
        row(second_gain),
        row(second_shift),
        row(up_bias),
        up_weight.reshape(27, width, width),
    )
    return result


def solution(mesh):
    placed = P("frames", "height", None, None)
    return jax.shard_map(
        local,
        mesh=mesh,
        in_specs=(placed,) + (P(),) * 11,
        out_specs=placed,
        check_vma=False,
    )
```

time: 288 us -> 72.3 us (0.25)
  the two profiles are of different devices: /device:TPU:0 before, /device:TPU:4 now
where the time goes in v1:
time: 72.3 us; the launch traced here: 71.9 us
  waiting for transfers between devices  28.9 us (40%)
  Pallas kernels  18 us (25%)
  starting transfers between devices  15 us (21%)
  local copies, waits for them, and re-layouts  6.01 us (8%)
  matrix products  2.69 us (4%)
  other arithmetic  1.02 us (1%)
    ppermute x17, waiting for transfers between devices, swapped(): return lax.ppermute(value, axis, [(i, i ^ mask) for i in range(count)])  24.5 us
    ppermute x17, starting transfers between devices, swapped(): return lax.ppermute(value, axis, [(i, i ^ mask) for i in range(count)])  12.6 us
    pallas_call x1, Pallas kernels, attention(): pl.pallas_call(functools.partial(attention_kernel, slabs, count), out_sha...  8.13 us
    pallas_call x1, Pallas kernels, upsample(): pl.pallas_call(functools.partial(upsample_kernel, count), out_shape=jax.S...  7.73 us
    ppermute x1, waiting for transfers between devices, local(): lax.ppermute(mixed, 'frames', [(i, i + 1) for i in range(groups - 1)])  4.41 us
    reshape x6, local copies, waits for them, and re-layouts, local(): row = lambda vector: vector.reshape(1, width)  4.1 us
    ppermute x1, starting transfers between devices, local(): lax.ppermute(mixed, 'frames', [(i, i + 1) for i in range(groups - 1)])  2.43 us
    pallas_call x1, Pallas kernels, local_stats(): pl.pallas_call(stats_kernel, out_shape=jax.ShapeDtypeStruct((2, width), F...  2.13 us
  transfers between devices with their start and end apart: 18, of which 12 were waited for; matrix products, arithmetic and copies ran while one was open for 10% of the time, Pallas kernels for 0%

profile of v1, /device:TPU:4, one launch (start us, length us, event | category | flops | bytes accessed | tf_op | source)
XLA Modules:
  0.0 71.9 jit_solution(11041394565080425063)
XLA Ops:
  0.0 2.1 %local_stats.1 = f32[2,384]{1,0:T(2,128)} custom-call(bf16[320,384]{1,0:T(8,128)(2,1)} %bitcast.9, bf16[384,384]{1,0:T(8,128)(2,1)} %constant.28.clone.same_ref), custom_call_target="tpu_custom_call" | custom-call | tf_op jit(solution)/shard_map/local_stats/pallas_call | solution.py:55
  2.1 1.4 %collective-permute-done = f32[2,384]{1,0:T(2,128)S(1)} collective-permute-done((f32[2,384]{1,0:T(2,128)}, f32[2,384]{1,0:T(2,128)S(1)}, u32[]{:S(2)}, u32[]{:S(2)}) %collective-permute-start) | collective-permute-done | bytes 3104 | tf_op jit(solution)/shard_map/ppermute | solution.py:21
  3.5 0.8 %add_multiply_fusion.9 = (f32[1,384]{1,0:T(1,128)S(1)}, f32[1,384]{1,0:T(1,128)S(1)}) fusion(f32[2,384]{1,0:T(2,128)S(1)} %collective-permute-done, f32[2,384]{1,0:T(2,128)} %local_stats.1), kind=kLoop, calls=%fused_computation.42 | loop fusion | flops 2688 | bytes 9216 | tf_op jit(solution)/shard_map/mul | solution.py:65
  4.3 1.6 %collective-permute-start.1 = (f32[2,384]{1,0:T(2,128)S(1)}, f32[2,384]{1,0:T(2,128)S(1)}, u32[]{:S(2)}, u32[]{:S(2)}) collective-permute-start(f32[2,384]{1,0:T(2,128)S(1)} %pad_maximum_fusion), channel_id=1, source_target_pairs={{0,2},{1,3},{2,0},{3,1},{4,6},{5,7},{6,4},{7,5},{8,10},{9,11},{10,... | collective-permute-start | bytes 9224 | tf_op jit(solution)/shard_map/ppermute | solution.py:21
  5.9 2.0 %collective-permute-done.1 = f32[2,384]{1,0:T(2,128)S(1)} collective-permute-done((f32[2,384]{1,0:T(2,128)S(1)}, f32[2,384]{1,0:T(2,128)S(1)}, u32[]{:S(2)}, u32[]{:S(2)}) %collective-permute-start.1) | collective-permute-done | bytes 3104 | tf_op jit(solution)/shard_map/ppermute | solution.py:21
  8.0 2.7 %collective-permute-start.2 = (f32[2,384]{1,0:T(2,128)S(1)}, f32[2,384]{1,0:T(2,128)S(1)}, u32[]{:S(2)}, u32[]{:S(2)}) collective-permute-start(f32[2,384]{1,0:T(2,128)S(1)} %pad_maximum_fusion.1), channel_id=1, source_target_pairs={{0,4},{1,5},{2,6},{3,7},{4,0},{5,1},{6,2},{7,3},{8,12},{9,13},{10,... | collective-permute-start | bytes 9224 | tf_op jit(solution)/shard_map/ppermute | solution.py:21
  11.0 1.6 %collective-permute-start.6 = (bf16[320,384]{1,0:T(8,128)(2,1)}, bf16[320,384]{1,0:T(8,128)(2,1)S(1)}, u32[]{:S(2)}, u32[]{:S(2)}) collective-permute-start(bf16[320,384]{1,0:T(8,128)(2,1)} %bitcast.11), channel_id=1, source_target_pairs={{0,2},{1,3},{2,0},{3,1},{4,6},{5,7},{6,4},{7,5},{8,10},{9,11},{10,... | collective-permute-start | bytes 737288 | tf_op jit(solution)/shard_map/ppermute | solution.py:21
  12.7 1.6 %collective-permute-start.3 = (f32[2,384]{1,0:T(2,128)S(1)}, f32[2,384]{1,0:T(2,128)S(1)}, u32[]{:S(2)}, u32[]{:S(2)}) collective-permute-start(f32[2,384]{1,0:T(2,128)S(1)} %pad_maximum_fusion.2), channel_id=1, source_target_pairs={{0,8},{8,0},{16,24},{24,16},{1,9},{9,1},{17,25},{25,17},{2,10},{10... | collective-permute-start | bytes 9224 | tf_op jit(solution)/shard_map/ppermute | solution.py:21
  14.2 1.3 %convolution_convert_fusion.1.qk_ref = bf16[384,384]{1,0:T(8,128)(2,1)S(1)} fusion(bf16[384,384]{1,0:T(8,128)(2,1)S(1)} %copy-done, bf16[384,384]{1,0:T(8,128)(2,1)} %param.17), kind=kOutput, calls=%fused_computation.1 | convolution fusion | flops 113393664 | bytes 884736 | tf_op jit(solution)/shard_map/dot_general | solution.py:276
  15.5 0.8 %collective-permute-done.3 = f32[2,384]{1,0:T(2,128)S(1)} collective-permute-done((f32[2,384]{1,0:T(2,128)S(1)}, f32[2,384]{1,0:T(2,128)S(1)}, u32[]{:S(2)}, u32[]{:S(2)}) %collective-permute-start.3) | collective-permute-done | bytes 3104 | tf_op jit(solution)/shard_map/ppermute | solution.py:21
  16.9 6.8 %collective-permute-done.8.refs_4_ = bf16[320,384]{1,0:T(8,128)(2,1)S(1)} collective-permute-done((bf16[320,384]{1,0:T(8,128)(2,1)}, bf16[320,384]{1,0:T(8,128)(2,1)S(1)}, u32[]{:S(2)}, u32[]{:S(2)}) %collective-permute-start.8) | collective-permute-done | bytes 245792 | tf_op jit(solution)/shard_map/ppermute | solution.py:21
  23.7 1.4 %convolution_convert_fusion.vo_ref = bf16[384,384]{1,0:T(8,128)(2,1)S(1)} fusion(bf16[384,384]{1,0:T(8,128)(2,1)} %param.18, bf16[384,384]{1,0:T(8,128)(2,1)} %param.19), kind=kOutput, calls=%fused_computation | convolution fusion | flops 113393664 | bytes 884736 | tf_op jit(solution)/shard_map/dot_general | solution.py:279
  25.0 0.7 reshape.29.gain_ref
  25.7 0.7 reshape.30.shift_ref
  26.4 0.7 reshape.31.bias_ref
  27.6 3.0 %collective-permute-done.10.refs_6_ = bf16[320,384]{1,0:T(8,128)(2,1)S(1)} collective-permute-done((bf16[320,384]{1,0:T(8,128)(2,1)S(1)}, bf16[320,384]{1,0:T(8,128)(2,1)S(1)}, u32[]{:S(2)}, u32[]{:S(2)}) %collective-permute-start.10) | collective-permute-done | bytes 245792 | tf_op jit(solution)/shard_map/ppermute | solution.py:21
  30.6 1.4 %collective-permute-done.11.refs_7_ = bf16[320,384]{1,0:T(8,128)(2,1)S(1)} collective-permute-done((bf16[320,384]{1,0:T(8,128)(2,1)S(1)}, bf16[320,384]{1,0:T(8,128)(2,1)S(1)}, u32[]{:S(2)}, u32[]{:S(2)}) %collective-permute-start.11) | collective-permute-done | bytes 245792 | tf_op jit(solution)/shard_map/ppermute | solution.py:21
  32.1 1.0 %copy-done.1 = bf16[384,384]{1,0:T(8,128)(2,1)S(1)} copy-done((bf16[384,384]{1,0:T(8,128)(2,1)S(1)}, bf16[384,384]{1,0:T(8,128)(2,1)}, u32[]{:S(2)}) %copy-start.1) | copy-done | bytes 294936
  33.1 0.9 %copy-done.2 = bf16[1,2,160,384]{3,2,1,0:T(8,128)(2,1)S(1)} copy-done((bf16[1,2,160,384]{3,2,1,0:T(8,128)(2,1)S(1)}, bf16[1,2,160,384]{3,2,1,0:T(8,128)(2,1)}, u32[]{:S(2)}) %copy-start.2) | copy-done | bytes 245784
  34.0 8.1 %attention.1 = (bf16[480,384]{1,0:T(8,128)(2,1)S(1)}, f32[2,384]{1,0:T(2,128)S(1)}) custom-call(s32[1]{0:T(128)} %bitcast.2.below_ref, f32[2,384]{1,0:T(2,128)S(1)} %pad_maximum_fusion.4.stats_ref, f32[1,384]{1,0:T(1,128)S(1)} %reshape.29.gain_ref, f32[1,384]{1,0:T(1,128)S(1)} %reshape.30.shift_ref, bf16[384,384]{1,0:T(8,128)(2,1)S(1)} %convolution_convert_fusion.1.qk_ref, ...), custom_call_target="tpu_custom_call" | custom-call | tf_op jit(solution)/shard_map/attention/pallas_call | solution.py:117
  42.3 1.0 %collective-permute-done.13 = f32[2,384]{1,0:T(2,128)S(1)} collective-permute-done((f32[2,384]{1,0:T(2,128)S(1)}, f32[2,384]{1,0:T(2,128)S(1)}, u32[]{:S(2)}, u32[]{:S(2)}) %collective-permute-start.13) | collective-permute-done | bytes 3104 | tf_op jit(solution)/shard_map/ppermute | solution.py:21
  43.7 3.3 %collective-permute-done.14 = f32[2,384]{1,0:T(2,128)S(1)} collective-permute-done((f32[2,384]{1,0:T(2,128)S(1)}, f32[2,384]{1,0:T(2,128)S(1)}, u32[]{:S(2)}, u32[]{:S(2)}) %collective-permute-start.14) | collective-permute-done | bytes 3104 | tf_op jit(solution)/shard_map/ppermute | solution.py:21
  47.1 1.1 %collective-permute-start.15 = (f32[2,384]{1,0:T(2,128)S(1)}, f32[2,384]{1,0:T(2,128)S(1)}, u32[]{:S(2)}, u32[]{:S(2)}) collective-permute-start(f32[2,384]{1,0:T(2,128)S(1)} %pad_maximum_fusion.6), channel_id=1, source_target_pairs={{0,4},{1,5},{2,6},{3,7},{4,0},{5,1},{6,2},{7,3},{8,12},{9,13},{10,... | collective-permute-start | bytes 9224 | tf_op jit(solution)/shard_map/ppermute | solution.py:21
  48.2 3.4 %collective-permute-done.15 = f32[2,384]{1,0:T(2,128)S(1)} collective-permute-done((f32[2,384]{1,0:T(2,128)S(1)}, f32[2,384]{1,0:T(2,128)S(1)}, u32[]{:S(2)}, u32[]{:S(2)}) %collective-permute-start.15) | collective-permute-done | bytes 3104 | tf_op jit(solution)/shard_map/ppermute | solution.py:21
  51.7 1.6 %collective-permute-start.16 = (f32[2,384]{1,0:T(2,128)S(1)}, f32[2,384]{1,0:T(2,128)S(1)}, u32[]{:S(2)}, u32[]{:S(2)}) collective-permute-start(f32[2,384]{1,0:T(2,128)S(1)} %pad_maximum_fusion.7), channel_id=1, source_target_pairs={{0,8},{8,0},{16,24},{24,16},{1,9},{9,1},{17,25},{25,17},{2,10},{10... | collective-permute-start | bytes 9224 | tf_op jit(solution)/shard_map/ppermute | solution.py:21
  53.2 2.4 %collective-permute-start.12 = (bf16[480,384]{1,0:T(8,128)(2,1)S(1)}, bf16[480,384]{1,0:T(8,128)(2,1)S(1)}, u32[]{:S(2)}, u32[]{:S(2)}) collective-permute-start(bf16[480,384]{1,0:T(8,128)(2,1)S(1)} %get-tuple-element.7.current_ref), channel_id=1, source_target_pairs={{0,8},{8,16},{16,24},{1,9},{9,17},{17,25},{2,10},{10,18},{18,26},{... | collective-permute-start | bytes 1105928 | tf_op jit(solution)/shard_map/ppermute | solution.py:293
  56.4 0.7 reshape.32.gain_ref
  57.1 0.7 reshape.33.shift_ref
  57.8 0.7 reshape.34.bias_ref
  58.5 1.2 %collective-permute-done.17 = f32[2,384]{1,0:T(2,128)S(1)} collective-permute-done((f32[2,384]{1,0:T(2,128)S(1)}, f32[2,384]{1,0:T(2,128)S(1)}, u32[]{:S(2)}, u32[]{:S(2)}) %collective-permute-start.17) | collective-permute-done | bytes 3104 | tf_op jit(solution)/shard_map/ppermute | solution.py:21
  59.7 4.4 %collective-permute-done.12.earlier_ref = bf16[480,384]{1,0:T(8,128)(2,1)S(1)} collective-permute-done((bf16[480,384]{1,0:T(8,128)(2,1)S(1)}, bf16[480,384]{1,0:T(8,128)(2,1)S(1)}, u32[]{:S(2)}, u32[]{:S(2)}) %collective-permute-start.12) | collective-permute-done | bytes 368672 | tf_op jit(solution)/shard_map/ppermute | solution.py:293
  64.1 7.7 %upsample.1 = bf16[2,4,320,384]{3,2,1,0:T(8,128)(2,1)} custom-call(s32[2]{0:T(128)S(1)} %add_convert_fusion.valid_ref, bf16[480,384]{1,0:T(8,128)(2,1)S(1)} %get-tuple-element.7.current_ref, bf16[480,384]{1,0:T(8,128)(2,1)S(1)} %collective-permute-done.12.earlier_ref, f32[2,384]{1,0:T(2,128)S(1)} %pad_maximum_fusion.9.stats_ref, ...), custom_call_target="tpu_custom_call" | custom-call | tf_op jit(solution)/shard_map/upsample/pallas_call | solution.py:214
  (42 shorter events, 2.9 us)
Async XLA Ops:
  0.0 14.2 %copy-start = (bf16[384,384]{1,0:T(8,128)(2,1)S(1)}, bf16[384,384]{1,0:T(8,128)(2,1)}, u32[]{:S(2)}) copy-start(bf16[384,384]{1,0:T(8,128)(2,1)} %param.16) | copy-start | bytes 884740
  2.1 1.4 %collective-permute-start = (f32[2,384]{1,0:T(2,128)}, f32[2,384]{1,0:T(2,128)S(1)}, u32[]{:S(2)}, u32[]{:S(2)}) collective-permute-start(f32[2,384]{1,0:T(2,128)} %local_stats.1), channel_id=1, source_target_pairs={{0,1},{1,0},{2,3},{3,2},{4,5},{5,4},{6,7},{7,6},{8,9},{9,8},{10,11... | collective-permute-start | bytes 9224 | tf_op jit(solution)/shard_map/ppermute | solution.py:21
  4.3 3.7 %collective-permute-start.1 = (f32[2,384]{1,0:T(2,128)S(1)}, f32[2,384]{1,0:T(2,128)S(1)}, u32[]{:S(2)}, u32[]{:S(2)}) collective-permute-start(f32[2,384]{1,0:T(2,128)S(1)} %pad_maximum_fusion), channel_id=1, source_target_pairs={{0,2},{1,3},{2,0},{3,1},{4,6},{5,7},{6,4},{7,5},{8,10},{9,11},{10,... | collective-permute-start | bytes 9224 | tf_op jit(solution)/shard_map/ppermute | solution.py:21
  8.0 4.7 %collective-permute-start.2 = (f32[2,384]{1,0:T(2,128)S(1)}, f32[2,384]{1,0:T(2,128)S(1)}, u32[]{:S(2)}, u32[]{:S(2)}) collective-permute-start(f32[2,384]{1,0:T(2,128)S(1)} %pad_maximum_fusion.1), channel_id=1, source_target_pairs={{0,4},{1,5},{2,6},{3,7},{4,0},{5,1},{6,2},{7,3},{8,12},{9,13},{10,... | collective-permute-start | bytes 9224 | tf_op jit(solution)/shard_map/ppermute | solution.py:21
  10.6 13.0 %collective-permute-start.8 = (bf16[320,384]{1,0:T(8,128)(2,1)}, bf16[320,384]{1,0:T(8,128)(2,1)S(1)}, u32[]{:S(2)}, u32[]{:S(2)}) collective-permute-start(bf16[320,384]{1,0:T(8,128)(2,1)} %bitcast.10), channel_id=1, source_target_pairs={{0,4},{1,5},{2,6},{3,7},{4,0},{5,1},{6,2},{7,3},{8,12},{9,13},{10,... | collective-permute-start | bytes 737288 | tf_op jit(solution)/shard_map/ppermute | solution.py:21
  11.0 16.1 %collective-permute-start.6 = (bf16[320,384]{1,0:T(8,128)(2,1)}, bf16[320,384]{1,0:T(8,128)(2,1)S(1)}, u32[]{:S(2)}, u32[]{:S(2)}) collective-permute-start(bf16[320,384]{1,0:T(8,128)(2,1)} %bitcast.11), channel_id=1, source_target_pairs={{0,2},{1,3},{2,0},{3,1},{4,6},{5,7},{6,4},{7,5},{8,10},{9,11},{10,... | collective-permute-start | bytes 737288 | tf_op jit(solution)/shard_map/ppermute | solution.py:21
  12.6 18.1 %collective-permute-start.5 = (bf16[320,384]{1,0:T(8,128)(2,1)}, bf16[320,384]{1,0:T(8,128)(2,1)S(1)}, u32[]{:S(2)}, u32[]{:S(2)}) collective-permute-start(bf16[320,384]{1,0:T(8,128)(2,1)} %bitcast.12), channel_id=1, source_target_pairs={{0,1},{1,0},{2,3},{3,2},{4,5},{5,4},{6,7},{7,6},{8,9},{9,8},{10,11... | collective-permute-start | bytes 737288 | tf_op jit(solution)/shard_map/ppermute | solution.py:21
  12.7 3.7 %collective-permute-start.3 = (f32[2,384]{1,0:T(2,128)S(1)}, f32[2,384]{1,0:T(2,128)S(1)}, u32[]{:S(2)}, u32[]{:S(2)}) collective-permute-start(f32[2,384]{1,0:T(2,128)S(1)} %pad_maximum_fusion.2), channel_id=1, source_target_pairs={{0,8},{8,0},{16,24},{24,16},{1,9},{9,1},{17,25},{25,17},{2,10},{10... | collective-permute-start | bytes 9224 | tf_op jit(solution)/shard_map/ppermute | solution.py:21
  16.4 14.2 %collective-permute-start.4 = (f32[2,384]{1,0:T(2,128)S(1)}, f32[2,384]{1,0:T(2,128)S(1)}, u32[]{:S(2)}, u32[]{:S(2)}) collective-permute-start(f32[2,384]{1,0:T(2,128)S(1)} %pad_maximum_fusion.3), channel_id=1, source_target_pairs={{0,16},{8,24},{16,0},{24,8},{1,17},{9,25},{17,1},{25,9},{2,18},{10... | collective-permute-start | bytes 9224 | tf_op jit(solution)/shard_map/ppermute | solution.py:21
  23.6 6.9 %collective-permute-start.10 = (bf16[320,384]{1,0:T(8,128)(2,1)S(1)}, bf16[320,384]{1,0:T(8,128)(2,1)S(1)}, u32[]{:S(2)}, u32[]{:S(2)}) collective-permute-start(bf16[320,384]{1,0:T(8,128)(2,1)S(1)} %collective-permute-done.8.refs_4_), channel_id=1, source_target_pairs={{0,2},{1,3},{2,0},{3,1},{4,6},{5,7},{6,4},{7,5},{8,10},{9,11},{10,... | collective-permute-start | bytes 737288 | tf_op jit(solution)/shard_map/ppermute | solution.py:21
  27.1 3.5 %collective-permute-start.9 = (bf16[320,384]{1,0:T(8,128)(2,1)S(1)}, bf16[320,384]{1,0:T(8,128)(2,1)S(1)}, u32[]{:S(2)}, u32[]{:S(2)}) collective-permute-start(bf16[320,384]{1,0:T(8,128)(2,1)S(1)} %collective-permute-done.8.refs_4_), channel_id=1, source_target_pairs={{0,1},{1,0},{2,3},{3,2},{4,5},{5,4},{6,7},{7,6},{8,9},{9,8},{10,11... | collective-permute-start | bytes 737288 | tf_op jit(solution)/shard_map/ppermute | solution.py:21
  27.1 3.5 %collective-permute-start.7 = (bf16[320,384]{1,0:T(8,128)(2,1)S(1)}, bf16[320,384]{1,0:T(8,128)(2,1)S(1)}, u32[]{:S(2)}, u32[]{:S(2)}) collective-permute-start(bf16[320,384]{1,0:T(8,128)(2,1)S(1)} %collective-permute-done.6.refs_2_), channel_id=1, source_target_pairs={{0,1},{1,0},{2,3},{3,2},{4,5},{5,4},{6,7},{7,6},{8,9},{9,8},{10,11... | collective-permute-start | bytes 737288 | tf_op jit(solution)/shard_map/ppermute | solution.py:21
  30.6 1.5 %collective-permute-start.11 = (bf16[320,384]{1,0:T(8,128)(2,1)S(1)}, bf16[320,384]{1,0:T(8,128)(2,1)S(1)}, u32[]{:S(2)}, u32[]{:S(2)}) collective-permute-start(bf16[320,384]{1,0:T(8,128)(2,1)S(1)} %collective-permute-done.10.refs_6_), channel_id=1, source_target_pairs={{0,1},{1,0},{2,3},{3,2},{4,5},{5,4},{6,7},{7,6},{8,9},{9,8},{10,11... | collective-permute-start | bytes 737288 | tf_op jit(solution)/shard_map/ppermute | solution.py:21
  32.1 1.0 %copy-start.1 = (bf16[384,384]{1,0:T(8,128)(2,1)S(1)}, bf16[384,384]{1,0:T(8,128)(2,1)}, u32[]{:S(2)}) copy-start(bf16[384,384]{1,0:T(8,128)(2,1)} %constant.28.clone.same_ref) | copy-start | bytes 884740
  33.1 0.9 %copy-start.2 = (bf16[1,2,160,384]{3,2,1,0:T(8,128)(2,1)S(1)}, bf16[1,2,160,384]{3,2,1,0:T(8,128)(2,1)}, u32[]{:S(2)}) copy-start(bf16[1,2,160,384]{3,2,1,0:T(8,128)(2,1)} %param.13) | copy-start | bytes 737284
  42.1 1.2 %collective-permute-start.13 = (f32[2,384]{1,0:T(2,128)S(1)}, f32[2,384]{1,0:T(2,128)S(1)}, u32[]{:S(2)}, u32[]{:S(2)}) collective-permute-start(f32[2,384]{1,0:T(2,128)S(1)} %get-tuple-element.8), channel_id=1, source_target_pairs={{0,1},{1,0},{2,3},{3,2},{4,5},{5,4},{6,7},{7,6},{8,9},{9,8},{10,11... | collective-permute-start | bytes 9224 | tf_op jit(solution)/shard_map/ppermute | solution.py:21
  43.4 3.7 %collective-permute-start.14 = (f32[2,384]{1,0:T(2,128)S(1)}, f32[2,384]{1,0:T(2,128)S(1)}, u32[]{:S(2)}, u32[]{:S(2)}) collective-permute-start(f32[2,384]{1,0:T(2,128)S(1)} %pad_maximum_fusion.5), channel_id=1, source_target_pairs={{0,2},{1,3},{2,0},{3,1},{4,6},{5,7},{6,4},{7,5},{8,10},{9,11},{10,... | collective-permute-start | bytes 9224 | tf_op jit(solution)/shard_map/ppermute | solution.py:21
  47.1 4.6 %collective-permute-start.15 = (f32[2,384]{1,0:T(2,128)S(1)}, f32[2,384]{1,0:T(2,128)S(1)}, u32[]{:S(2)}, u32[]{:S(2)}) collective-permute-start(f32[2,384]{1,0:T(2,128)S(1)} %pad_maximum_fusion.6), channel_id=1, source_target_pairs={{0,4},{1,5},{2,6},{3,7},{4,0},{5,1},{6,2},{7,3},{8,12},{9,13},{10,... | collective-permute-start | bytes 9224 | tf_op jit(solution)/shard_map/ppermute | solution.py:21
  51.7 4.0 %collective-permute-start.16 = (f32[2,384]{1,0:T(2,128)S(1)}, f32[2,384]{1,0:T(2,128)S(1)}, u32[]{:S(2)}, u32[]{:S(2)}) collective-permute-start(f32[2,384]{1,0:T(2,128)S(1)} %pad_maximum_fusion.7), channel_id=1, source_target_pairs={{0,8},{8,0},{16,24},{24,16},{1,9},{9,1},{17,25},{25,17},{2,10},{10... | collective-permute-start | bytes 9224 | tf_op jit(solution)/shard_map/ppermute | solution.py:21
  53.2 10.9 %collective-permute-start.12 = (bf16[480,384]{1,0:T(8,128)(2,1)S(1)}, bf16[480,384]{1,0:T(8,128)(2,1)S(1)}, u32[]{:S(2)}, u32[]{:S(2)}) collective-permute-start(bf16[480,384]{1,0:T(8,128)(2,1)S(1)} %get-tuple-element.7.current_ref), channel_id=1, source_target_pairs={{0,8},{8,16},{16,24},{1,9},{9,17},{17,25},{2,10},{10,18},{18,26},{... | collective-permute-start | bytes 1105928 | tf_op jit(solution)/shard_map/ppermute | solution.py:293
  55.7 4.0 %collective-permute-start.17 = (f32[2,384]{1,0:T(2,128)S(1)}, f32[2,384]{1,0:T(2,128)S(1)}, u32[]{:S(2)}, u32[]{:S(2)}) collective-permute-start(f32[2,384]{1,0:T(2,128)S(1)} %pad_maximum_fusion.8), channel_id=1, source_target_pairs={{0,16},{8,24},{16,0},{24,8},{1,17},{9,25},{17,1},{25,9},{2,18},{10... | collective-permute-start | bytes 9224 | tf_op jit(solution)/shard_map/ppermute | solution.py:21

commit v2 on v1

v2 whole, which is shorter than its diff:
```python
import functools
import math

import jax
import jax.numpy as jnp
import numpy as np
from jax import lax
from jax.experimental import pallas as pl
from jax.experimental.pallas import tpu as pltpu
from jax.sharding import PartitionSpec as P

GROUPS = 32
EPS = 1e-05
F32 = jnp.float32
BF16 = jnp.bfloat16
VMEM_LIMIT = 48 * 1024 * 1024


def swapped(value, axis, mask):
    count = lax.axis_size(axis)
    return lax.ppermute(value, axis, [(i, i ^ mask) for i in range(count)])


def group_sums(rows):
    width = rows[0].shape[1]
    row = lax.broadcasted_iota(jnp.int32, (8 * len(rows), width), 0)
    parts = jnp.zeros((8 * len(rows), width), F32)
    for i, rest in enumerate(rows):
        for j in range(3):
            part = rest.astype(BF16).astype(F32)
            rest = rest - part
            parts = jnp.where(row == 8 * i + j, part, parts)
    per_group = width // GROUPS
    groups = [
        jnp.floor((lax.broadcasted_iota(jnp.int32, (width, width), d).astype(F32) + 0.5) * (1.0 / per_group))
        for d in range(2)
    ]
    same_group = jnp.where(groups[0] == groups[1], 1.0, 0.0).astype(BF16)
    summed = jnp.dot(parts.astype(BF16), same_group, preferred_element_type=F32)
    return [jnp.sum(summed[8 * i : 8 * i + 8], axis=0, keepdims=True) for i in range(len(rows))]


def mean_and_spread(blocks):
    count = len(blocks) * blocks[0].shape[0]
    mean = sum(jnp.sum(b, axis=0, keepdims=True) for b in blocks) * (1.0 / count)
    return mean, sum(jnp.sum(jnp.square(b - mean), axis=0, keepdims=True) for b in blocks)


def group_mean_and_variance(means, spread, count):
    per_group = means.shape[1] // GROUPS
    mean = group_sums([means])[0] * (1.0 / per_group)
    gap = means - mean
    total = group_sums([spread + gap * gap * count])[0]
    return mean, total * (1.0 / (per_group * count))


def stats_kernel(own_hbm, other_ref, out_ref, own, sem):
    copy = pltpu.make_async_copy(own_hbm, own, sem)
    copy.start()
    copy.wait()
    mean, spread = mean_and_spread([own[...].astype(F32), other_ref[...].astype(F32)])
    for i in range(out_ref.shape[0]):
        out_ref[i, 0:1, :] = mean
        out_ref[i, 1:2, :] = spread


def local_stats(own, other, copies):
    vmem = pl.BlockSpec(memory_space=pltpu.VMEM)
    return pl.pallas_call(
        stats_kernel,
        out_shape=jax.ShapeDtypeStruct((copies, 2, own.shape[1]), F32),
        in_specs=[pl.BlockSpec(memory_space=pltpu.HBM), vmem],
        out_specs=vmem,
        scratch_shapes=[pltpu.VMEM(own.shape, own.dtype), pltpu.SemaphoreType.DMA],
        cost_estimate=pl.CostEstimate(flops=1 << 20, bytes_accessed=0, transcendentals=0),
        name="local_stats",
    )(own, other)


def prepare_kernel(query_ref, key_ref, value_ref, mix_ref, *refs):
    *vector_refs, qk_ref, vo_ref, vectors_ref = refs
    width = query_ref.shape[0]
    qk_ref[...] = lax.dot_general(
        query_ref[...], key_ref[...], (((1,), (1,)), ((), ())), preferred_element_type=F32
    ).astype(BF16)
    vo_ref[...] = jnp.dot(value_ref[...], mix_ref[...], preferred_element_type=F32).astype(BF16)
    for i, ref in enumerate(vector_refs):
        vectors_ref[i : i + 1, :] = ref[...].reshape(1, width)


def prepare(query, key, value, mix, *vectors):
    square = jax.ShapeDtypeStruct(query.shape, BF16)
    return pl.pallas_call(
        prepare_kernel,
        out_shape=(square, square, jax.ShapeDtypeStruct((len(vectors), query.shape[0]), F32)),
        cost_estimate=pl.CostEstimate(flops=4 * query.shape[0] ** 3, bytes_accessed=0, transcendentals=0),
        name="prepare",
    )(query, key, value, mix, *vectors)


def merged(stats, count):
    mean = jnp.mean(stats[:, 0], axis=0, keepdims=True)
    gap = stats[:, 0] - mean
    return mean, jnp.sum(stats[:, 1] + gap * gap * count, axis=0, keepdims=True)


def attention_kernel(starts, count, below_ref, stats_ref, qk_ref, vo_ref, vectors_ref, *refs):
    blocks = refs[: len(starts)]
    mixed_ref, out_stats_ref, keys, sems = refs[len(starts) :]
    positions, width = blocks[0].shape
    cols = positions // 2
    copies = [
        pltpu.make_async_copy(
            block, keys.at[pl.ds(start, block.shape[0]), :], sems.at[i]
        )
        for i, (start, block) in enumerate(zip(starts, blocks))
    ]
    for copy in copies:
        copy.start()
    mean, variance = group_mean_and_variance(stats_ref[0:1, :], stats_ref[1:2, :], count)
    gain, shift, bias = (vectors_ref[i : i + 1, :] for i in range(3))
    factor = gain * lax.rsqrt(variance + EPS)
    offset = shift - mean * factor
    scale = width ** (-0.5) * math.log2(math.e)
    for copy in copies:
        copy.wait()
    below = pl.multiple_of(below_ref[0] * positions, positions)
    for row in range(3):
        if row < 2:
            own = keys[row * cols : (row + 1) * cols, :].astype(F32)
        else:
            own = keys[pl.ds(below, cols), :].astype(F32)
        normed = ((own - mean) * factor + shift).astype(BF16)
        turned = jnp.dot(normed, qk_ref[...], preferred_element_type=F32) * scale
        constant = jnp.sum(turned * offset, axis=1, keepdims=True)
        queries = (turned * factor).astype(BF16)
        scores = lax.dot_general(
            queries, keys[...], (((1,), (1,)), ((), ())), preferred_element_type=F32
        )
        highest = jnp.max(scores, axis=1, keepdims=True) + constant
        probs = jnp.exp2(scores + (constant - highest)).astype(BF16)
        total = jnp.sum(probs.astype(F32), axis=1, keepdims=True)
        summed = jnp.dot(probs, keys[...], preferred_element_type=F32)
        attended = ((summed / total - mean) * factor + shift).astype(BF16)
        branch = jnp.dot(attended, vo_ref[...], preferred_element_type=F32) + bias
        mixed_ref[row * cols : (row + 1) * cols, :] = (own + branch).astype(BF16)
    mean, spread = mean_and_spread([mixed_ref[0:positions, :].astype(F32)])
    for i in range(out_stats_ref.shape[0]):
        out_stats_ref[i, 0:1, :] = mean
        out_stats_ref[i, 1:2, :] = spread


def attention(blocks, below, stats, count, qk, vo, vectors, stat_copies):
    starts, blocks = zip(*blocks)
    positions, width = blocks[0].shape
    vmem = pl.BlockSpec(memory_space=pltpu.VMEM)
    return pl.pallas_call(
        functools.partial(attention_kernel, starts, count),
        out_shape=(
            jax.ShapeDtypeStruct((positions // 2 * 3, width), BF16),
            jax.ShapeDtypeStruct((stat_copies, 2, width), F32),
        ),
        in_specs=[pl.BlockSpec(memory_space=pltpu.SMEM)]
        + [vmem] * 4
        + [pl.BlockSpec(memory_space=pltpu.HBM)]
        + [pl.BlockSpec(memory_space=pl.ANY)] * (len(blocks) - 1),
        out_specs=(vmem, vmem),
        scratch_shapes=[
            pltpu.VMEM((sum(b.shape[0] for b in blocks), width), BF16),
            pltpu.SemaphoreType.DMA((len(blocks),)),
        ],
        compiler_params=pltpu.CompilerParams(vmem_limit_bytes=VMEM_LIMIT),
        name="attention",
    )(below, stats, qk, vo, vectors, *blocks)


SPACE_TAPS = (((1, 0),), ((2, 0), (0, 1)))


def upsample_kernel(count, valid_ref, current_ref, earlier_ref, stats_ref, vectors_ref, weight_hbm, out_hbm, active, weight, wide, out, weight_sems, out_sems):
    positions, width = current_ref.shape
    cols = positions // 3
    order = []
    for odd_row in range(2):
        for odd_time in range(2):
            for odd_col in range(2):
                taps = []
                for time_tap, source in (((0, 0), (2, 1)), ((1, 0),))[odd_time]:
                    for row_tap, row_step in SPACE_TAPS[odd_row]:
                        for col_tap, col_step in SPACE_TAPS[odd_col]:
                            index = (time_tap * 3 + row_tap) * 3 + col_tap
                            taps.append((index, source * 2 + col_step, row_step))
                order.append((odd_time, odd_row, odd_col, taps))
    weight_copies = {}
    for *_, taps in order:
        for index, *_ in taps:
            weight_copies[index] = pltpu.make_async_copy(
                weight_hbm.at[index], weight.at[index], weight_sems.at[index]
            )
            weight_copies[index].start()
    mean, variance = group_mean_and_variance(*merged(stats_ref[...], count // stats_ref.shape[0]), count)
    gain, shift, bias = (vectors_ref[i : i + 1, :] for i in range(3, 6))
    factor = gain * lax.rsqrt(variance + EPS)
    col = lax.broadcasted_iota(jnp.int32, (cols, width), 0)
    for source, ref in enumerate((current_ref, earlier_ref)):
        for row in range(3):
            value = (ref[row * cols : (row + 1) * cols, :].astype(F32) - mean) * factor + shift
            value = value / (1.0 + jnp.exp(-value))
            kept = (valid_ref[0] if row == 2 else 1) * (valid_ref[1] if source else 1)
            value = jnp.where(kept > 0, value, 0.0)
            place = slice(row * cols, (row + 1) * cols)
            active[2 * source, place, :] = value.astype(BF16)
            moved = jnp.where(col == cols - 1, 0.0, pltpu.roll(value, cols - 1, 0))
            active[2 * source + 1, place, :] = moved.astype(BF16)
    out_copies = []
    for odd_time, odd_row, odd_col, taps in order:
        for index, *_ in taps:
            weight_copies[index].wait()
        windows = [
            active[which, row_step * cols : (row_step + 2) * cols, :] for _, which, row_step in taps
        ]
        stacked = [weight[index] for index, *_ in taps]
        summed = jnp.dot(
            jnp.concatenate(windows, axis=1),
            jnp.concatenate(stacked, axis=0),
            preferred_element_type=F32,
        )
        summed = summed + bias
        for row in range(2):
            for lane in range(width // 128):
                wide[row, lane, pl.ds(odd_col, cols, stride=2), :] = summed[
                    row * cols : (row + 1) * cols, lane * 128 : (lane + 1) * 128
                ]
        if odd_col == 1:
            for row in range(2):
                for lane in range(width // 128):
                    out[odd_time, 2 * row + odd_row, :, lane * 128 : (lane + 1) * 128] = wide[
                        row, lane
                    ].astype(BF16)
                copy = pltpu.make_async_copy(
                    out.at[odd_time, 2 * row + odd_row],
                    out_hbm.at[odd_time, 2 * row + odd_row],
                    out_sems.at[odd_time, 2 * row + odd_row],
                )
                copy.start()
                out_copies.append(copy)
    for copy in out_copies:
        copy.wait()


def upsample(valid, current, earlier, stats, count, vectors, weight):
    positions, width = current.shape
    cols = positions // 3
    vmem = pl.BlockSpec(memory_space=pltpu.VMEM)
    taps = weight.shape[0]
    return pl.pallas_call(
        functools.partial(upsample_kernel, count),
        out_shape=jax.ShapeDtypeStruct((2, 4, 2 * cols, width), BF16),
        in_specs=[pl.BlockSpec(memory_space=pltpu.SMEM)]
        + [vmem] * 4
        + [pl.BlockSpec(memory_space=pltpu.HBM)],
        out_specs=pl.BlockSpec(memory_space=pl.ANY),
        scratch_shapes=[
            pltpu.VMEM((4, positions, width), BF16),
            pltpu.VMEM((taps, width, width), BF16),
            pltpu.VMEM((2, width // 128, 2 * cols, 128), F32),
            pltpu.VMEM((2, 4, 2 * cols, width), BF16),
            pltpu.SemaphoreType.DMA((taps,)),
            pltpu.SemaphoreType.DMA((2, 4)),
        ],
        compiler_params=pltpu.CompilerParams(vmem_limit_bytes=VMEM_LIMIT),
        name="upsample",
    )(valid, current, earlier, stats, vectors, weight)


def local(
    latent,
    first_gain,
    first_shift,
    query_weight,
    key_weight,
    value_weight,
    out_weight,
    out_bias,
    second_gain,
    second_shift,
    up_weight,
    up_bias,
):
    frames, rows, cols, width = latent.shape
    positions = rows * cols
    height, groups = lax.axis_size("height"), lax.axis_size("frames")
    slab, group = lax.axis_index("height"), lax.axis_index("frames")
    count = positions * height * groups
    block = latent.reshape(positions, width)

    slots = {0: block, 1: swapped(block, "height", 1)}
    direct = [1 << i for i in range(1, (height - 1).bit_length())][::-1]
    forwarded = sorted((m for m in range(2, height, 2) if m not in direct), key=lambda m: (bin(m).count("1"), -m))
    for mask in direct:
        slots[mask] = swapped(block, "height", mask)
    held = 2 * positions

    def early_work(own, other, *parameters):
        stats = local_stats(own, other, groups)
        stats = lax.all_to_all(stats, "frames", split_axis=0, concat_axis=0, tiled=True)
        return jnp.concatenate(merged(stats, held), axis=0), *prepare(*parameters)

    parameters = (query_weight, key_weight, value_weight, out_weight)
    parameters += (first_gain, first_shift, out_bias, second_gain, second_shift, up_bias)
    first, qk, vo, vectors = lax.cond(
        group < groups,
        early_work,
        lambda *arguments: jax.tree.map(
            lambda kind: jnp.zeros(kind.shape, kind.dtype), jax.eval_shape(early_work, *arguments)
        ),
        block,
        slots[1],
        *parameters,
    )
    held = held * groups
    ready = lax.optimization_barrier([slots[m] for m in direct])
    slots.update(zip(direct, ready))
    for mask in forwarded:
        lowest = mask & -mask
        slots[mask] = swapped(slots[mask ^ lowest], "height", lowest)
    for mask in direct:
        pair = jnp.stack([first, swapped(first, "height", mask)])
        first, held = jnp.concatenate(merged(pair, held), axis=0), held * 2
    for mask in direct + forwarded:
        slots[mask | 1] = swapped(slots[mask], "height", 1)
    below = jnp.where(slab + 1 < height, slab ^ (slab + 1), 0).astype(jnp.int32).reshape(1)

    mixed, second = attention(
        [(m * positions, slots[m]) for m in range(height)],
        below,
        first,
        count,
        qk,
        vo,
        vectors,
        groups * height,
    )
    earlier = lax.ppermute(mixed, "frames", [(i, i + 1) for i in range(groups - 1)])
    second = lax.all_to_all(second, ("frames", "height"), split_axis=0, concat_axis=0, tiled=True)
    valid = jnp.stack([slab + 1 < height, group > 0]).astype(jnp.int32)
    result = upsample(
        valid,
        mixed,
        earlier,
        second,
        count,
        vectors,
        up_weight.reshape(27, width, width),
    )
    return result


def solution(mesh):
    placed = P("frames", "height", None, None)
    return jax.shard_map(
        local,
        mesh=mesh,
        in_specs=(placed,) + (P(),) * 11,
        out_specs=placed,
        check_vma=False,
    )
```

time: 72.3 us -> 59.5 us (0.82)
  the two profiles are of different devices: /device:TPU:4 before, /device:TPU:0 now
where the time goes in v2:
time: 59.5 us; the launch traced here: 59.2 us
  Pallas kernels  20.9 us (35%)
  starting transfers between devices  20.3 us (34%)
  waiting for transfers between devices  17.5 us (29%)
    pallas_call x1, Pallas kernels, upsample(): pl.pallas_call(functools.partial(upsample_kernel, count), out_shape=jax.S...  8.81 us
    ppermute x9, starting transfers between devices, swapped(): return lax.ppermute(value, axis, [(i, i ^ mask) for i in range(count)])  8.54 us
    pallas_call x1, Pallas kernels, attention(): pl.pallas_call(functools.partial(attention_kernel, starts, count), out_sh...  8.51 us
    all_to_all x1, waiting for transfers between devices, local(): lax.all_to_all(second, ('frames', 'height'), split_axis=0, concat_axis=0,...  7.7 us
    ppermute x9, waiting for transfers between devices, swapped(): return lax.ppermute(value, axis, [(i, i ^ mask) for i in range(count)])  6.87 us
    all_to_all x1, starting transfers between devices, local(): lax.all_to_all(second, ('frames', 'height'), split_axis=0, concat_axis=0,...  5.1 us
    all_to_all x1, starting transfers between devices, early_work(): lax.all_to_all(stats, 'frames', split_axis=0, concat_axis=0, tiled=True)  3.73 us
    ppermute x1, starting transfers between devices, local(): lax.ppermute(mixed, 'frames', [(i, i + 1) for i in range(groups - 1)])  2.95 us
  transfers between devices with their start and end apart: 12, of which 6 were waited for; matrix products, arithmetic and copies ran while one was open for 1% of the time, Pallas kernels for 6%

profile of v2, /device:TPU:0, one launch (start us, length us, event | category | flops | bytes accessed | tf_op | source)
XLA Modules:
  0.0 59.2 jit_solution(11865307805259407831)
XLA Ops:
  0.0 0.5 collective-permute-start
  0.5 3.6 %collective-permute-start.3 = (bf16[320,384]{1,0:T(8,128)(2,1)}, bf16[320,384]{1,0:T(8,128)(2,1)S(1)}, u32[]{:S(2)}, u32[]{:S(2)}) collective-permute-start(bf16[320,384]{1,0:T(8,128)(2,1)} %bitcast.56), channel_id=1, source_target_pairs={{0,4},{1,5},{2,6},{3,7},{4,0},{5,1},{6,2},{7,3},{8,12},{9,13},{10,... | collective-permute-start | bytes 737288 | tf_op jit(solution)/shard_map/ppermute | solution.py:21
  4.0 1.6 %collective-permute-start.4 = (bf16[320,384]{1,0:T(8,128)(2,1)}, bf16[320,384]{1,0:T(8,128)(2,1)S(1)}, u32[]{:S(2)}, u32[]{:S(2)}) collective-permute-start(bf16[320,384]{1,0:T(8,128)(2,1)} %bitcast.57), channel_id=1, source_target_pairs={{0,2},{1,3},{2,0},{3,1},{4,6},{5,7},{6,4},{7,5},{8,10},{9,11},{10,... | collective-permute-start | bytes 737288 | tf_op jit(solution)/shard_map/ppermute | solution.py:21
  5.6 0.0 collective-permute-done.refs_1_
  5.6 10.4 %conditional.1 = (f32[2,384]{1,0:T(2,128)S(1)}, bf16[384,384]{1,0:T(8,128)(2,1)S(1)}, bf16[384,384]{1,0:T(8,128)(2,1)S(1)}, f32[6,384]{1,0:T(8,128)S(1)}, f32[1,2,384]{2,1,0:T(2,128)S(1)}) conditional(s32[]{:T(128)} %convert_element_type.7, () %tuple.16, (bf16[320,384]{1,0:T(8,128)(2,1)}, bf16[320,384]{1,0:T(8,128)(2,1)S(1)}, ...), branch_computations={%region_0.0_spmd, %region_1.0_spmd} | conditional | flops 227551360 | bytes 605240 | solution.py:311
  5.6 1.8 %local_stats.1 = f32[4,2,384]{2,1,0:T(2,128)} custom-call(bf16[320,384]{1,0:T(8,128)(2,1)} %get-tuple-element.30.own_hbm, bf16[320,384]{1,0:T(8,128)(2,1)S(1)} %get-tuple-element.31.other_ref), custom_call_target="tpu_custom_call" | custom-call | flops 1048576 | tf_op jit(solution)/shard_map/cond/branch_1_fun/local_stats/pallas_call | solution.py:69
  7.4 3.7 %all-to-all-start = ((f32[4,2,384]{2,1,0:T(2,128)}), f32[4,2,384]{2,1,0:T(2,128)S(1)}, u32[]{:S(2)}, u32[]{:S(2)}) async-start(f32[4,2,384]{2,1,0:T(2,128)} %local_stats.1), calls=%async_computation | async-start | bytes 24576 | tf_op jit(solution)/shard_map/cond/branch_1_fun/all_to_all | solution.py:306
  11.2 1.8 %prepare.1 = (bf16[384,384]{1,0:T(8,128)(2,1)S(1)}, bf16[384,384]{1,0:T(8,128)(2,1)S(1)}, f32[6,384]{1,0:T(8,128)S(1)}) custom-call(bf16[384,384]{1,0:T(8,128)(2,1)} %get-tuple-element.73.query_ref, bf16[384,384]{1,0:T(8,128)(2,1)} %get-tuple-element.74.key_ref, bf16[384,384]{1,0:T(8,128)(2,1)} %get-tuple-element.75.value_ref, ...), custom_call_target="tpu_custom_call" | custom-call | flops 226492416 | tf_op jit(solution)/shard_map/cond/branch_1_fun/prepare/pallas_call | solution.py:93
  13.0 2.9 %all-to-all-done = f32[4,2,384]{2,1,0:T(2,128)S(1)} async-done(((f32[4,2,384]{2,1,0:T(2,128)}), f32[4,2,384]{2,1,0:T(2,128)S(1)}, u32[]{:S(2)}, u32[]{:S(2)}) %all-to-all-start) | async-done | bytes 12320 | tf_op jit(solution)/shard_map/cond/branch_1_fun/all_to_all | solution.py:306
  16.0 0.4 collective-permute-start.1
  16.4 0.0 collective-permute-done.3.refs_4_
  16.4 0.1 collective-permute-done.4.refs_2_
  16.4 1.5 %collective-permute-start.7 = (bf16[320,384]{1,0:T(8,128)(2,1)S(1)}, bf16[320,384]{1,0:T(8,128)(2,1)S(1)}, u32[]{:S(2)}, u32[]{:S(2)}) collective-permute-start(bf16[320,384]{1,0:T(8,128)(2,1)S(1)} %collective-permute-done.3.refs_4_), channel_id=1, source_target_pairs={{0,2},{1,3},{2,0},{3,1},{4,6},{5,7},{6,4},{7,5},{8,10},{9,11},{10,... | collective-permute-start | bytes 737288 | tf_op jit(solution)/shard_map/ppermute | solution.py:21
  18.0 2.7 %collective-permute-done.1 = f32[2,384]{1,0:T(2,128)S(1)} collective-permute-done((f32[2,384]{1,0:T(2,128)S(1)}, f32[2,384]{1,0:T(2,128)S(1)}, u32[]{:S(2)}, u32[]{:S(2)}) %collective-permute-start.1) | collective-permute-done | bytes 3104 | tf_op jit(solution)/shard_map/ppermute | solution.py:21
  20.7 0.4 collective-permute-start.2
  21.1 0.0 collective-permute-start.6
  21.1 0.5 collective-permute-start.5
  21.7 2.7 %collective-permute-done.2 = f32[2,384]{1,0:T(2,128)S(1)} collective-permute-done((f32[2,384]{1,0:T(2,128)S(1)}, f32[2,384]{1,0:T(2,128)S(1)}, u32[]{:S(2)}, u32[]{:S(2)}) %collective-permute-start.2) | collective-permute-done | bytes 3104 | tf_op jit(solution)/shard_map/ppermute | solution.py:21
  24.4 0.0 collective-permute-done.7.refs_6_
  24.4 0.1 collective-permute-start.8
  24.6 0.0 collective-permute-done.6.refs_5_
  24.6 0.0 collective-permute-done.5.refs_3_
  24.6 1.4 %collective-permute-done.8.refs_7_ = bf16[320,384]{1,0:T(8,128)(2,1)S(1)} collective-permute-done((bf16[320,384]{1,0:T(8,128)(2,1)S(1)}, bf16[320,384]{1,0:T(8,128)(2,1)S(1)}, u32[]{:S(2)}, u32[]{:S(2)}) %collective-permute-start.8) | collective-permute-done | bytes 245792 | tf_op jit(solution)/shard_map/ppermute | solution.py:21
  26.0 8.5 %attention.1 = (bf16[480,384]{1,0:T(8,128)(2,1)S(1)}, f32[32,2,384]{2,1,0:T(2,128)}) custom-call(s32[1]{0:T(128)} %bitcast.4.below_ref, f32[2,384]{1,0:T(2,128)S(1)} %pad_maximum_fusion.4.stats_ref, bf16[384,384]{1,0:T(8,128)(2,1)S(1)} %get-tuple-element.56.qk_ref, bf16[384,384]{1,0:T(8,128)(2,1)S(1)} %get-tuple-element.57.vo_ref, ...), custom_call_target="tpu_custom_call" | custom-call | tf_op jit(solution)/shard_map/attention/pallas_call | solution.py:157
  34.5 3.0 %collective-permute-start.9 = (bf16[480,384]{1,0:T(8,128)(2,1)S(1)}, bf16[480,384]{1,0:T(8,128)(2,1)S(1)}, u32[]{:S(2)}, u32[]{:S(2)}) collective-permute-start(bf16[480,384]{1,0:T(8,128)(2,1)S(1)} %get-tuple-element.61.current_ref), channel_id=1, source_target_pairs={{0,8},{8,16},{16,24},{1,9},{9,17},{17,25},{2,10},{10,18},{18,26},{... | collective-permute-start | bytes 1105928 | tf_op jit(solution)/shard_map/ppermute | solution.py:344
  37.5 5.1 %all-to-all-start.1 = ((f32[32,2,384]{2,1,0:T(2,128)}), f32[32,2,384]{2,1,0:T(2,128)S(1)}, u32[]{:S(2)}, u32[]{:S(2)}) async-start(f32[32,2,384]{2,1,0:T(2,128)} %get-tuple-element.62), calls=%async_computation.1 | async-start | bytes 196608 | tf_op jit(solution)/shard_map/all_to_all | solution.py:345
  42.6 0.1 add_convert_fusion.valid_ref
  42.7 7.7 %all-to-all-done.1.stats_ref = f32[32,2,384]{2,1,0:T(2,128)S(1)} async-done(((f32[32,2,384]{2,1,0:T(2,128)}), f32[32,2,384]{2,1,0:T(2,128)S(1)}, u32[]{:S(2)}, u32[]{:S(2)}) %all-to-all-start.1) | async-done | bytes 98336 | tf_op jit(solution)/shard_map/all_to_all | solution.py:345
  50.4 0.0 collective-permute-done.9.earlier_ref
  50.4 8.8 %upsample.1 = bf16[2,4,320,384]{3,2,1,0:T(8,128)(2,1)} custom-call(s32[2]{0:T(128)S(1)} %add_convert_fusion.valid_ref, bf16[480,384]{1,0:T(8,128)(2,1)S(1)} %get-tuple-element.61.current_ref, bf16[480,384]{1,0:T(8,128)(2,1)S(1)} %collective-permute-done.9.earlier_ref, f32[32,2,384]{2,1,0:T(2,128)S(1)} %all-to-all-done.1.stats_ref, ...), custom_call_target="tpu_custom_call" | custom-call | tf_op jit(solution)/shard_map/upsample/pallas_call | solution.py:256
  (21 shorter events, 0.2 us)
Async XLA Ops:
  0.0 5.6 %collective-permute-start = (bf16[320,384]{1,0:T(8,128)(2,1)}, bf16[320,384]{1,0:T(8,128)(2,1)S(1)}, u32[]{:S(2)}, u32[]{:S(2)}) collective-permute-start(bf16[320,384]{1,0:T(8,128)(2,1)} %bitcast.55), channel_id=1, source_target_pairs={{0,1},{1,0},{2,3},{3,2},{4,5},{5,4},{6,7},{7,6},{8,9},{9,8},{10,11... | collective-permute-start | bytes 737288 | tf_op jit(solution)/shard_map/ppermute | solution.py:21
  0.5 15.9 %collective-permute-start.3 = (bf16[320,384]{1,0:T(8,128)(2,1)}, bf16[320,384]{1,0:T(8,128)(2,1)S(1)}, u32[]{:S(2)}, u32[]{:S(2)}) collective-permute-start(bf16[320,384]{1,0:T(8,128)(2,1)} %bitcast.56), channel_id=1, source_target_pairs={{0,4},{1,5},{2,6},{3,7},{4,0},{5,1},{6,2},{7,3},{8,12},{9,13},{10,... | collective-permute-start | bytes 737288 | tf_op jit(solution)/shard_map/ppermute | solution.py:21
  4.0 12.4 %collective-permute-start.4 = (bf16[320,384]{1,0:T(8,128)(2,1)}, bf16[320,384]{1,0:T(8,128)(2,1)S(1)}, u32[]{:S(2)}, u32[]{:S(2)}) collective-permute-start(bf16[320,384]{1,0:T(8,128)(2,1)} %bitcast.57), channel_id=1, source_target_pairs={{0,2},{1,3},{2,0},{3,1},{4,6},{5,7},{6,4},{7,5},{8,10},{9,11},{10,... | collective-permute-start | bytes 737288 | tf_op jit(solution)/shard_map/ppermute | solution.py:21
  7.4 8.4 %all-to-all-start = ((f32[4,2,384]{2,1,0:T(2,128)}), f32[4,2,384]{2,1,0:T(2,128)S(1)}, u32[]{:S(2)}, u32[]{:S(2)}) async-start(f32[4,2,384]{2,1,0:T(2,128)} %local_stats.1), calls=%async_computation | async-start | bytes 24576 | tf_op jit(solution)/shard_map/cond/branch_1_fun/all_to_all | solution.py:306
  16.0 4.7 %collective-permute-start.1 = (f32[2,384]{1,0:T(2,128)S(1)}, f32[2,384]{1,0:T(2,128)S(1)}, u32[]{:S(2)}, u32[]{:S(2)}) collective-permute-start(f32[2,384]{1,0:T(2,128)S(1)} %get-tuple-element.55), channel_id=1, source_target_pairs={{0,4},{1,5},{2,6},{3,7},{4,0},{5,1},{6,2},{7,3},{8,12},{9,13},{10,... | collective-permute-start | bytes 9224 | tf_op jit(solution)/shard_map/ppermute | solution.py:21
  16.4 8.0 %collective-permute-start.7 = (bf16[320,384]{1,0:T(8,128)(2,1)S(1)}, bf16[320,384]{1,0:T(8,128)(2,1)S(1)}, u32[]{:S(2)}, u32[]{:S(2)}) collective-permute-start(bf16[320,384]{1,0:T(8,128)(2,1)S(1)} %collective-permute-done.3.refs_4_), channel_id=1, source_target_pairs={{0,2},{1,3},{2,0},{3,1},{4,6},{5,7},{6,4},{7,5},{8,10},{9,11},{10,... | collective-permute-start | bytes 737288 | tf_op jit(solution)/shard_map/ppermute | solution.py:21
  20.7 3.7 %collective-permute-start.2 = (f32[2,384]{1,0:T(2,128)S(1)}, f32[2,384]{1,0:T(2,128)S(1)}, u32[]{:S(2)}, u32[]{:S(2)}) collective-permute-start(f32[2,384]{1,0:T(2,128)S(1)} %get-tuple-element.92), channel_id=1, source_target_pairs={{0,2},{1,3},{2,0},{3,1},{4,6},{5,7},{6,4},{7,5},{8,10},{9,11},{10,... | collective-permute-start | bytes 9224 | tf_op jit(solution)/shard_map/ppermute | solution.py:21
  21.1 3.4 %collective-permute-start.6 = (bf16[320,384]{1,0:T(8,128)(2,1)S(1)}, bf16[320,384]{1,0:T(8,128)(2,1)S(1)}, u32[]{:S(2)}, u32[]{:S(2)}) collective-permute-start(bf16[320,384]{1,0:T(8,128)(2,1)S(1)} %collective-permute-done.3.refs_4_), channel_id=1, source_target_pairs={{0,1},{1,0},{2,3},{3,2},{4,5},{5,4},{6,7},{7,6},{8,9},{9,8},{10,11... | collective-permute-start | bytes 737288 | tf_op jit(solution)/shard_map/ppermute | solution.py:21
  21.1 3.4 %collective-permute-start.5 = (bf16[320,384]{1,0:T(8,128)(2,1)S(1)}, bf16[320,384]{1,0:T(8,128)(2,1)S(1)}, u32[]{:S(2)}, u32[]{:S(2)}) collective-permute-start(bf16[320,384]{1,0:T(8,128)(2,1)S(1)} %collective-permute-done.4.refs_2_), channel_id=1, source_target_pairs={{0,1},{1,0},{2,3},{3,2},{4,5},{5,4},{6,7},{7,6},{8,9},{9,8},{10,11... | collective-permute-start | bytes 737288 | tf_op jit(solution)/shard_map/ppermute | solution.py:21
  24.4 1.6 %collective-permute-start.8 = (bf16[320,384]{1,0:T(8,128)(2,1)S(1)}, bf16[320,384]{1,0:T(8,128)(2,1)S(1)}, u32[]{:S(2)}, u32[]{:S(2)}) collective-permute-start(bf16[320,384]{1,0:T(8,128)(2,1)S(1)} %collective-permute-done.7.refs_6_), channel_id=1, source_target_pairs={{0,1},{1,0},{2,3},{3,2},{4,5},{5,4},{6,7},{7,6},{8,9},{9,8},{10,11... | collective-permute-start | bytes 737288 | tf_op jit(solution)/shard_map/ppermute | solution.py:21
  34.5 15.8 %collective-permute-start.9 = (bf16[480,384]{1,0:T(8,128)(2,1)S(1)}, bf16[480,384]{1,0:T(8,128)(2,1)S(1)}, u32[]{:S(2)}, u32[]{:S(2)}) collective-permute-start(bf16[480,384]{1,0:T(8,128)(2,1)S(1)} %get-tuple-element.61.current_ref), channel_id=1, source_target_pairs={{0,8},{8,16},{16,24},{1,9},{9,17},{17,25},{2,10},{10,18},{18,26},{... | collective-permute-start | bytes 1105928 | tf_op jit(solution)/shard_map/ppermute | solution.py:344
  37.5 12.9 %all-to-all-start.1 = ((f32[32,2,384]{2,1,0:T(2,128)}), f32[32,2,384]{2,1,0:T(2,128)S(1)}, u32[]{:S(2)}, u32[]{:S(2)}) async-start(f32[32,2,384]{2,1,0:T(2,128)} %get-tuple-element.62), calls=%async_computation.1 | async-start | bytes 196608 | tf_op jit(solution)/shard_map/all_to_all | solution.py:345

commit v3 on v2

v3 whole, which is shorter than its diff:
```python
import functools
import math

import jax
import jax.numpy as jnp
import numpy as np
from jax import lax
from jax.experimental import pallas as pl
from jax.experimental.pallas import tpu as pltpu
from jax.sharding import PartitionSpec as P

GROUPS = 32
EPS = 1e-05
F32 = jnp.float32
BF16 = jnp.bfloat16
VMEM_LIMIT = 26 * 1024 * 1024
AT_ONCE = 8


def swapped(value, axis, mask):
    count = lax.axis_size(axis)
    return lax.ppermute(value, axis, [(i, i ^ mask) for i in range(count)])


def group_sum(vector, same_group):
    row = lax.broadcasted_iota(jnp.int32, (8, vector.shape[1]), 0)
    parts = jnp.zeros((8, vector.shape[1]), F32)
    for i in range(3):
        part = vector.astype(BF16).astype(F32)
        vector = vector - part
        parts = jnp.where(row == i, part, parts)
    summed = jnp.dot(parts.astype(BF16), same_group, preferred_element_type=F32)
    return jnp.sum(summed, axis=0, keepdims=True)


def mean_and_spread(blocks):
    count = len(blocks) * blocks[0].shape[0]
    mean = sum(jnp.sum(b, axis=0, keepdims=True) for b in blocks) * (1.0 / count)
    return mean, sum(jnp.sum(jnp.square(b - mean), axis=0, keepdims=True) for b in blocks)


def group_mean_and_variance(means, spread, count, same_group):
    per_group = means.shape[1] // GROUPS
    mean = group_sum(means, same_group) * (1.0 / per_group)
    gap = means - mean
    total = group_sum(spread + gap * gap * count, same_group)
    return mean, total * (1.0 / (per_group * count))


def stats_kernel(own_hbm, other_ref, out_ref, own_ref, sem):
    copy = pltpu.make_async_copy(own_hbm, own_ref, sem)
    copy.start()
    copy.wait()
    mean, spread = mean_and_spread([own_ref[...].astype(F32), other_ref[...].astype(F32)])
    for i in range(out_ref.shape[0]):
        out_ref[i, 0:1, :] = mean
        out_ref[i, 1:2, :] = spread


def local_stats(own, other, copies):
    vmem = pl.BlockSpec(memory_space=pltpu.VMEM)
    return pl.pallas_call(
        stats_kernel,
        out_shape=(
            jax.ShapeDtypeStruct((copies, 2, own.shape[1]), F32),
            jax.ShapeDtypeStruct(own.shape, own.dtype),
        ),
        in_specs=[pl.BlockSpec(memory_space=pl.ANY), vmem],
        out_specs=(vmem, vmem),
        scratch_shapes=[pltpu.SemaphoreType.DMA],
        cost_estimate=pl.CostEstimate(flops=1 << 20, bytes_accessed=0, transcendentals=0),
        name="local_stats",
    )(own, other)


SPACE_TAPS = (((1, 0),), ((2, 0), (0, 1)))


def prepare_kernel(query_ref, key_ref, value_ref, mix_ref, *refs):
    *vector_refs, qk_ref, vo_ref, vectors_ref, same_ref = refs
    width = query_ref.shape[0]
    qk_ref[...] = lax.dot_general(
        query_ref[...], key_ref[...], (((1,), (1,)), ((), ())), preferred_element_type=F32
    ).astype(BF16)
    vo_ref[...] = jnp.dot(value_ref[...], mix_ref[...], preferred_element_type=F32).astype(BF16)
    for i, ref in enumerate(vector_refs):
        vectors_ref[i : i + 1, :] = ref[...].reshape(1, width)
    groups = [
        jnp.floor((lax.broadcasted_iota(jnp.int32, (width, width), d).astype(F32) + 0.5) * (GROUPS / width))
        for d in range(2)
    ]
    same_ref[...] = jnp.where(groups[0] == groups[1], 1.0, 0.0).astype(BF16)


def prepare(query, key, value, mix, *vectors):
    square = jax.ShapeDtypeStruct(query.shape, BF16)
    return pl.pallas_call(
        prepare_kernel,
        out_shape=(square, square, jax.ShapeDtypeStruct((len(vectors), query.shape[0]), F32), square),
        cost_estimate=pl.CostEstimate(flops=4 * query.shape[0] ** 3, bytes_accessed=0, transcendentals=0),
        name="prepare",
    )(query, key, value, mix, *vectors)


def merged(stats, count):
    mean = jnp.mean(stats[:, 0], axis=0, keepdims=True)
    gap = stats[:, 0] - mean
    return mean, jnp.sum(stats[:, 1] + gap * gap * count, axis=0, keepdims=True)


def attention_kernel(count, distance_ref, stats_ref, qk_ref, vo_ref, vectors_ref, same_ref, *refs):
    *blocks, mixed_ref, out_stats_ref = refs
    positions, width = blocks[0].shape
    cols = positions // 2
    mean, variance = group_mean_and_variance(
        stats_ref[0:1, :], stats_ref[1:2, :], count, same_ref[...]
    )
    gain, shift, bias = (vectors_ref[i : i + 1, :] for i in range(3))
    factor = gain * lax.rsqrt(variance + EPS)
    offset = shift - mean * factor
    scale = width ** (-0.5) * math.log2(math.e)
    below = blocks[1][0:cols, :]
    mask = 3
    while mask < len(blocks):
        below = jnp.where(distance_ref[0] == mask, blocks[mask][0:cols, :], below)
        mask = 2 * mask + 1
    own = jnp.concatenate([blocks[0][...], below], axis=0).astype(F32)
    normed = ((own - mean) * factor + shift).astype(BF16)
    turned = jnp.dot(normed, qk_ref[...], preferred_element_type=F32) * scale
    constant = jnp.sum(turned * offset, axis=1, keepdims=True)
    queries = (turned * factor).astype(BF16)
    highest = None
    for first in range(0, len(blocks), AT_ONCE):
        keys = jnp.concatenate([block[...] for block in blocks[first : first + AT_ONCE]], axis=0)
        scores = lax.dot_general(
            queries, keys, (((1,), (1,)), ((), ())), preferred_element_type=F32
        )
        newest = jnp.max(scores, axis=1, keepdims=True) + constant
        if highest is not None:
            newest = jnp.maximum(highest, newest)
        probs = jnp.exp2(scores + (constant - newest)).astype(BF16)
        part = jnp.sum(probs.astype(F32), axis=1, keepdims=True)
        product = jnp.dot(probs, keys, preferred_element_type=F32)
        if highest is None:
            total, summed = part, product
        else:
            fade = jnp.exp2(highest - newest)
            total, summed = total * fade + part, summed * fade + product
        highest = newest
    attended = ((summed / total - mean) * factor + shift).astype(BF16)
    branch = jnp.dot(attended, vo_ref[...], preferred_element_type=F32) + bias
    mixed = (own + branch).astype(BF16)
    mixed_ref[...] = mixed
    mean, spread = mean_and_spread([mixed[:positions].astype(F32)])
    for i in range(out_stats_ref.shape[0]):
        out_stats_ref[i, 0:1, :] = mean
        out_stats_ref[i, 1:2, :] = spread


def attention(blocks, distance, stats, count, qk, vo, vectors, same_group, stat_copies):
    positions, width = blocks[0].shape
    vmem = pl.BlockSpec(memory_space=pltpu.VMEM)
    return pl.pallas_call(
        functools.partial(attention_kernel, count),
        out_shape=(
            jax.ShapeDtypeStruct((positions // 2 * 3, width), BF16),
            jax.ShapeDtypeStruct((stat_copies, 2, width), F32),
        ),
        in_specs=[pl.BlockSpec(memory_space=pltpu.SMEM)] + [vmem] * (5 + len(blocks)),
        out_specs=(vmem, vmem),
        compiler_params=pltpu.CompilerParams(vmem_limit_bytes=VMEM_LIMIT * (2 if len(blocks) > AT_ONCE else 1)),
        name="attention",
    )(distance, stats, qk, vo, vectors, same_group, *blocks)


def fetch_kernel(after, weight_hbm, middle_ref, sem):
    copy = pltpu.make_async_copy(weight_hbm.at[:, 1], middle_ref, sem)
    copy.start()
    copy.wait()


def fetch(after, weight):
    width = weight.shape[-1]
    anywhere = pl.BlockSpec(memory_space=pl.ANY)
    return pl.pallas_call(
        fetch_kernel,
        out_shape=pltpu.VMEM((3, 3, width, width), BF16),
        in_specs=[anywhere, anywhere],
        out_specs=pl.BlockSpec(memory_space=pltpu.VMEM),
        scratch_shapes=[pltpu.SemaphoreType.DMA],
        cost_estimate=pl.CostEstimate(flops=0, bytes_accessed=36 * width**2, transcendentals=0),
        compiler_params=pltpu.CompilerParams(vmem_limit_bytes=VMEM_LIMIT),
        name="fetch",
    )(after, pltpu.with_memory_space_constraint(weight, pltpu.HBM))


def upsample_kernel(count, valid_ref, current_ref, earlier_ref, stats_ref, vectors_ref, same_ref, middle_ref, weight_hbm, out_hbm, now, before, wide, out, weight, weight_sems, out_sems):
    positions, width = current_ref.shape
    cols = positions // 3
    copies = {
        r: pltpu.make_async_copy(weight_hbm.at[:, r], weight.at[:, r // 2], weight_sems.at[r // 2]) for r in (2, 0)
    }
    for copy in copies.values():
        copy.start()
    mean, variance = group_mean_and_variance(
        *merged(stats_ref[...], count // stats_ref.shape[0]), count, same_ref[...]
    )
    gain, shift, bias = (vectors_ref[i : i + 1, :] for i in range(3, 6))
    factor = gain * lax.rsqrt(variance + EPS)
    col = lax.broadcasted_iota(jnp.int32, (cols, width), 0)
    for target, source_ref, known in ((now, current_ref, None), (before, earlier_ref, valid_ref[1])):
        for row in range(3):
            source = source_ref[row * cols : (row + 1) * cols, :]
            value = (source.astype(F32) - mean) * factor + shift
            value = value / (1.0 + jnp.exp(-value))
            kept = known
            if row == 2:
                kept = valid_ref[0] if known is None else valid_ref[0] * known
            if kept is not None:
                value = jnp.where(kept > 0, value, 0.0)
            here = slice(row * cols, (row + 1) * cols)
            target[here, 0:width] = value.astype(BF16)
            moved = jnp.where(col == cols - 1, 0.0, pltpu.roll(value, cols - 1, 0))
            target[here, width : 2 * width] = moved.astype(BF16)
    out_copies = []

    def multiplied(odd_row, odd_col):
        taps = [(r, c) for r, _ in SPACE_TAPS[odd_row] for c, _ in SPACE_TAPS[odd_col]]

        def product(active, *times):
            lanes = slice(0, 2 * width if odd_col else width)
            windows = [active[step * cols : (step + 2) * cols, lanes] for _, step in SPACE_TAPS[odd_row]]
            stacked = [jnp.concatenate([(middle_ref[t, c] if r == 1 else weight[t, r // 2, c]) for t in times], axis=1) for r, c in taps]
            return jnp.dot(
                jnp.concatenate(windows, axis=1),
                jnp.concatenate(stacked, axis=0),
                preferred_element_type=F32,
            )

        both = product(now, 0, 1)
        return both[:, :width] + product(before, 2) + bias, both[:, width:] + bias

    def stored(odd_row, odd_col, sums):
        for odd_time, summed in enumerate(sums):
            for row in range(2):
                for lane in range(width // 128):
                    wide[odd_time, row, lane, pl.ds(odd_col, cols, stride=2), :] = summed[
                        row * cols : (row + 1) * cols, lane * 128 : (lane + 1) * 128
                    ]
                if odd_col == 1:
                    for lane in range(width // 128):
                        out[odd_time, row, odd_row, :, lane * 128 : (lane + 1) * 128] = wide[
                            odd_time, row, lane
                        ].astype(BF16)
            if odd_col == 1:
                place = (odd_time, slice(None), odd_row)
                copy = pltpu.make_async_copy(
                    out.at[*place], out_hbm.at[*place], out_sems.at[odd_time, odd_row]
                )
                copy.start()
                out_copies.append(copy)

    first = [(phase, multiplied(*phase)) for phase in ((0, 0), (0, 1))]
    stored(*first[0][0], first[0][1])
    for copy in copies.values():
        copy.wait()
    stored(*first[1][0], first[1][1])
    for phase in ((1, 0), (1, 1)):
        stored(*phase, multiplied(*phase))
    for copy in out_copies:
        copy.wait()


def upsample(valid, current, earlier, stats, count, vectors, same_group, middle, weight):
    positions, width = current.shape
    cols = positions // 3
    vmem = pl.BlockSpec(memory_space=pltpu.VMEM)
    result = pl.pallas_call(
        functools.partial(upsample_kernel, count),
        out_shape=jax.ShapeDtypeStruct((2, 2, 2, 2 * cols, width), BF16),
        in_specs=[pl.BlockSpec(memory_space=pltpu.SMEM)]
        + [vmem] * 6
        + [pl.BlockSpec(memory_space=pl.ANY)],
        out_specs=pl.BlockSpec(memory_space=pl.ANY),
        scratch_shapes=[
            pltpu.VMEM((3 * cols, 2 * width), BF16),
            pltpu.VMEM((3 * cols, 2 * width), BF16),
            pltpu.VMEM((2, 2, width // 128, 2 * cols, 128), F32),
            pltpu.VMEM((2, 2, 2, 2 * cols, width), BF16),
            pltpu.VMEM((3, 2, 3, width, width), BF16),
            pltpu.SemaphoreType.DMA((2,)),
            pltpu.SemaphoreType.DMA((2, 2)),
        ],
        compiler_params=pltpu.CompilerParams(vmem_limit_bytes=VMEM_LIMIT),
        name="upsample",
    )(
        valid, current, earlier, stats, vectors, same_group, middle, pltpu.with_memory_space_constraint(weight, pltpu.HBM)
    )
    return result.reshape(2, 4, 2 * cols, width)


def local(
    latent,
    first_gain,
    first_shift,
    query_weight,
    key_weight,
    value_weight,
    out_weight,
    out_bias,
    second_gain,
    second_shift,
    up_weight,
    up_bias,
):
    frames, rows, cols, width = latent.shape
    positions = rows * cols
    height, groups = lax.axis_size("height"), lax.axis_size("frames")
    slab, group = lax.axis_index("height"), lax.axis_index("frames")
    count = positions * height * groups
    block = latent.reshape(positions, width)

    slots = {0: block, 1: swapped(block, "height", 1)}
    direct = [1 << i for i in range(1, (height - 1).bit_length())][::-1]
    forwarded = sorted((m for m in range(2, height, 2) if m not in direct), key=lambda m: (bin(m).count("1"), -m))
    for mask in direct:
        slots[mask] = swapped(block, "height", mask)
    held = 2 * positions

    def early_work(own, other, *parameters):
        stats, own = local_stats(own, other, groups)
        stats = lax.all_to_all(stats, "frames", split_axis=0, concat_axis=0, tiled=True)
        return jnp.concatenate(merged(stats, held), axis=0), own, *prepare(*parameters)

    parameters = (query_weight, key_weight, value_weight, out_weight)
    parameters += (first_gain, first_shift, out_bias, second_gain, second_shift, up_bias)
    first, slots[0], qk, vo, vectors, same_group = lax.cond(
        group < groups,
        early_work,
        lambda *arguments: jax.tree.map(
            lambda kind: jnp.zeros(kind.shape, kind.dtype), jax.eval_shape(early_work, *arguments)
        ),
        block,
        slots[1],
        *parameters,
    )
    held = held * groups
    ready = lax.optimization_barrier([slots[m] for m in direct])
    slots.update(zip(direct, ready))
    for mask in forwarded:
        lowest = mask & -mask
        slots[mask] = swapped(slots[mask ^ lowest], "height", lowest)
    for mask in direct:
        pair = jnp.stack([first, swapped(first, "height", mask)])
        first, held = jnp.concatenate(merged(pair, held), axis=0), held * 2
    for mask in direct + forwarded:
        slots[mask | 1] = swapped(slots[mask], "height", 1)
    distance = (slab ^ (slab + 1)).astype(jnp.int32).reshape(1)

    blocks = [slots[m] for m in range(height)]
    mixed, second = attention(
        blocks, distance, first, count, qk, vo, vectors, same_group, groups * height
    )
    middle = fetch(mixed, up_weight)
    earlier = lax.ppermute(mixed, "frames", [(i, i + 1) for i in range(groups - 1)])
    second = lax.all_to_all(second, ("frames", "height"), split_axis=0, concat_axis=0, tiled=True)
    valid = jnp.stack([slab + 1 < height, group > 0]).astype(jnp.int32)
    return upsample(
        valid, mixed, earlier, second, count, vectors, same_group, middle, up_weight
    )


def solution(mesh):
    placed = P("frames", "height", None, None)
    return jax.shard_map(
        local,
        mesh=mesh,
        in_specs=(placed,) + (P(),) * 11,
        out_specs=placed,
        check_vma=False,
    )
```

time: 59.5 us -> 54 us (0.908)
  Pallas kernels: 20.9 us -> 17.6 us
  starting transfers between devices: 20.3 us -> 18.9 us
  waiting for transfers between devices: 17.5 us -> 16.7 us
    all_to_all x1, waiting for transfers between devices: 7.7 us -> 5.92 us  [local(): lax.all_to_all(second, ('frames', 'height'), split_axis=0, concat_axis=0,...]
    pallas_call x1, Pallas kernels: 8.81 us -> 7.12 us  [upsample(): pl.pallas_call(functools.partial(upsample_kernel, count), out_shape=jax.S...]
    pallas_call x2 -> x3, Pallas kernels: 10.3 us -> 8.64 us  [the longest x1 5.05 us: attention(): pl.pallas_call(functools.partial(attention_kernel, count), out_shape=(jax...]
    ppermute x9, starting transfers between devices: 8.54 us -> 7.47 us  [swapped(): return lax.ppermute(value, axis, [(i, i ^ mask) for i in range(count)])]
    ppermute x9, waiting for transfers between devices: 6.87 us -> 7.94 us  [swapped(): return lax.ppermute(value, axis, [(i, i ^ mask) for i in range(count)])]
  transfers between devices with their start and end apart: 12 -> 12, of which waited for: 6 -> 6; matrix products, arithmetic and copies ran while one was open for 1% -> 1% of each run, Pallas kernels for 6% -> 10%
where the time goes in v3:
time: 54 us; the launch traced here: 53.7 us
  starting transfers between devices  18.9 us (35%)
  Pallas kernels  17.6 us (33%)
  waiting for transfers between devices  16.7 us (31%)
    ppermute x9, waiting for transfers between devices, swapped(): return lax.ppermute(value, axis, [(i, i ^ mask) for i in range(count)])  7.94 us
    ppermute x9, starting transfers between devices, swapped(): return lax.ppermute(value, axis, [(i, i ^ mask) for i in range(count)])  7.47 us
    pallas_call x1, Pallas kernels, upsample(): pl.pallas_call(functools.partial(upsample_kernel, count), out_shape=jax.S...  7.12 us
    all_to_all x1, waiting for transfers between devices, local(): lax.all_to_all(second, ('frames', 'height'), split_axis=0, concat_axis=0,...  5.92 us
    pallas_call x1, Pallas kernels, attention(): pl.pallas_call(functools.partial(attention_kernel, count), out_shape=(jax...  5.05 us
    all_to_all x1, starting transfers between devices, local(): lax.all_to_all(second, ('frames', 'height'), split_axis=0, concat_axis=0,...  4.81 us
    all_to_all x1, starting transfers between devices, early_work(): lax.all_to_all(stats, 'frames', split_axis=0, concat_axis=0, tiled=True)  3.73 us
    all_to_all x1, waiting for transfers between devices, early_work(): lax.all_to_all(stats, 'frames', split_axis=0, concat_axis=0, tiled=True)  2.87 us
  transfers between devices with their start and end apart: 12, of which 6 were waited for; matrix products, arithmetic and copies ran while one was open for 1% of the time, Pallas kernels for 10%

profile of v3, /device:TPU:0, one launch (start us, length us, event | category | flops | bytes accessed | tf_op | source)
XLA Modules:
  0.0 53.7 jit_solution(11762773193996492100)
XLA Ops:
  0.0 0.5 collective-permute-start
  0.5 2.6 %collective-permute-start.4 = (bf16[320,384]{1,0:T(8,128)(2,1)}, bf16[320,384]{1,0:T(8,128)(2,1)S(1)}, u32[]{:S(2)}, u32[]{:S(2)}) collective-permute-start(bf16[320,384]{1,0:T(8,128)(2,1)} %bitcast.55), channel_id=1, source_target_pairs={{0,2},{1,3},{2,0},{3,1},{4,6},{5,7},{6,4},{7,5},{8,10},{9,11},{10,... | collective-permute-start | bytes 737288 | tf_op jit(solution)/shard_map/ppermute | solution.py:22
  3.0 2.6 %collective-permute-start.3 = (bf16[320,384]{1,0:T(8,128)(2,1)}, bf16[320,384]{1,0:T(8,128)(2,1)S(1)}, u32[]{:S(2)}, u32[]{:S(2)}) collective-permute-start(bf16[320,384]{1,0:T(8,128)(2,1)} %bitcast.56), channel_id=1, source_target_pairs={{0,4},{1,5},{2,6},{3,7},{4,0},{5,1},{6,2},{7,3},{8,12},{9,13},{10,... | collective-permute-start | bytes 737288 | tf_op jit(solution)/shard_map/ppermute | solution.py:22
  5.6 0.0 collective-permute-done.refs_1_
  5.6 10.4 %conditional.1 = (f32[2,384]{1,0:T(2,128)S(1)}, bf16[320,384]{1,0:T(8,128)(2,1)S(1)}, bf16[384,384]{1,0:T(8,128)(2,1)S(1)}, bf16[384,384]{1,0:T(8,128)(2,1)S(1)}...) conditional(s32[]{:T(128)} %convert_element_type.7, () %tuple.16, ...), branch_computations={%region_0.0_spmd, %region_1.0_spmd} | conditional | flops 227551360 | bytes 1145932 | solution.py:337
  5.6 1.8 %local_stats.1 = (f32[4,2,384]{2,1,0:T(2,128)}, bf16[320,384]{1,0:T(8,128)(2,1)S(1)}) custom-call(bf16[320,384]{1,0:T(8,128)(2,1)} %get-tuple-element.30.own_hbm, bf16[320,384]{1,0:T(8,128)(2,1)S(1)} %get-tuple-element.31.other_ref), custom_call_target="tpu_custom_call" | custom-call | flops 1048576 | tf_op jit(solution)/shard_map/cond/branch_1_fun/local_stats/pallas_call | solution.py:62
  7.5 3.7 %all-to-all-start = ((f32[4,2,384]{2,1,0:T(2,128)}), f32[4,2,384]{2,1,0:T(2,128)S(1)}, u32[]{:S(2)}, u32[]{:S(2)}) async-start(f32[4,2,384]{2,1,0:T(2,128)} %get-tuple-element.32), calls=%async_computation | async-start | bytes 24576 | tf_op jit(solution)/shard_map/cond/branch_1_fun/all_to_all | solution.py:332
  11.2 1.8 %prepare.1 = (bf16[384,384]{1,0:T(8,128)(2,1)S(1)}, bf16[384,384]{1,0:T(8,128)(2,1)S(1)}, f32[6,384]{1,0:T(8,128)S(1)}, bf16[384,384]{1,0:T(8,128)(2,1)S(1)}) custom-call(bf16[384,384]{1,0:T(8,128)(2,1)} %get-tuple-element.80.query_ref, bf16[384,384]{1,0:T(8,128)(2,1)} %get-tuple-element.81.key_ref, bf16[384,384]{1,0:T(8,128)(2,1)} %get-tuple-element.82.value_ref, ...), custom_call_target="tpu_custom_call" | custom-call | flops 226492416 | tf_op jit(solution)/shard_map/cond/branch_1_fun/prepare/pallas_call | solution.py:97
  13.0 2.9 %all-to-all-done = f32[4,2,384]{2,1,0:T(2,128)S(1)} async-done(((f32[4,2,384]{2,1,0:T(2,128)}), f32[4,2,384]{2,1,0:T(2,128)S(1)}, u32[]{:S(2)}, u32[]{:S(2)}) %all-to-all-start) | async-done | bytes 12320 | tf_op jit(solution)/shard_map/cond/branch_1_fun/all_to_all | solution.py:332
  16.0 0.0 copy-start
  16.0 0.4 collective-permute-start.1
  16.4 0.0 collective-permute-done.4.refs_2_
  16.4 1.1 %collective-permute-done.3.refs_4_ = bf16[320,384]{1,0:T(8,128)(2,1)S(1)} collective-permute-done((bf16[320,384]{1,0:T(8,128)(2,1)}, bf16[320,384]{1,0:T(8,128)(2,1)S(1)}, u32[]{:S(2)}, u32[]{:S(2)}) %collective-permute-start.3) | collective-permute-done | bytes 245792 | tf_op jit(solution)/shard_map/ppermute | solution.py:22
  17.6 0.4 collective-permute-start.7
  18.0 2.7 %collective-permute-done.1 = f32[2,384]{1,0:T(2,128)S(1)} collective-permute-done((f32[2,384]{1,0:T(2,128)S(1)}, f32[2,384]{1,0:T(2,128)S(1)}, u32[]{:S(2)}, u32[]{:S(2)}) %collective-permute-start.1) | collective-permute-done | bytes 3104 | tf_op jit(solution)/shard_map/ppermute | solution.py:22
  20.8 0.4 collective-permute-start.2
  21.2 0.0 collective-permute-start.6
  21.2 0.5 collective-permute-start.5
  21.7 2.7 %collective-permute-done.2 = f32[2,384]{1,0:T(2,128)S(1)} collective-permute-done((f32[2,384]{1,0:T(2,128)S(1)}, f32[2,384]{1,0:T(2,128)S(1)}, u32[]{:S(2)}, u32[]{:S(2)}) %collective-permute-start.2) | collective-permute-done | bytes 3104 | tf_op jit(solution)/shard_map/ppermute | solution.py:22
  24.4 0.0 collective-permute-done.7.refs_6_
  24.5 0.1 collective-permute-start.8
  24.6 0.0 collective-permute-done.5.refs_3_
  24.6 0.0 collective-permute-done.6.refs_5_
  24.6 1.4 %collective-permute-done.8.refs_7_ = bf16[320,384]{1,0:T(8,128)(2,1)S(1)} collective-permute-done((bf16[320,384]{1,0:T(8,128)(2,1)S(1)}, bf16[320,384]{1,0:T(8,128)(2,1)S(1)}, u32[]{:S(2)}, u32[]{:S(2)}) %collective-permute-start.8) | collective-permute-done | bytes 245792 | tf_op jit(solution)/shard_map/ppermute | solution.py:22
  26.0 5.1 %attention.1 = (bf16[480,384]{1,0:T(8,128)(2,1)S(1)}, f32[32,2,384]{2,1,0:T(2,128)}) custom-call(s32[1]{0:T(128)} %bitcast.4.distance_ref, f32[2,384]{1,0:T(2,128)S(1)} %pad_maximum_fusion.4.stats_ref, bf16[384,384]{1,0:T(8,128)(2,1)S(1)} %get-tuple-element.61.qk_ref, bf16[384,384]{1,0:T(8,128)(2,1)S(1)} %get-tuple-element.62.vo_ref, ...), custom_call_target="tpu_custom_call" | custom-call | tf_op jit(solution)/shard_map/attention/pallas_call | solution.py:163
  31.1 2.9 %collective-permute-start.9 = (bf16[480,384]{1,0:T(8,128)(2,1)S(1)}, bf16[480,384]{1,0:T(8,128)(2,1)S(1)}, u32[]{:S(2)}, u32[]{:S(2)}) collective-permute-start(bf16[480,384]{1,0:T(8,128)(2,1)S(1)} %get-tuple-element.68.after.current_ref), channel_id=1, source_target_pairs={{0,8},{8,16},{16,24},{1,9},{9,17},{17,25},{2,10},{10,18},{18,26},{... | collective-permute-start | bytes 1105928 | tf_op jit(solution)/shard_map/ppermute | solution.py:365
  34.0 4.8 %all-to-all-start.1 = ((f32[32,2,384]{2,1,0:T(2,128)}), f32[32,2,384]{2,1,0:T(2,128)S(1)}, u32[]{:S(2)}, u32[]{:S(2)}) async-start(f32[32,2,384]{2,1,0:T(2,128)} %get-tuple-element.69), calls=%async_computation.1 | async-start | bytes 196608 | tf_op jit(solution)/shard_map/all_to_all | solution.py:366
  38.8 0.1 add_convert_fusion.valid_ref
  38.9 1.8 %fetch.1.middle_ref = bf16[3,3,384,384]{3,2,1,0:T(8,128)(2,1)S(1)} custom-call(bf16[480,384]{1,0:T(8,128)(2,1)S(1)} %get-tuple-element.68.after.current_ref, bf16[3,3,3,384,384]{4,3,2,1,0:T(8,128)(2,1)} %weight_hbm.3), custom_call_target="tpu_custom_call" | custom-call | bytes 5308416 | tf_op jit(solution)/shard_map/fetch/pallas_call | solution.py:185
  40.6 5.9 %all-to-all-done.1.stats_ref = f32[32,2,384]{2,1,0:T(2,128)S(1)} async-done(((f32[32,2,384]{2,1,0:T(2,128)}), f32[32,2,384]{2,1,0:T(2,128)S(1)}, u32[]{:S(2)}, u32[]{:S(2)}) %all-to-all-start.1) | async-done | bytes 98336 | tf_op jit(solution)/shard_map/all_to_all | solution.py:366
  46.6 0.0 collective-permute-done.9.earlier_ref
  46.6 7.1 %upsample.1 = bf16[2,2,2,320,384]{4,3,2,1,0:T(8,128)(2,1)} custom-call(s32[2]{0:T(128)S(1)} %add_convert_fusion.valid_ref, bf16[480,384]{1,0:T(8,128)(2,1)S(1)} %get-tuple-element.68.after.current_ref, bf16[480,384]{1,0:T(8,128)(2,1)S(1)} %collective-permute-done.9.earlier_ref, f32[32,2,384]{2,1,0:T(2,128)S(1)} %all-to-all-done.1.stats_ref, ...), custom_call_target="tpu_custom_call" | custom-call | tf_op jit(solution)/shard_map/upsample/pallas_call | solution.py:278
  (22 shorter events, 0.2 us)
Async XLA Ops:
  0.0 5.6 %collective-permute-start = (bf16[320,384]{1,0:T(8,128)(2,1)}, bf16[320,384]{1,0:T(8,128)(2,1)S(1)}, u32[]{:S(2)}, u32[]{:S(2)}) collective-permute-start(bf16[320,384]{1,0:T(8,128)(2,1)} %bitcast.54), channel_id=1, source_target_pairs={{0,1},{1,0},{2,3},{3,2},{4,5},{5,4},{6,7},{7,6},{8,9},{9,8},{10,11... | collective-permute-start | bytes 737288 | tf_op jit(solution)/shard_map/ppermute | solution.py:22
  0.5 16.0 %collective-permute-start.4 = (bf16[320,384]{1,0:T(8,128)(2,1)}, bf16[320,384]{1,0:T(8,128)(2,1)S(1)}, u32[]{:S(2)}, u32[]{:S(2)}) collective-permute-start(bf16[320,384]{1,0:T(8,128)(2,1)} %bitcast.55), channel_id=1, source_target_pairs={{0,2},{1,3},{2,0},{3,1},{4,6},{5,7},{6,4},{7,5},{8,10},{9,11},{10,... | collective-permute-start | bytes 737288 | tf_op jit(solution)/shard_map/ppermute | solution.py:22
  3.0 14.5 %collective-permute-start.3 = (bf16[320,384]{1,0:T(8,128)(2,1)}, bf16[320,384]{1,0:T(8,128)(2,1)S(1)}, u32[]{:S(2)}, u32[]{:S(2)}) collective-permute-start(bf16[320,384]{1,0:T(8,128)(2,1)} %bitcast.56), channel_id=1, source_target_pairs={{0,4},{1,5},{2,6},{3,7},{4,0},{5,1},{6,2},{7,3},{8,12},{9,13},{10,... | collective-permute-start | bytes 737288 | tf_op jit(solution)/shard_map/ppermute | solution.py:22
  7.5 8.4 %all-to-all-start = ((f32[4,2,384]{2,1,0:T(2,128)}), f32[4,2,384]{2,1,0:T(2,128)S(1)}, u32[]{:S(2)}, u32[]{:S(2)}) async-start(f32[4,2,384]{2,1,0:T(2,128)} %get-tuple-element.32), calls=%async_computation | async-start | bytes 24576 | tf_op jit(solution)/shard_map/cond/branch_1_fun/all_to_all | solution.py:332
  16.0 22.8 %copy-start = (bf16[384,384]{1,0:T(8,128)(2,1)}, bf16[384,384]{1,0:T(8,128)(2,1)S(1)}, u32[]{:S(2)}) copy-start(bf16[384,384]{1,0:T(8,128)(2,1)S(1)} %get-tuple-element.64.same_ref) | copy-start | bytes 884740
  16.0 4.7 %collective-permute-start.1 = (f32[2,384]{1,0:T(2,128)S(1)}, f32[2,384]{1,0:T(2,128)S(1)}, u32[]{:S(2)}, u32[]{:S(2)}) collective-permute-start(f32[2,384]{1,0:T(2,128)S(1)} %get-tuple-element.60), channel_id=1, source_target_pairs={{0,4},{1,5},{2,6},{3,7},{4,0},{5,1},{6,2},{7,3},{8,12},{9,13},{10,... | collective-permute-start | bytes 9224 | tf_op jit(solution)/shard_map/ppermute | solution.py:22
  17.6 6.9 %collective-permute-start.7 = (bf16[320,384]{1,0:T(8,128)(2,1)S(1)}, bf16[320,384]{1,0:T(8,128)(2,1)S(1)}, u32[]{:S(2)}, u32[]{:S(2)}) collective-permute-start(bf16[320,384]{1,0:T(8,128)(2,1)S(1)} %collective-permute-done.3.refs_4_), channel_id=1, source_target_pairs={{0,2},{1,3},{2,0},{3,1},{4,6},{5,7},{6,4},{7,5},{8,10},{9,11},{10,... | collective-permute-start | bytes 737288 | tf_op jit(solution)/shard_map/ppermute | solution.py:22
  20.8 3.7 %collective-permute-start.2 = (f32[2,384]{1,0:T(2,128)S(1)}, f32[2,384]{1,0:T(2,128)S(1)}, u32[]{:S(2)}, u32[]{:S(2)}) collective-permute-start(f32[2,384]{1,0:T(2,128)S(1)} %get-tuple-element.99), channel_id=1, source_target_pairs={{0,2},{1,3},{2,0},{3,1},{4,6},{5,7},{6,4},{7,5},{8,10},{9,11},{10,... | collective-permute-start | bytes 9224 | tf_op jit(solution)/shard_map/ppermute | solution.py:22
  21.2 3.4 %collective-permute-start.6 = (bf16[320,384]{1,0:T(8,128)(2,1)S(1)}, bf16[320,384]{1,0:T(8,128)(2,1)S(1)}, u32[]{:S(2)}, u32[]{:S(2)}) collective-permute-start(bf16[320,384]{1,0:T(8,128)(2,1)S(1)} %collective-permute-done.3.refs_4_), channel_id=1, source_target_pairs={{0,1},{1,0},{2,3},{3,2},{4,5},{5,4},{6,7},{7,6},{8,9},{9,8},{10,11... | collective-permute-start | bytes 737288 | tf_op jit(solution)/shard_map/ppermute | solution.py:22
  21.2 3.4 %collective-permute-start.5 = (bf16[320,384]{1,0:T(8,128)(2,1)S(1)}, bf16[320,384]{1,0:T(8,128)(2,1)S(1)}, u32[]{:S(2)}, u32[]{:S(2)}) collective-permute-start(bf16[320,384]{1,0:T(8,128)(2,1)S(1)} %collective-permute-done.4.refs_2_), channel_id=1, source_target_pairs={{0,1},{1,0},{2,3},{3,2},{4,5},{5,4},{6,7},{7,6},{8,9},{9,8},{10,11... | collective-permute-start | bytes 737288 | tf_op jit(solution)/shard_map/ppermute | solution.py:22
  24.5 1.6 %collective-permute-start.8 = (bf16[320,384]{1,0:T(8,128)(2,1)S(1)}, bf16[320,384]{1,0:T(8,128)(2,1)S(1)}, u32[]{:S(2)}, u32[]{:S(2)}) collective-permute-start(bf16[320,384]{1,0:T(8,128)(2,1)S(1)} %collective-permute-done.7.refs_6_), channel_id=1, source_target_pairs={{0,1},{1,0},{2,3},{3,2},{4,5},{5,4},{6,7},{7,6},{8,9},{9,8},{10,11... | collective-permute-start | bytes 737288 | tf_op jit(solution)/shard_map/ppermute | solution.py:22
  31.1 15.5 %collective-permute-start.9 = (bf16[480,384]{1,0:T(8,128)(2,1)S(1)}, bf16[480,384]{1,0:T(8,128)(2,1)S(1)}, u32[]{:S(2)}, u32[]{:S(2)}) collective-permute-start(bf16[480,384]{1,0:T(8,128)(2,1)S(1)} %get-tuple-element.68.after.current_ref), channel_id=1, source_target_pairs={{0,8},{8,16},{16,24},{1,9},{9,17},{17,25},{2,10},{10,18},{18,26},{... | collective-permute-start | bytes 1105928 | tf_op jit(solution)/shard_map/ppermute | solution.py:365
  34.0 12.6 %all-to-all-start.1 = ((f32[32,2,384]{2,1,0:T(2,128)}), f32[32,2,384]{2,1,0:T(2,128)S(1)}, u32[]{:S(2)}, u32[]{:S(2)}) async-start(f32[32,2,384]{2,1,0:T(2,128)} %get-tuple-element.69), calls=%async_computation.1 | async-start | bytes 196608 | tf_op jit(solution)/shard_map/all_to_all | solution.py:366

commit v4 on v3

--- a/solution.py
+++ b/solution.py
@@ -15,6 +15,7 @@
 BF16 = jnp.bfloat16
 VMEM_LIMIT = 26 * 1024 * 1024
 AT_ONCE = 8
+LANES = 128
 
 
 def swapped(value, axis, mask):
@@ -22,15 +23,18 @@
     return lax.ppermute(value, axis, [(i, i ^ mask) for i in range(count)])
 
 
-def group_sum(vector, same_group):
-    row = lax.broadcasted_iota(jnp.int32, (8, vector.shape[1]), 0)
-    parts = jnp.zeros((8, vector.shape[1]), F32)
-    for i in range(3):
-        part = vector.astype(BF16).astype(F32)
-        vector = vector - part
-        parts = jnp.where(row == i, part, parts)
-    summed = jnp.dot(parts.astype(BF16), same_group, preferred_element_type=F32)
-    return jnp.sum(summed, axis=0, keepdims=True)
+def exact_product(rows, matrix, contracted=0):
+    row = lax.broadcasted_iota(jnp.int32, (8 * len(rows), rows[0].shape[1]), 0)
+    parts = jnp.zeros(row.shape, F32)
+    for i, rest in enumerate(rows):
+        for j in range(3):
+            part = rest.astype(BF16).astype(F32)
+            rest = rest - part
+            parts = jnp.where(row == 8 * i + j, part, parts)
+    summed = lax.dot_general(
+        parts.astype(BF16), matrix, (((1,), (contracted,)), ((), ())), preferred_element_type=F32
+    )
+    return [jnp.sum(summed[8 * i : 8 * i + 8], axis=0, keepdims=True) for i in range(len(rows))]
 
 
 def mean_and_spread(blocks):
@@ -39,12 +43,10 @@
     return mean, sum(jnp.sum(jnp.square(b - mean), axis=0, keepdims=True) for b in blocks)
 
 
-def group_mean_and_variance(means, spread, count, same_group):
-    per_group = means.shape[1] // GROUPS
-    mean = group_sum(means, same_group) * (1.0 / per_group)
+def group_mean_and_spread(means, spread, count, same_group):
+    mean = exact_product([means], same_group)[0] * (GROUPS / means.shape[1])
     gap = means - mean
-    total = group_sum(spread + gap * gap * count, same_group)
-    return mean, total * (1.0 / (per_group * count))
+    return mean, spread + gap * gap * count
 
 
 def stats_kernel(own_hbm, other_ref, out_ref, own_ref, sem):
@@ -77,7 +79,7 @@
 
 
 def prepare_kernel(query_ref, key_ref, value_ref, mix_ref, *refs):
-    *vector_refs, qk_ref, vo_ref, vectors_ref, same_ref = refs
+    *vector_refs, qk_ref, vo_ref, vectors_ref, same_ref, member_ref = refs
     width = query_ref.shape[0]
     qk_ref[...] = lax.dot_general(
         query_ref[...], key_ref[...], (((1,), (1,)), ((), ())), preferred_element_type=F32
@@ -85,18 +87,25 @@
     vo_ref[...] = jnp.dot(value_ref[...], mix_ref[...], preferred_element_type=F32).astype(BF16)
     for i, ref in enumerate(vector_refs):
         vectors_ref[i : i + 1, :] = ref[...].reshape(1, width)
-    groups = [
-        jnp.floor((lax.broadcasted_iota(jnp.int32, (width, width), d).astype(F32) + 0.5) * (GROUPS / width))
-        for d in range(2)
-    ]
-    same_ref[...] = jnp.where(groups[0] == groups[1], 1.0, 0.0).astype(BF16)
+    group = lambda dim: jnp.floor(
+        (lax.broadcasted_iota(jnp.int32, (width, width), dim).astype(F32) + 0.5) * (GROUPS / width)
+    )
+    same_ref[...] = jnp.where(group(0) == group(1), 1.0, 0.0).astype(BF16)
+    lane = lax.broadcasted_iota(jnp.int32, member_ref.shape, 1).astype(F32)
+    member_ref[...] = jnp.where(group(0)[:, :LANES] == lane, 1.0, 0.0).astype(BF16)
 
 
 def prepare(query, key, value, mix, *vectors):
     square = jax.ShapeDtypeStruct(query.shape, BF16)
     return pl.pallas_call(
         prepare_kernel,
-        out_shape=(square, square, jax.ShapeDtypeStruct((len(vectors), query.shape[0]), F32), square),
+        out_shape=(
+            square,
+            square,
+            jax.ShapeDtypeStruct((len(vectors), query.shape[0]), F32),
+            square,
+            jax.ShapeDtypeStruct((query.shape[0], LANES), BF16),
+        ),
         cost_estimate=pl.CostEstimate(flops=4 * query.shape[0] ** 3, bytes_accessed=0, transcendentals=0),
         name="prepare",
     )(query, key, value, mix, *vectors)
@@ -108,13 +117,14 @@
     return mean, jnp.sum(stats[:, 1] + gap * gap * count, axis=0, keepdims=True)
 
 
-def attention_kernel(count, distance_ref, stats_ref, qk_ref, vo_ref, vectors_ref, same_ref, *refs):
+def attention_kernel(count, distance_ref, stats_ref, qk_ref, vo_ref, vectors_ref, same_ref, member_ref, *refs):
     *blocks, mixed_ref, out_stats_ref = refs
     positions, width = blocks[0].shape
     cols = positions // 2
-    mean, variance = group_mean_and_variance(
+    mean, spread = group_mean_and_spread(
         stats_ref[0:1, :], stats_ref[1:2, :], count, same_ref[...]
     )
+    variance = exact_product([spread], same_ref[...])[0] * (GROUPS / (width * count))
     gain, shift, bias = (vectors_ref[i : i + 1, :] for i in range(3))
     factor = gain * lax.rsqrt(variance + EPS)
     offset = shift - mean * factor
@@ -139,8 +149,9 @@
         if highest is not None:
             newest = jnp.maximum(highest, newest)
         probs = jnp.exp2(scores + (constant - newest)).astype(BF16)
-        part = jnp.sum(probs.astype(F32), axis=1, keepdims=True)
-        product = jnp.dot(probs, keys, preferred_element_type=F32)
+        wide_keys = jnp.concatenate([keys, jnp.ones((keys.shape[0], 128), BF16)], axis=1)
+        product = jnp.dot(probs, wide_keys, preferred_element_type=F32)
+        product, part = product[:, :width], product[:, width : width + 1]
         if highest is None:
             total, summed = part, product
         else:
@@ -152,25 +163,27 @@
     mixed = (own + branch).astype(BF16)
     mixed_ref[...] = mixed
     mean, spread = mean_and_spread([mixed[:positions].astype(F32)])
+    _, group_spread = group_mean_and_spread(mean, spread, positions, same_ref[...])
+    mean, spread = exact_product([mean * (GROUPS / width), group_spread], member_ref[...])
     for i in range(out_stats_ref.shape[0]):
         out_stats_ref[i, 0:1, :] = mean
         out_stats_ref[i, 1:2, :] = spread
 
 
-def attention(blocks, distance, stats, count, qk, vo, vectors, same_group, stat_copies):
+def attention(blocks, distance, stats, count, qk, vo, vectors, same_group, member, stat_copies):
     positions, width = blocks[0].shape
     vmem = pl.BlockSpec(memory_space=pltpu.VMEM)
     return pl.pallas_call(
         functools.partial(attention_kernel, count),
         out_shape=(
             jax.ShapeDtypeStruct((positions // 2 * 3, width), BF16),
-            jax.ShapeDtypeStruct((stat_copies, 2, width), F32),
+            jax.ShapeDtypeStruct((stat_copies, 2, LANES), F32),
         ),
-        in_specs=[pl.BlockSpec(memory_space=pltpu.SMEM)] + [vmem] * (5 + len(blocks)),
+        in_specs=[pl.BlockSpec(memory_space=pltpu.SMEM)] + [vmem] * (6 + len(blocks)),
         out_specs=(vmem, vmem),
         compiler_params=pltpu.CompilerParams(vmem_limit_bytes=VMEM_LIMIT * (2 if len(blocks) > AT_ONCE else 1)),
         name="attention",
-    )(distance, stats, qk, vo, vectors, same_group, *blocks)
+    )(distance, stats, qk, vo, vectors, same_group, member, *blocks)
 
 
 def fetch_kernel(after, weight_hbm, middle_ref, sem):
@@ -194,7 +207,7 @@
     )(after, pltpu.with_memory_space_constraint(weight, pltpu.HBM))
 
 
-def upsample_kernel(count, valid_ref, current_ref, earlier_ref, stats_ref, vectors_ref, same_ref, middle_ref, weight_hbm, out_hbm, now, before, wide, out, weight, weight_sems, out_sems):
+def upsample_kernel(count, valid_ref, current_ref, earlier_ref, stats_ref, vectors_ref, member_ref, middle_ref, weight_hbm, out_hbm, now, before, wide, out, weight, weight_sems, out_sems):
     positions, width = current_ref.shape
     cols = positions // 3
     copies = {
@@ -202,9 +215,9 @@
     }
     for copy in copies.values():
         copy.start()
-    mean, variance = group_mean_and_variance(
-        *merged(stats_ref[...], count // stats_ref.shape[0]), count, same_ref[...]
-    )
+    entries = count * width // GROUPS
+    mean, spread = merged(stats_ref[...], entries // stats_ref.shape[0])
+    mean, variance = exact_product([mean, spread * (1.0 / entries)], member_ref[...], 1)
     gain, shift, bias = (vectors_ref[i : i + 1, :] for i in range(3, 6))
     factor = gain * lax.rsqrt(variance + EPS)
     col = lax.broadcasted_iota(jnp.int32, (cols, width), 0)
@@ -262,16 +275,16 @@
 
     first = [(phase, multiplied(*phase)) for phase in ((0, 0), (0, 1))]
     stored(*first[0][0], first[0][1])
+    stored(*first[1][0], first[1][1])
     for copy in copies.values():
         copy.wait()
-    stored(*first[1][0], first[1][1])
     for phase in ((1, 0), (1, 1)):
         stored(*phase, multiplied(*phase))
     for copy in out_copies:
         copy.wait()
 
 
-def upsample(valid, current, earlier, stats, count, vectors, same_group, middle, weight):
+def upsample(valid, current, earlier, stats, count, vectors, member, middle, weight):
     positions, width = current.shape
     cols = positions // 3
     vmem = pl.BlockSpec(memory_space=pltpu.VMEM)
@@ -294,7 +307,7 @@
         compiler_params=pltpu.CompilerParams(vmem_limit_bytes=VMEM_LIMIT),
         name="upsample",
     )(
-        valid, current, earlier, stats, vectors, same_group, middle, pltpu.with_memory_space_constraint(weight, pltpu.HBM)
+        valid, current, earlier, stats, vectors, member, middle, pltpu.with_memory_space_constraint(weight, pltpu.HBM)
     )
     return result.reshape(2, 4, 2 * cols, width)
 
@@ -321,7 +334,7 @@
     block = latent.reshape(positions, width)
 
     slots = {0: block, 1: swapped(block, "height", 1)}
-    direct = [1 << i for i in range(1, (height - 1).bit_length())][::-1]
+    direct = [1 << i for i in range(1, (height - 1).bit_length())]
     forwarded = sorted((m for m in range(2, height, 2) if m not in direct), key=lambda m: (bin(m).count("1"), -m))
     for mask in direct:
         slots[mask] = swapped(block, "height", mask)
@@ -334,7 +347,7 @@
 
     parameters = (query_weight, key_weight, value_weight, out_weight)
     parameters += (first_gain, first_shift, out_bias, second_gain, second_shift, up_bias)
-    first, slots[0], qk, vo, vectors, same_group = lax.cond(
+    first, slots[0], qk, vo, vectors, same_group, member = lax.cond(
         group < groups,
         early_work,
         lambda *arguments: jax.tree.map(
@@ -345,7 +358,7 @@
         *parameters,
     )
     held = held * groups
-    ready = lax.optimization_barrier([slots[m] for m in direct])
+    _, *ready = lax.optimization_barrier([first] + [slots[m] for m in direct])
     slots.update(zip(direct, ready))
     for mask in forwarded:
         lowest = mask & -mask
@@ -359,14 +372,14 @@
 
     blocks = [slots[m] for m in range(height)]
     mixed, second = attention(
-        blocks, distance, first, count, qk, vo, vectors, same_group, groups * height
+        blocks, distance, first, count, qk, vo, vectors, same_group, member, groups * height
     )
     middle = fetch(mixed, up_weight)
     earlier = lax.ppermute(mixed, "frames", [(i, i + 1) for i in range(groups - 1)])
     second = lax.all_to_all(second, ("frames", "height"), split_axis=0, concat_axis=0, tiled=True)
     valid = jnp.stack([slab + 1 < height, group > 0]).astype(jnp.int32)
     return upsample(
-        valid, mixed, earlier, second, count, vectors, same_group, middle, up_weight
+        valid, mixed, earlier, second, count, vectors, member, middle, up_weight
     )
 
 

time: 54 us -> 52.7 us (0.976)
  waiting for transfers between devices: 16.7 us -> 14.6 us
  starting transfers between devices: 18.9 us -> 20.6 us
  Pallas kernels: 17.6 us -> 16.7 us
    ppermute x9, waiting for transfers between devices: 7.94 us -> 6.36 us  [swapped(): return lax.ppermute(value, axis, [(i, i ^ mask) for i in range(count)])]
    ppermute x9, starting transfers between devices: 7.47 us -> 8.97 us  [swapped(): return lax.ppermute(value, axis, [(i, i ^ mask) for i in range(count)])]
    pallas_call x1, Pallas kernels: 7.12 us -> 6.42 us  [upsample(): pl.pallas_call(functools.partial(upsample_kernel, count), out_shape=jax.S...]
  transfers between devices with their start and end apart: 12 -> 12, of which waited for: 6 -> 5; matrix products, arithmetic and copies ran while one was open for 1% -> 1% of each run, Pallas kernels for 10% -> 10%
where the time goes in v4:
time: 52.7 us; the launch traced here: 52.4 us
  starting transfers between devices  20.6 us (39%)
  Pallas kernels  16.7 us (32%)
  waiting for transfers between devices  14.6 us (28%)
    ppermute x9, starting transfers between devices, swapped(): return lax.ppermute(value, axis, [(i, i ^ mask) for i in range(count)])  8.97 us
    pallas_call x1, Pallas kernels, upsample(): pl.pallas_call(functools.partial(upsample_kernel, count), out_shape=jax.S...  6.42 us
    ppermute x9, waiting for transfers between devices, swapped(): return lax.ppermute(value, axis, [(i, i ^ mask) for i in range(count)])  6.36 us
    all_to_all x1, waiting for transfers between devices, local(): lax.all_to_all(second, ('frames', 'height'), split_axis=0, concat_axis=0,...  5.4 us
    all_to_all x1, starting transfers between devices, local(): lax.all_to_all(second, ('frames', 'height'), split_axis=0, concat_axis=0,...  5.06 us
    pallas_call x1, Pallas kernels, attention(): pl.pallas_call(functools.partial(attention_kernel, count), out_shape=(jax...  4.83 us
    all_to_all x1, starting transfers between devices, early_work(): lax.all_to_all(stats, 'frames', split_axis=0, concat_axis=0, tiled=True)  3.73 us
    ppermute x1, starting transfers between devices, local(): lax.ppermute(mixed, 'frames', [(i, i + 1) for i in range(groups - 1)])  2.89 us
  transfers between devices with their start and end apart: 12, of which 5 were waited for; matrix products, arithmetic and copies ran while one was open for 1% of the time, Pallas kernels for 10%

profile of v4, /device:TPU:0, one launch (start us, length us, event | category | flops | bytes accessed | tf_op | source)
XLA Modules:
  0.0 52.4 jit_solution(13516896881012937190)
XLA Ops:
  0.0 0.5 collective-permute-start
  0.5 3.6 %collective-permute-start.4 = (bf16[320,384]{1,0:T(8,128)(2,1)}, bf16[320,384]{1,0:T(8,128)(2,1)S(1)}, u32[]{:S(2)}, u32[]{:S(2)}) collective-permute-start(bf16[320,384]{1,0:T(8,128)(2,1)} %bitcast.55), channel_id=1, source_target_pairs={{0,4},{1,5},{2,6},{3,7},{4,0},{5,1},{6,2},{7,3},{8,12},{9,13},{10,... | collective-permute-start | bytes 737288 | tf_op jit(solution)/shard_map/ppermute | solution.py:23
  4.0 1.6 %collective-permute-start.3 = (bf16[320,384]{1,0:T(8,128)(2,1)}, bf16[320,384]{1,0:T(8,128)(2,1)S(1)}, u32[]{:S(2)}, u32[]{:S(2)}) collective-permute-start(bf16[320,384]{1,0:T(8,128)(2,1)} %bitcast.56), channel_id=1, source_target_pairs={{0,2},{1,3},{2,0},{3,1},{4,6},{5,7},{6,4},{7,5},{8,10},{9,11},{10,... | collective-permute-start | bytes 737288 | tf_op jit(solution)/shard_map/ppermute | solution.py:23
  5.6 0.0 collective-permute-done.refs_1_
  5.6 10.4 %conditional.1 = (f32[2,384]{1,0:T(2,128)S(1)}, bf16[320,384]{1,0:T(8,128)(2,1)S(1)}, bf16[384,384]{1,0:T(8,128)(2,1)S(1)}, bf16[384,384]{1,0:T(8,128)(2,1)S(1)}...) conditional(s32[]{:T(128)} %convert_element_type.7, () %tuple.14, ...), branch_computations={%region_0.0_spmd, %region_1.0_spmd} | conditional | flops 227551360 | bytes 1244246 | solution.py:350
  5.6 1.8 %local_stats.1 = (f32[4,2,384]{2,1,0:T(2,128)}, bf16[320,384]{1,0:T(8,128)(2,1)S(1)}) custom-call(bf16[320,384]{1,0:T(8,128)(2,1)} %get-tuple-element.29.own_hbm, bf16[320,384]{1,0:T(8,128)(2,1)S(1)} %get-tuple-element.30.other_ref), custom_call_target="tpu_custom_call" | custom-call | flops 1048576 | tf_op jit(solution)/shard_map/cond/branch_1_fun/local_stats/pallas_call | solution.py:64
  7.5 3.7 %all-to-all-start = ((f32[4,2,384]{2,1,0:T(2,128)}), f32[4,2,384]{2,1,0:T(2,128)S(1)}, u32[]{:S(2)}, u32[]{:S(2)}) async-start(f32[4,2,384]{2,1,0:T(2,128)} %get-tuple-element.31), calls=%async_computation | async-start | bytes 24576 | tf_op jit(solution)/shard_map/cond/branch_1_fun/all_to_all | solution.py:345
  11.2 1.8 %prepare.1 = (bf16[384,384]{1,0:T(8,128)(2,1)S(1)}, bf16[384,384]{1,0:T(8,128)(2,1)S(1)}, f32[6,384]{1,0:T(8,128)S(1)}, bf16[384,384]{1,0:T(8,128)(2,1)S(1)}, bf16[384,128]{1,0:T(8,128)(2,1)S(1)}) custom-call(bf16[384,384]{1,0:T(8,128)(2,1)} %get-tuple-element.81.query_ref, bf16[384,384]{1,0:T(8,128)(2,1)} %get-tuple-element.82.key_ref, ...), custom_call_target="tpu_custom_call" | custom-call | flops 226492416 | tf_op jit(solution)/shard_map/cond/branch_1_fun/prepare/pallas_call | solution.py:100
  13.0 2.9 %all-to-all-done = f32[4,2,384]{2,1,0:T(2,128)S(1)} async-done(((f32[4,2,384]{2,1,0:T(2,128)}), f32[4,2,384]{2,1,0:T(2,128)S(1)}, u32[]{:S(2)}, u32[]{:S(2)}) %all-to-all-start) | async-done | bytes 12320 | tf_op jit(solution)/shard_map/cond/branch_1_fun/all_to_all | solution.py:345
  16.0 0.5 collective-permute-start.1
  16.5 0.0 collective-permute-done.4.refs_4_
  16.5 0.0 collective-permute-done.3.refs_2_
  16.5 1.6 %collective-permute-start.7 = (bf16[320,384]{1,0:T(8,128)(2,1)S(1)}, bf16[320,384]{1,0:T(8,128)(2,1)S(1)}, u32[]{:S(2)}, u32[]{:S(2)}) collective-permute-start(bf16[320,384]{1,0:T(8,128)(2,1)S(1)} %collective-permute-done.4.refs_4_), channel_id=1, source_target_pairs={{0,2},{1,3},{2,0},{3,1},{4,6},{5,7},{6,4},{7,5},{8,10},{9,11},{10,... | collective-permute-start | bytes 737288 | tf_op jit(solution)/shard_map/ppermute | solution.py:23
  18.1 1.6 %collective-permute-done.1 = f32[2,384]{1,0:T(2,128)S(1)} collective-permute-done((f32[2,384]{1,0:T(2,128)S(1)}, f32[2,384]{1,0:T(2,128)S(1)}, u32[]{:S(2)}, u32[]{:S(2)}) %collective-permute-start.1) | collective-permute-done | bytes 3104 | tf_op jit(solution)/shard_map/ppermute | solution.py:23
  19.8 0.7 %collective-permute-start.2 = (f32[2,384]{1,0:T(2,128)S(1)}, f32[2,384]{1,0:T(2,128)S(1)}, u32[]{:S(2)}, u32[]{:S(2)}) collective-permute-start(f32[2,384]{1,0:T(2,128)S(1)} %get-tuple-element.100), channel_id=1, source_target_pairs={{0,4},{1,5},{2,6},{3,7},{4,0},{5,1},{6,2},{7,3},{8,12},{9,13},{10,... | collective-permute-start | bytes 9224 | tf_op jit(solution)/shard_map/ppermute | solution.py:23
  20.4 0.0 collective-permute-start.6
  20.4 0.5 collective-permute-start.5
  21.0 3.4 %collective-permute-done.2 = f32[2,384]{1,0:T(2,128)S(1)} collective-permute-done((f32[2,384]{1,0:T(2,128)S(1)}, f32[2,384]{1,0:T(2,128)S(1)}, u32[]{:S(2)}, u32[]{:S(2)}) %collective-permute-start.2) | collective-permute-done | bytes 3104 | tf_op jit(solution)/shard_map/ppermute | solution.py:23
  24.4 0.0 collective-permute-done.7.refs_6_
  24.4 0.1 collective-permute-start.8
  24.5 0.0 collective-permute-done.5.refs_3_
  24.5 0.0 collective-permute-done.6.refs_5_
  24.5 1.4 %collective-permute-done.8.refs_7_ = bf16[320,384]{1,0:T(8,128)(2,1)S(1)} collective-permute-done((bf16[320,384]{1,0:T(8,128)(2,1)S(1)}, bf16[320,384]{1,0:T(8,128)(2,1)S(1)}, u32[]{:S(2)}, u32[]{:S(2)}) %collective-permute-start.8) | collective-permute-done | bytes 245792 | tf_op jit(solution)/shard_map/ppermute | solution.py:23
  25.9 4.8 %attention.1 = (bf16[480,384]{1,0:T(8,128)(2,1)S(1)}, f32[32,2,128]{2,1,0:T(2,128)}) custom-call(s32[1]{0:T(128)} %bitcast.4.distance_ref, f32[2,384]{1,0:T(2,128)S(1)} %pad_maximum_fusion.4.stats_ref, bf16[384,384]{1,0:T(8,128)(2,1)S(1)} %get-tuple-element.60.qk_ref, bf16[384,384]{1,0:T(8,128)(2,1)S(1)} %get-tuple-element.61.vo_ref, ...), custom_call_target="tpu_custom_call" | custom-call | tf_op jit(solution)/shard_map/attention/pallas_call | solution.py:176
  30.8 2.9 %collective-permute-start.9 = (bf16[480,384]{1,0:T(8,128)(2,1)S(1)}, bf16[480,384]{1,0:T(8,128)(2,1)S(1)}, u32[]{:S(2)}, u32[]{:S(2)}) collective-permute-start(bf16[480,384]{1,0:T(8,128)(2,1)S(1)} %get-tuple-element.68.after.current_ref), channel_id=1, source_target_pairs={{0,8},{8,16},{16,24},{1,9},{9,17},{17,25},{2,10},{10,18},{18,26},{... | collective-permute-start | bytes 1105928 | tf_op jit(solution)/shard_map/ppermute | solution.py:378
  33.7 5.1 %all-to-all-start.1 = ((f32[32,2,128]{2,1,0:T(2,128)}), f32[32,2,128]{2,1,0:T(2,128)S(1)}, u32[]{:S(2)}, u32[]{:S(2)}) async-start(f32[32,2,128]{2,1,0:T(2,128)} %get-tuple-element.69), calls=%async_computation.1 | async-start | bytes 65536 | tf_op jit(solution)/shard_map/all_to_all | solution.py:379
  38.7 0.1 add_convert_fusion.valid_ref
  38.8 1.8 %fetch.1.middle_ref = bf16[3,3,384,384]{3,2,1,0:T(8,128)(2,1)S(1)} custom-call(bf16[480,384]{1,0:T(8,128)(2,1)S(1)} %get-tuple-element.68.after.current_ref, bf16[3,3,3,384,384]{4,3,2,1,0:T(8,128)(2,1)} %weight_hbm.3), custom_call_target="tpu_custom_call" | custom-call | bytes 5308416 | tf_op jit(solution)/shard_map/fetch/pallas_call | solution.py:198
  40.6 5.4 %all-to-all-done.1.stats_ref = f32[32,2,128]{2,1,0:T(2,128)S(1)} async-done(((f32[32,2,128]{2,1,0:T(2,128)}), f32[32,2,128]{2,1,0:T(2,128)S(1)}, u32[]{:S(2)}, u32[]{:S(2)}) %all-to-all-start.1) | async-done | bytes 32800 | tf_op jit(solution)/shard_map/all_to_all | solution.py:379
  46.0 0.0 collective-permute-done.9.earlier_ref
  46.0 6.4 %upsample.1 = bf16[2,2,2,320,384]{4,3,2,1,0:T(8,128)(2,1)} custom-call(s32[2]{0:T(128)S(1)} %add_convert_fusion.valid_ref, bf16[480,384]{1,0:T(8,128)(2,1)S(1)} %get-tuple-element.68.after.current_ref, bf16[480,384]{1,0:T(8,128)(2,1)S(1)} %collective-permute-done.9.earlier_ref, f32[32,2,128]{2,1,0:T(2,128)S(1)} %all-to-all-done.1.stats_ref, ...), custom_call_target="tpu_custom_call" | custom-call | tf_op jit(solution)/shard_map/upsample/pallas_call | solution.py:291
  (21 shorter events, 0.2 us)
Async XLA Ops:
  0.0 5.6 %collective-permute-start = (bf16[320,384]{1,0:T(8,128)(2,1)}, bf16[320,384]{1,0:T(8,128)(2,1)S(1)}, u32[]{:S(2)}, u32[]{:S(2)}) collective-permute-start(bf16[320,384]{1,0:T(8,128)(2,1)} %bitcast.54), channel_id=1, source_target_pairs={{0,1},{1,0},{2,3},{3,2},{4,5},{5,4},{6,7},{7,6},{8,9},{9,8},{10,11... | collective-permute-start | bytes 737288 | tf_op jit(solution)/shard_map/ppermute | solution.py:23
  0.5 16.1 %collective-permute-start.4 = (bf16[320,384]{1,0:T(8,128)(2,1)}, bf16[320,384]{1,0:T(8,128)(2,1)S(1)}, u32[]{:S(2)}, u32[]{:S(2)}) collective-permute-start(bf16[320,384]{1,0:T(8,128)(2,1)} %bitcast.55), channel_id=1, source_target_pairs={{0,4},{1,5},{2,6},{3,7},{4,0},{5,1},{6,2},{7,3},{8,12},{9,13},{10,... | collective-permute-start | bytes 737288 | tf_op jit(solution)/shard_map/ppermute | solution.py:23
  4.0 12.5 %collective-permute-start.3 = (bf16[320,384]{1,0:T(8,128)(2,1)}, bf16[320,384]{1,0:T(8,128)(2,1)S(1)}, u32[]{:S(2)}, u32[]{:S(2)}) collective-permute-start(bf16[320,384]{1,0:T(8,128)(2,1)} %bitcast.56), channel_id=1, source_target_pairs={{0,2},{1,3},{2,0},{3,1},{4,6},{5,7},{6,4},{7,5},{8,10},{9,11},{10,... | collective-permute-start | bytes 737288 | tf_op jit(solution)/shard_map/ppermute | solution.py:23
  7.5 8.4 %all-to-all-start = ((f32[4,2,384]{2,1,0:T(2,128)}), f32[4,2,384]{2,1,0:T(2,128)S(1)}, u32[]{:S(2)}, u32[]{:S(2)}) async-start(f32[4,2,384]{2,1,0:T(2,128)} %get-tuple-element.31), calls=%async_computation | async-start | bytes 24576 | tf_op jit(solution)/shard_map/cond/branch_1_fun/all_to_all | solution.py:345
  16.0 3.7 %collective-permute-start.1 = (f32[2,384]{1,0:T(2,128)S(1)}, f32[2,384]{1,0:T(2,128)S(1)}, u32[]{:S(2)}, u32[]{:S(2)}) collective-permute-start(f32[2,384]{1,0:T(2,128)S(1)} %get-tuple-element.59), channel_id=1, source_target_pairs={{0,2},{1,3},{2,0},{3,1},{4,6},{5,7},{6,4},{7,5},{8,10},{9,11},{10,... | collective-permute-start | bytes 9224 | tf_op jit(solution)/shard_map/ppermute | solution.py:23
  16.5 7.8 %collective-permute-start.7 = (bf16[320,384]{1,0:T(8,128)(2,1)S(1)}, bf16[320,384]{1,0:T(8,128)(2,1)S(1)}, u32[]{:S(2)}, u32[]{:S(2)}) collective-permute-start(bf16[320,384]{1,0:T(8,128)(2,1)S(1)} %collective-permute-done.4.refs_4_), channel_id=1, source_target_pairs={{0,2},{1,3},{2,0},{3,1},{4,6},{5,7},{6,4},{7,5},{8,10},{9,11},{10,... | collective-permute-start | bytes 737288 | tf_op jit(solution)/shard_map/ppermute | solution.py:23
  19.8 4.6 %collective-permute-start.2 = (f32[2,384]{1,0:T(2,128)S(1)}, f32[2,384]{1,0:T(2,128)S(1)}, u32[]{:S(2)}, u32[]{:S(2)}) collective-permute-start(f32[2,384]{1,0:T(2,128)S(1)} %get-tuple-element.100), channel_id=1, source_target_pairs={{0,4},{1,5},{2,6},{3,7},{4,0},{5,1},{6,2},{7,3},{8,12},{9,13},{10,... | collective-permute-start | bytes 9224 | tf_op jit(solution)/shard_map/ppermute | solution.py:23
  20.4 4.1 %collective-permute-start.6 = (bf16[320,384]{1,0:T(8,128)(2,1)S(1)}, bf16[320,384]{1,0:T(8,128)(2,1)S(1)}, u32[]{:S(2)}, u32[]{:S(2)}) collective-permute-start(bf16[320,384]{1,0:T(8,128)(2,1)S(1)} %collective-permute-done.4.refs_4_), channel_id=1, source_target_pairs={{0,1},{1,0},{2,3},{3,2},{4,5},{5,4},{6,7},{7,6},{8,9},{9,8},{10,11... | collective-permute-start | bytes 737288 | tf_op jit(solution)/shard_map/ppermute | solution.py:23
  20.4 4.1 %collective-permute-start.5 = (bf16[320,384]{1,0:T(8,128)(2,1)S(1)}, bf16[320,384]{1,0:T(8,128)(2,1)S(1)}, u32[]{:S(2)}, u32[]{:S(2)}) collective-permute-start(bf16[320,384]{1,0:T(8,128)(2,1)S(1)} %collective-permute-done.3.refs_2_), channel_id=1, source_target_pairs={{0,1},{1,0},{2,3},{3,2},{4,5},{5,4},{6,7},{7,6},{8,9},{9,8},{10,11... | collective-permute-start | bytes 737288 | tf_op jit(solution)/shard_map/ppermute | solution.py:23
  24.4 1.6 %collective-permute-start.8 = (bf16[320,384]{1,0:T(8,128)(2,1)S(1)}, bf16[320,384]{1,0:T(8,128)(2,1)S(1)}, u32[]{:S(2)}, u32[]{:S(2)}) collective-permute-start(bf16[320,384]{1,0:T(8,128)(2,1)S(1)} %collective-permute-done.7.refs_6_), channel_id=1, source_target_pairs={{0,1},{1,0},{2,3},{3,2},{4,5},{5,4},{6,7},{7,6},{8,9},{9,8},{10,11... | collective-permute-start | bytes 737288 | tf_op jit(solution)/shard_map/ppermute | solution.py:23
  30.8 15.2 %collective-permute-start.9 = (bf16[480,384]{1,0:T(8,128)(2,1)S(1)}, bf16[480,384]{1,0:T(8,128)(2,1)S(1)}, u32[]{:S(2)}, u32[]{:S(2)}) collective-permute-start(bf16[480,384]{1,0:T(8,128)(2,1)S(1)} %get-tuple-element.68.after.current_ref), channel_id=1, source_target_pairs={{0,8},{8,16},{16,24},{1,9},{9,17},{17,25},{2,10},{10,18},{18,26},{... | collective-permute-start | bytes 1105928 | tf_op jit(solution)/shard_map/ppermute | solution.py:378
  33.7 12.3 %all-to-all-start.1 = ((f32[32,2,128]{2,1,0:T(2,128)}), f32[32,2,128]{2,1,0:T(2,128)S(1)}, u32[]{:S(2)}, u32[]{:S(2)}) async-start(f32[32,2,128]{2,1,0:T(2,128)} %get-tuple-element.69), calls=%async_computation.1 | async-start | bytes 65536 | tf_op jit(solution)/shard_map/all_to_all | solution.py:379

commit v5 on v4

--- a/solution.py
+++ b/solution.py
@@ -375,7 +375,7 @@
         blocks, distance, first, count, qk, vo, vectors, same_group, member, groups * height
     )
     middle = fetch(mixed, up_weight)
-    earlier = lax.ppermute(mixed, "frames", [(i, i + 1) for i in range(groups - 1)])
+    earlier = lax.ppermute(mixed, "frames", [(i, (i + 1) % groups) for i in range(groups)])
     second = lax.all_to_all(second, ("frames", "height"), split_axis=0, concat_axis=0, tiled=True)
     valid = jnp.stack([slab + 1 < height, group > 0]).astype(jnp.int32)
     return upsample(

time: 52.7 us -> 50.8 us (0.964)
  starting transfers between devices: 20.6 us -> 18.7 us
    ppermute x1, starting transfers between devices: 2.89 us -> 0.98 us  [local(): lax.ppermute(mixed, 'frames', [(i, (i + 1) % groups) for i in range(group...]
  transfers between devices with their start and end apart: 12 -> 12, of which waited for: 5 -> 5; matrix products, arithmetic and copies ran while one was open for 1% -> 1% of each run, Pallas kernels for 10% -> 11%
where the time goes in v5:
time: 50.8 us; the launch traced here: 50.5 us
  starting transfers between devices  18.7 us (37%)
  Pallas kernels  16.7 us (33%)
  waiting for transfers between devices  14.6 us (29%)
    ppermute x9, starting transfers between devices, swapped(): return lax.ppermute(value, axis, [(i, i ^ mask) for i in range(count)])  8.97 us
    pallas_call x1, Pallas kernels, upsample(): pl.pallas_call(functools.partial(upsample_kernel, count), out_shape=jax.S...  6.42 us
    ppermute x9, waiting for transfers between devices, swapped(): return lax.ppermute(value, axis, [(i, i ^ mask) for i in range(count)])  6.36 us
    all_to_all x1, waiting for transfers between devices, local(): lax.all_to_all(second, ('frames', 'height'), split_axis=0, concat_axis=0,...  5.4 us
    all_to_all x1, starting transfers between devices, local(): lax.all_to_all(second, ('frames', 'height'), split_axis=0, concat_axis=0,...  5.08 us
    pallas_call x1, Pallas kernels, attention(): pl.pallas_call(functools.partial(attention_kernel, count), out_shape=(jax...  4.83 us
    all_to_all x1, starting transfers between devices, early_work(): lax.all_to_all(stats, 'frames', split_axis=0, concat_axis=0, tiled=True)  3.73 us
    all_to_all x1, waiting for transfers between devices, early_work(): lax.all_to_all(stats, 'frames', split_axis=0, concat_axis=0, tiled=True)  2.86 us
  transfers between devices with their start and end apart: 12, of which 5 were waited for; matrix products, arithmetic and copies ran while one was open for 1% of the time, Pallas kernels for 11%

profile of v5, /device:TPU:0, one launch (start us, length us, event | category | flops | bytes accessed | tf_op | source)
XLA Modules:
  0.0 50.5 jit_solution(14272970302907615808)
XLA Ops:
  0.0 0.5 collective-permute-start
  0.5 3.6 %collective-permute-start.4 = (bf16[320,384]{1,0:T(8,128)(2,1)}, bf16[320,384]{1,0:T(8,128)(2,1)S(1)}, u32[]{:S(2)}, u32[]{:S(2)}) collective-permute-start(bf16[320,384]{1,0:T(8,128)(2,1)} %bitcast.55), channel_id=1, source_target_pairs={{0,4},{1,5},{2,6},{3,7},{4,0},{5,1},{6,2},{7,3},{8,12},{9,13},{10,... | collective-permute-start | bytes 737288 | tf_op jit(solution)/shard_map/ppermute | solution.py:23
  4.0 1.6 %collective-permute-start.3 = (bf16[320,384]{1,0:T(8,128)(2,1)}, bf16[320,384]{1,0:T(8,128)(2,1)S(1)}, u32[]{:S(2)}, u32[]{:S(2)}) collective-permute-start(bf16[320,384]{1,0:T(8,128)(2,1)} %bitcast.56), channel_id=1, source_target_pairs={{0,2},{1,3},{2,0},{3,1},{4,6},{5,7},{6,4},{7,5},{8,10},{9,11},{10,... | collective-permute-start | bytes 737288 | tf_op jit(solution)/shard_map/ppermute | solution.py:23
  5.6 0.0 collective-permute-done.refs_1_
  5.6 10.4 %conditional.1 = (f32[2,384]{1,0:T(2,128)S(1)}, bf16[320,384]{1,0:T(8,128)(2,1)S(1)}, bf16[384,384]{1,0:T(8,128)(2,1)S(1)}, bf16[384,384]{1,0:T(8,128)(2,1)S(1)}...) conditional(s32[]{:T(128)} %convert_element_type.7, () %tuple.14, ...), branch_computations={%region_0.0_spmd, %region_1.0_spmd} | conditional | flops 227551360 | bytes 1244246 | solution.py:350
  5.6 1.8 %local_stats.1 = (f32[4,2,384]{2,1,0:T(2,128)}, bf16[320,384]{1,0:T(8,128)(2,1)S(1)}) custom-call(bf16[320,384]{1,0:T(8,128)(2,1)} %get-tuple-element.29.own_hbm, bf16[320,384]{1,0:T(8,128)(2,1)S(1)} %get-tuple-element.30.other_ref), custom_call_target="tpu_custom_call" | custom-call | flops 1048576 | tf_op jit(solution)/shard_map/cond/branch_1_fun/local_stats/pallas_call | solution.py:64
  7.5 3.7 %all-to-all-start = ((f32[4,2,384]{2,1,0:T(2,128)}), f32[4,2,384]{2,1,0:T(2,128)S(1)}, u32[]{:S(2)}, u32[]{:S(2)}) async-start(f32[4,2,384]{2,1,0:T(2,128)} %get-tuple-element.31), calls=%async_computation | async-start | bytes 24576 | tf_op jit(solution)/shard_map/cond/branch_1_fun/all_to_all | solution.py:345
  11.2 1.8 %prepare.1 = (bf16[384,384]{1,0:T(8,128)(2,1)S(1)}, bf16[384,384]{1,0:T(8,128)(2,1)S(1)}, f32[6,384]{1,0:T(8,128)S(1)}, bf16[384,384]{1,0:T(8,128)(2,1)S(1)}, bf16[384,128]{1,0:T(8,128)(2,1)S(1)}) custom-call(bf16[384,384]{1,0:T(8,128)(2,1)} %get-tuple-element.81.query_ref, bf16[384,384]{1,0:T(8,128)(2,1)} %get-tuple-element.82.key_ref, ...), custom_call_target="tpu_custom_call" | custom-call | flops 226492416 | tf_op jit(solution)/shard_map/cond/branch_1_fun/prepare/pallas_call | solution.py:100
  13.0 2.9 %all-to-all-done = f32[4,2,384]{2,1,0:T(2,128)S(1)} async-done(((f32[4,2,384]{2,1,0:T(2,128)}), f32[4,2,384]{2,1,0:T(2,128)S(1)}, u32[]{:S(2)}, u32[]{:S(2)}) %all-to-all-start) | async-done | bytes 12320 | tf_op jit(solution)/shard_map/cond/branch_1_fun/all_to_all | solution.py:345
  16.0 0.5 %collective-permute-start.1 = (f32[2,384]{1,0:T(2,128)S(1)}, f32[2,384]{1,0:T(2,128)S(1)}, u32[]{:S(2)}, u32[]{:S(2)}) collective-permute-start(f32[2,384]{1,0:T(2,128)S(1)} %get-tuple-element.59), channel_id=1, source_target_pairs={{0,2},{1,3},{2,0},{3,1},{4,6},{5,7},{6,4},{7,5},{8,10},{9,11},{10,... | collective-permute-start | bytes 9224 | tf_op jit(solution)/shard_map/ppermute | solution.py:23
  16.5 0.0 collective-permute-done.4.refs_4_
  16.5 0.0 collective-permute-done.3.refs_2_
  16.5 1.6 %collective-permute-start.7 = (bf16[320,384]{1,0:T(8,128)(2,1)S(1)}, bf16[320,384]{1,0:T(8,128)(2,1)S(1)}, u32[]{:S(2)}, u32[]{:S(2)}) collective-permute-start(bf16[320,384]{1,0:T(8,128)(2,1)S(1)} %collective-permute-done.4.refs_4_), channel_id=1, source_target_pairs={{0,2},{1,3},{2,0},{3,1},{4,6},{5,7},{6,4},{7,5},{8,10},{9,11},{10,... | collective-permute-start | bytes 737288 | tf_op jit(solution)/shard_map/ppermute | solution.py:23
  18.1 1.6 %collective-permute-done.1 = f32[2,384]{1,0:T(2,128)S(1)} collective-permute-done((f32[2,384]{1,0:T(2,128)S(1)}, f32[2,384]{1,0:T(2,128)S(1)}, u32[]{:S(2)}, u32[]{:S(2)}) %collective-permute-start.1) | collective-permute-done | bytes 3104 | tf_op jit(solution)/shard_map/ppermute | solution.py:23
  19.8 0.7 %collective-permute-start.2 = (f32[2,384]{1,0:T(2,128)S(1)}, f32[2,384]{1,0:T(2,128)S(1)}, u32[]{:S(2)}, u32[]{:S(2)}) collective-permute-start(f32[2,384]{1,0:T(2,128)S(1)} %get-tuple-element.100), channel_id=1, source_target_pairs={{0,4},{1,5},{2,6},{3,7},{4,0},{5,1},{6,2},{7,3},{8,12},{9,13},{10,... | collective-permute-start | bytes 9224 | tf_op jit(solution)/shard_map/ppermute | solution.py:23
  20.4 0.0 collective-permute-start.6
  20.4 0.5 %collective-permute-start.5 = (bf16[320,384]{1,0:T(8,128)(2,1)S(1)}, bf16[320,384]{1,0:T(8,128)(2,1)S(1)}, u32[]{:S(2)}, u32[]{:S(2)}) collective-permute-start(bf16[320,384]{1,0:T(8,128)(2,1)S(1)} %collective-permute-done.3.refs_2_), channel_id=1, source_target_pairs={{0,1},{1,0},{2,3},{3,2},{4,5},{5,4},{6,7},{7,6},{8,9},{9,8},{10,11... | collective-permute-start | bytes 737288 | tf_op jit(solution)/shard_map/ppermute | solution.py:23
  21.0 3.4 %collective-permute-done.2 = f32[2,384]{1,0:T(2,128)S(1)} collective-permute-done((f32[2,384]{1,0:T(2,128)S(1)}, f32[2,384]{1,0:T(2,128)S(1)}, u32[]{:S(2)}, u32[]{:S(2)}) %collective-permute-start.2) | collective-permute-done | bytes 3104 | tf_op jit(solution)/shard_map/ppermute | solution.py:23
  24.4 0.0 collective-permute-done.7.refs_6_
  24.4 0.1 collective-permute-start.8
  24.5 0.0 collective-permute-done.5.refs_3_
  24.5 0.0 collective-permute-done.6.refs_5_
  24.5 1.4 %collective-permute-done.8.refs_7_ = bf16[320,384]{1,0:T(8,128)(2,1)S(1)} collective-permute-done((bf16[320,384]{1,0:T(8,128)(2,1)S(1)}, bf16[320,384]{1,0:T(8,128)(2,1)S(1)}, u32[]{:S(2)}, u32[]{:S(2)}) %collective-permute-start.8) | collective-permute-done | bytes 245792 | tf_op jit(solution)/shard_map/ppermute | solution.py:23
  25.9 4.8 %attention.1 = (bf16[480,384]{1,0:T(8,128)(2,1)S(1)}, f32[32,2,128]{2,1,0:T(2,128)}) custom-call(s32[1]{0:T(128)} %bitcast.4.distance_ref, f32[2,384]{1,0:T(2,128)S(1)} %pad_maximum_fusion.4.stats_ref, bf16[384,384]{1,0:T(8,128)(2,1)S(1)} %get-tuple-element.60.qk_ref, bf16[384,384]{1,0:T(8,128)(2,1)S(1)} %get-tuple-element.61.vo_ref, ...), custom_call_target="tpu_custom_call" | custom-call | tf_op jit(solution)/shard_map/attention/pallas_call | solution.py:176
  30.8 1.0 %collective-permute-start.9 = (bf16[480,384]{1,0:T(8,128)(2,1)S(1)}, bf16[480,384]{1,0:T(8,128)(2,1)S(1)}, u32[]{:S(2)}, u32[]{:S(2)}) collective-permute-start(bf16[480,384]{1,0:T(8,128)(2,1)S(1)} %get-tuple-element.68.after.current_ref), channel_id=1, source_target_pairs={{0,8},{8,16},{16,24},{24,0},{1,9},{9,17},{17,25},{25,1},{2,10},{10... | collective-permute-start | bytes 1105928 | tf_op jit(solution)/shard_map/ppermute | solution.py:378
  31.7 5.1 %all-to-all-start.1 = ((f32[32,2,128]{2,1,0:T(2,128)}), f32[32,2,128]{2,1,0:T(2,128)S(1)}, u32[]{:S(2)}, u32[]{:S(2)}) async-start(f32[32,2,128]{2,1,0:T(2,128)} %get-tuple-element.69), calls=%async_computation.1 | async-start | bytes 65536 | tf_op jit(solution)/shard_map/all_to_all | solution.py:379
  36.8 0.1 add_convert_fusion.valid_ref
  36.9 1.8 %fetch.1.middle_ref = bf16[3,3,384,384]{3,2,1,0:T(8,128)(2,1)S(1)} custom-call(bf16[480,384]{1,0:T(8,128)(2,1)S(1)} %get-tuple-element.68.after.current_ref, bf16[3,3,3,384,384]{4,3,2,1,0:T(8,128)(2,1)} %weight_hbm.3), custom_call_target="tpu_custom_call" | custom-call | bytes 5308416 | tf_op jit(solution)/shard_map/fetch/pallas_call | solution.py:198
  38.7 5.4 %all-to-all-done.1.stats_ref = f32[32,2,128]{2,1,0:T(2,128)S(1)} async-done(((f32[32,2,128]{2,1,0:T(2,128)}), f32[32,2,128]{2,1,0:T(2,128)S(1)}, u32[]{:S(2)}, u32[]{:S(2)}) %all-to-all-start.1) | async-done | bytes 32800 | tf_op jit(solution)/shard_map/all_to_all | solution.py:379
  44.1 0.0 collective-permute-done.9.earlier_ref
  44.1 6.4 %upsample.1 = bf16[2,2,2,320,384]{4,3,2,1,0:T(8,128)(2,1)} custom-call(s32[2]{0:T(128)S(1)} %add_convert_fusion.valid_ref, bf16[480,384]{1,0:T(8,128)(2,1)S(1)} %get-tuple-element.68.after.current_ref, bf16[480,384]{1,0:T(8,128)(2,1)S(1)} %collective-permute-done.9.earlier_ref, f32[32,2,128]{2,1,0:T(2,128)S(1)} %all-to-all-done.1.stats_ref, ...), custom_call_target="tpu_custom_call" | custom-call | tf_op jit(solution)/shard_map/upsample/pallas_call | solution.py:291
  (21 shorter events, 0.2 us)
Async XLA Ops:
  0.0 5.6 %collective-permute-start = (bf16[320,384]{1,0:T(8,128)(2,1)}, bf16[320,384]{1,0:T(8,128)(2,1)S(1)}, u32[]{:S(2)}, u32[]{:S(2)}) collective-permute-start(bf16[320,384]{1,0:T(8,128)(2,1)} %bitcast.54), channel_id=1, source_target_pairs={{0,1},{1,0},{2,3},{3,2},{4,5},{5,4},{6,7},{7,6},{8,9},{9,8},{10,11... | collective-permute-start | bytes 737288 | tf_op jit(solution)/shard_map/ppermute | solution.py:23
  0.5 16.1 %collective-permute-start.4 = (bf16[320,384]{1,0:T(8,128)(2,1)}, bf16[320,384]{1,0:T(8,128)(2,1)S(1)}, u32[]{:S(2)}, u32[]{:S(2)}) collective-permute-start(bf16[320,384]{1,0:T(8,128)(2,1)} %bitcast.55), channel_id=1, source_target_pairs={{0,4},{1,5},{2,6},{3,7},{4,0},{5,1},{6,2},{7,3},{8,12},{9,13},{10,... | collective-permute-start | bytes 737288 | tf_op jit(solution)/shard_map/ppermute | solution.py:23
  4.0 12.5 %collective-permute-start.3 = (bf16[320,384]{1,0:T(8,128)(2,1)}, bf16[320,384]{1,0:T(8,128)(2,1)S(1)}, u32[]{:S(2)}, u32[]{:S(2)}) collective-permute-start(bf16[320,384]{1,0:T(8,128)(2,1)} %bitcast.56), channel_id=1, source_target_pairs={{0,2},{1,3},{2,0},{3,1},{4,6},{5,7},{6,4},{7,5},{8,10},{9,11},{10,... | collective-permute-start | bytes 737288 | tf_op jit(solution)/shard_map/ppermute | solution.py:23
  7.5 8.4 %all-to-all-start = ((f32[4,2,384]{2,1,0:T(2,128)}), f32[4,2,384]{2,1,0:T(2,128)S(1)}, u32[]{:S(2)}, u32[]{:S(2)}) async-start(f32[4,2,384]{2,1,0:T(2,128)} %get-tuple-element.31), calls=%async_computation | async-start | bytes 24576 | tf_op jit(solution)/shard_map/cond/branch_1_fun/all_to_all | solution.py:345
  16.0 3.7 %collective-permute-start.1 = (f32[2,384]{1,0:T(2,128)S(1)}, f32[2,384]{1,0:T(2,128)S(1)}, u32[]{:S(2)}, u32[]{:S(2)}) collective-permute-start(f32[2,384]{1,0:T(2,128)S(1)} %get-tuple-element.59), channel_id=1, source_target_pairs={{0,2},{1,3},{2,0},{3,1},{4,6},{5,7},{6,4},{7,5},{8,10},{9,11},{10,... | collective-permute-start | bytes 9224 | tf_op jit(solution)/shard_map/ppermute | solution.py:23
  16.5 7.8 %collective-permute-start.7 = (bf16[320,384]{1,0:T(8,128)(2,1)S(1)}, bf16[320,384]{1,0:T(8,128)(2,1)S(1)}, u32[]{:S(2)}, u32[]{:S(2)}) collective-permute-start(bf16[320,384]{1,0:T(8,128)(2,1)S(1)} %collective-permute-done.4.refs_4_), channel_id=1, source_target_pairs={{0,2},{1,3},{2,0},{3,1},{4,6},{5,7},{6,4},{7,5},{8,10},{9,11},{10,... | collective-permute-start | bytes 737288 | tf_op jit(solution)/shard_map/ppermute | solution.py:23
  19.8 4.6 %collective-permute-start.2 = (f32[2,384]{1,0:T(2,128)S(1)}, f32[2,384]{1,0:T(2,128)S(1)}, u32[]{:S(2)}, u32[]{:S(2)}) collective-permute-start(f32[2,384]{1,0:T(2,128)S(1)} %get-tuple-element.100), channel_id=1, source_target_pairs={{0,4},{1,5},{2,6},{3,7},{4,0},{5,1},{6,2},{7,3},{8,12},{9,13},{10,... | collective-permute-start | bytes 9224 | tf_op jit(solution)/shard_map/ppermute | solution.py:23
  20.4 4.1 %collective-permute-start.6 = (bf16[320,384]{1,0:T(8,128)(2,1)S(1)}, bf16[320,384]{1,0:T(8,128)(2,1)S(1)}, u32[]{:S(2)}, u32[]{:S(2)}) collective-permute-start(bf16[320,384]{1,0:T(8,128)(2,1)S(1)} %collective-permute-done.4.refs_4_), channel_id=1, source_target_pairs={{0,1},{1,0},{2,3},{3,2},{4,5},{5,4},{6,7},{7,6},{8,9},{9,8},{10,11... | collective-permute-start | bytes 737288 | tf_op jit(solution)/shard_map/ppermute | solution.py:23
  20.4 4.1 %collective-permute-start.5 = (bf16[320,384]{1,0:T(8,128)(2,1)S(1)}, bf16[320,384]{1,0:T(8,128)(2,1)S(1)}, u32[]{:S(2)}, u32[]{:S(2)}) collective-permute-start(bf16[320,384]{1,0:T(8,128)(2,1)S(1)} %collective-permute-done.3.refs_2_), channel_id=1, source_target_pairs={{0,1},{1,0},{2,3},{3,2},{4,5},{5,4},{6,7},{7,6},{8,9},{9,8},{10,11... | collective-permute-start | bytes 737288 | tf_op jit(solution)/shard_map/ppermute | solution.py:23
  24.4 1.6 %collective-permute-start.8 = (bf16[320,384]{1,0:T(8,128)(2,1)S(1)}, bf16[320,384]{1,0:T(8,128)(2,1)S(1)}, u32[]{:S(2)}, u32[]{:S(2)}) collective-permute-start(bf16[320,384]{1,0:T(8,128)(2,1)S(1)} %collective-permute-done.7.refs_6_), channel_id=1, source_target_pairs={{0,1},{1,0},{2,3},{3,2},{4,5},{5,4},{6,7},{7,6},{8,9},{9,8},{10,11... | collective-permute-start | bytes 737288 | tf_op jit(solution)/shard_map/ppermute | solution.py:23
  30.8 13.3 %collective-permute-start.9 = (bf16[480,384]{1,0:T(8,128)(2,1)S(1)}, bf16[480,384]{1,0:T(8,128)(2,1)S(1)}, u32[]{:S(2)}, u32[]{:S(2)}) collective-permute-start(bf16[480,384]{1,0:T(8,128)(2,1)S(1)} %get-tuple-element.68.after.current_ref), channel_id=1, source_target_pairs={{0,8},{8,16},{16,24},{24,0},{1,9},{9,17},{17,25},{25,1},{2,10},{10... | collective-permute-start | bytes 1105928 | tf_op jit(solution)/shard_map/ppermute | solution.py:378
  31.7 12.3 %all-to-all-start.1 = ((f32[32,2,128]{2,1,0:T(2,128)}), f32[32,2,128]{2,1,0:T(2,128)S(1)}, u32[]{:S(2)}, u32[]{:S(2)}) async-start(f32[32,2,128]{2,1,0:T(2,128)} %get-tuple-element.69), calls=%async_computation.1 | async-start | bytes 65536 | tf_op jit(solution)/shard_map/all_to_all | solution.py:379

commit v6 on v5

--- a/solution.py
+++ b/solution.py
@@ -334,15 +334,16 @@
     block = latent.reshape(positions, width)
 
     slots = {0: block, 1: swapped(block, "height", 1)}
-    direct = [1 << i for i in range(1, (height - 1).bit_length())]
+    direct = [1 << i for i in range(1, (height - 1).bit_length())][::-1]
     forwarded = sorted((m for m in range(2, height, 2) if m not in direct), key=lambda m: (bin(m).count("1"), -m))
     for mask in direct:
         slots[mask] = swapped(block, "height", mask)
     held = 2 * positions
 
     def early_work(own, other, *parameters):
-        stats, own = local_stats(own, other, groups)
-        stats = lax.all_to_all(stats, "frames", split_axis=0, concat_axis=0, tiled=True)
+        stats, own = local_stats(own, other, 1)
+        masks = range(1, groups)
+        stats = jnp.stack([stats[0]] + [swapped(stats[0], "frames", mask) for mask in masks])
         return jnp.concatenate(merged(stats, held), axis=0), own, *prepare(*parameters)
 
     parameters = (query_weight, key_weight, value_weight, out_weight)

time: 50.8 us -> 50.5 us (level)
  starting transfers between devices: 18.7 us -> 17.3 us
  other arithmetic: 0.28 us -> 0.97 us
  waiting for transfers between devices: 14.6 us -> 15.2 us
    all_to_all x1 -> x0, starting transfers between devices: 3.73 us -> none  [early_work(): lax.all_to_all(stats, 'frames', split_axis=0, concat_axis=0, tiled=True)]
    ppermute x9 -> x12, waiting for transfers between devices: 6.36 us -> 9.82 us  [swapped(): return lax.ppermute(value, axis, [(i, i ^ mask) for i in range(count)])]
    all_to_all x1 -> x0, waiting for transfers between devices: 2.86 us -> none  [early_work(): lax.all_to_all(stats, 'frames', split_axis=0, concat_axis=0, tiled=True)]
    ppermute x9 -> x12, starting transfers between devices: 8.97 us -> 11 us  [swapped(): return lax.ppermute(value, axis, [(i, i ^ mask) for i in range(count)])]
    another operation x0 -> x1, other arithmetic: none -> 0.69 us  [early_work(): jnp.stack([stats[0]] + [swapped(stats[0], 'frames', mask) for mask in mas...]
    ppermute x1, starting transfers between devices: 0.98 us -> 1.5 us  [local(): lax.ppermute(mixed, 'frames', [(i, (i + 1) % groups) for i in range(group...]
  transfers between devices with their start and end apart: 12 -> 14, of which waited for: 5 -> 7; matrix products, arithmetic and copies ran while one was open for 1% -> 2% of each run, Pallas kernels for 11% -> 11%
where the time goes in v6:
time: 50.5 us; the launch traced here: 50.3 us
  starting transfers between devices  17.3 us (34%)
  Pallas kernels  16.6 us (33%)
  waiting for transfers between devices  15.2 us (30%)
  other arithmetic  0.97 us (2%)
    ppermute x12, starting transfers between devices, swapped(): return lax.ppermute(value, axis, [(i, i ^ mask) for i in range(count)])  11 us
    ppermute x12, waiting for transfers between devices, swapped(): return lax.ppermute(value, axis, [(i, i ^ mask) for i in range(count)])  9.82 us
    pallas_call x1, Pallas kernels, upsample(): pl.pallas_call(functools.partial(upsample_kernel, count), out_shape=jax.S...  6.42 us
    all_to_all x1, waiting for transfers between devices, local(): lax.all_to_all(second, ('frames', 'height'), split_axis=0, concat_axis=0,...  5.4 us
    all_to_all x1, starting transfers between devices, local(): lax.all_to_all(second, ('frames', 'height'), split_axis=0, concat_axis=0,...  4.82 us
    pallas_call x1, Pallas kernels, attention(): pl.pallas_call(functools.partial(attention_kernel, count), out_shape=(jax...  4.81 us
    pallas_call x1, Pallas kernels, prepare(): pl.pallas_call(prepare_kernel, out_shape=(square, square, jax.ShapeDtypeS...  1.83 us
    pallas_call x1, Pallas kernels, local_stats(): pl.pallas_call(stats_kernel, out_shape=(jax.ShapeDtypeStruct((copies, 2,...  1.8 us
  transfers between devices with their start and end apart: 14, of which 7 were waited for; matrix products, arithmetic and copies ran while one was open for 2% of the time, Pallas kernels for 11%

profile of v6, /device:TPU:0, one launch (start us, length us, event | category | flops | bytes accessed | tf_op | source)
XLA Modules:
  0.0 50.3 jit_solution(2749923546416910475)
XLA Ops:
  0.0 0.5 collective-permute-start.3
  0.5 2.6 %collective-permute-start.7 = (bf16[320,384]{1,0:T(8,128)(2,1)}, bf16[320,384]{1,0:T(8,128)(2,1)S(1)}, u32[]{:S(2)}, u32[]{:S(2)}) collective-permute-start(bf16[320,384]{1,0:T(8,128)(2,1)} %bitcast.59), channel_id=1, source_target_pairs={{0,2},{1,3},{2,0},{3,1},{4,6},{5,7},{6,4},{7,5},{8,10},{9,11},{10,... | collective-permute-start | bytes 737288 | tf_op jit(solution)/shard_map/ppermute | solution.py:23
  3.0 2.6 %collective-permute-start.6 = (bf16[320,384]{1,0:T(8,128)(2,1)}, bf16[320,384]{1,0:T(8,128)(2,1)S(1)}, u32[]{:S(2)}, u32[]{:S(2)}) collective-permute-start(bf16[320,384]{1,0:T(8,128)(2,1)} %bitcast.60), channel_id=1, source_target_pairs={{0,4},{1,5},{2,6},{3,7},{4,0},{5,1},{6,2},{7,3},{8,12},{9,13},{10,... | collective-permute-start | bytes 737288 | tf_op jit(solution)/shard_map/ppermute | solution.py:23
  5.6 9.4 %conditional.1 = (f32[2,384]{1,0:T(2,128)S(1)}, bf16[320,384]{1,0:T(8,128)(2,1)S(1)}, bf16[384,384]{1,0:T(8,128)(2,1)S(1)}, bf16[384,384]{1,0:T(8,128)(2,1)S(1)}...) conditional(s32[]{:T(128)} %convert_element_type.7, () %tuple.14, ...), branch_computations={%region_0.0_spmd, %region_1.0_spmd} | conditional | flops 227560576 | bytes 1244246 | solution.py:351
  5.6 1.8 %local_stats.1 = (f32[1,2,384]{2,1,0:T(2,128)}, bf16[320,384]{1,0:T(8,128)(2,1)S(1)}) custom-call(bf16[320,384]{1,0:T(8,128)(2,1)} %get-tuple-element.29.own_hbm, bf16[320,384]{1,0:T(8,128)(2,1)S(1)} %get-tuple-element.30.other_ref), custom_call_target="tpu_custom_call" | custom-call | flops 1048576 | tf_op jit(solution)/shard_map/cond/branch_1_fun/local_stats/pallas_call | solution.py:64
  7.4 2.5 %collective-permute-start.2 = (f32[2,384]{1,0:T(2,128)}, f32[2,384]{1,0:T(2,128)S(1)}, u32[]{:S(2)}, u32[]{:S(2)}) collective-permute-start(f32[2,384]{1,0:T(2,128)} %bitcast.62), channel_id=1, source_target_pairs={{0,24},{8,16},{16,8},{24,0},{1,25},{9,17},{17,9},{25,1},{2,26},{10... | collective-permute-start | bytes 9224 | tf_op jit(solution)/shard_map/cond/branch_1_fun/ppermute | solution.py:23
  9.9 0.5 %collective-permute-start.1 = (f32[2,384]{1,0:T(2,128)}, f32[2,384]{1,0:T(2,128)S(1)}, u32[]{:S(2)}, u32[]{:S(2)}) collective-permute-start(f32[2,384]{1,0:T(2,128)} %bitcast.63), channel_id=1, source_target_pairs={{0,16},{8,24},{16,0},{24,8},{1,17},{9,25},{17,1},{25,9},{2,18},{10... | collective-permute-start | bytes 9224 | tf_op jit(solution)/shard_map/cond/branch_1_fun/ppermute | solution.py:23
  10.5 0.5 %collective-permute-start = (f32[2,384]{1,0:T(2,128)}, f32[2,384]{1,0:T(2,128)S(1)}, u32[]{:S(2)}, u32[]{:S(2)}) collective-permute-start(f32[2,384]{1,0:T(2,128)} %bitcast.64), channel_id=1, source_target_pairs={{0,8},{8,0},{16,24},{24,16},{1,9},{9,1},{17,25},{25,17},{2,10},{10... | collective-permute-start | bytes 9224 | tf_op jit(solution)/shard_map/cond/branch_1_fun/ppermute | solution.py:23
  11.0 1.8 %prepare.1 = (bf16[384,384]{1,0:T(8,128)(2,1)S(1)}, bf16[384,384]{1,0:T(8,128)(2,1)S(1)}, f32[6,384]{1,0:T(8,128)S(1)}, bf16[384,384]{1,0:T(8,128)(2,1)S(1)}, bf16[384,128]{1,0:T(8,128)(2,1)S(1)}) custom-call(bf16[384,384]{1,0:T(8,128)(2,1)} %get-tuple-element.81.query_ref, bf16[384,384]{1,0:T(8,128)(2,1)} %get-tuple-element.82.key_ref, ...), custom_call_target="tpu_custom_call" | custom-call | flops 226492416 | tf_op jit(solution)/shard_map/cond/branch_1_fun/prepare/pallas_call | solution.py:100
  12.8 0.0 collective-permute-done.2
  12.8 0.9 %collective-permute-done.1 = f32[2,384]{1,0:T(2,128)S(1)} collective-permute-done((f32[2,384]{1,0:T(2,128)}, f32[2,384]{1,0:T(2,128)S(1)}, u32[]{:S(2)}, u32[]{:S(2)}) %collective-permute-start.1) | collective-permute-done | bytes 3104 | tf_op jit(solution)/shard_map/cond/branch_1_fun/ppermute | solution.py:23
  13.8 0.5 %collective-permute-done = f32[2,384]{1,0:T(2,128)S(1)} collective-permute-done((f32[2,384]{1,0:T(2,128)}, f32[2,384]{1,0:T(2,128)S(1)}, u32[]{:S(2)}, u32[]{:S(2)}) %collective-permute-start) | collective-permute-done | bytes 3104 | tf_op jit(solution)/shard_map/cond/branch_1_fun/ppermute | solution.py:23
  14.3 0.7 %pad_maximum_fusion = f32[4,2,384]{2,1,0:T(2,128)S(1)} fusion(f32[1,2,384]{2,1,0:T(2,128)S(1)} %bitcast.65, f32[1,2,384]{2,1,0:T(2,128)S(1)} %bitcast.66, f32[1,2,384]{2,1,0:T(2,128)S(1)} %bitcast.67, f32[1,2,384]{2,1,0:T(2,128)} %get-tuple-element.31), kind=kLoop, calls=%fused_computation | loop fusion | flops 9216 | bytes 24576 | tf_op jit(solution)/shard_map/cond/branch_1_fun/stack | solution.py:346
  15.1 0.4 collective-permute-start.4
  15.5 2.2 %collective-permute-done.6.refs_4_ = bf16[320,384]{1,0:T(8,128)(2,1)S(1)} collective-permute-done((bf16[320,384]{1,0:T(8,128)(2,1)}, bf16[320,384]{1,0:T(8,128)(2,1)S(1)}, u32[]{:S(2)}, u32[]{:S(2)}) %collective-permute-start.6) | collective-permute-done | bytes 245792 | tf_op jit(solution)/shard_map/ppermute | solution.py:23
  17.6 0.4 collective-permute-start.10
  18.0 1.7 %collective-permute-done.4 = f32[2,384]{1,0:T(2,128)S(1)} collective-permute-done((f32[2,384]{1,0:T(2,128)S(1)}, f32[2,384]{1,0:T(2,128)S(1)}, u32[]{:S(2)}, u32[]{:S(2)}) %collective-permute-start.4) | collective-permute-done | bytes 3104 | tf_op jit(solution)/shard_map/ppermute | solution.py:23
  19.8 0.4 collective-permute-start.5
  20.2 0.0 collective-permute-start.9
  20.2 0.5 %collective-permute-start.8 = (bf16[320,384]{1,0:T(8,128)(2,1)S(1)}, bf16[320,384]{1,0:T(8,128)(2,1)S(1)}, u32[]{:S(2)}, u32[]{:S(2)}) collective-permute-start(bf16[320,384]{1,0:T(8,128)(2,1)S(1)} %collective-permute-done.7.refs_2_), channel_id=1, source_target_pairs={{0,1},{1,0},{2,3},{3,2},{4,5},{5,4},{6,7},{7,6},{8,9},{9,8},{10,11... | collective-permute-start | bytes 737288 | tf_op jit(solution)/shard_map/ppermute | solution.py:23
  20.7 3.1 %collective-permute-done.5 = f32[2,384]{1,0:T(2,128)S(1)} collective-permute-done((f32[2,384]{1,0:T(2,128)S(1)}, f32[2,384]{1,0:T(2,128)S(1)}, u32[]{:S(2)}, u32[]{:S(2)}) %collective-permute-start.5) | collective-permute-done | bytes 3104 | tf_op jit(solution)/shard_map/ppermute | solution.py:23
  23.9 0.0 collective-permute-done.10.refs_6_
  23.9 0.1 collective-permute-start.11
  24.1 0.0 collective-permute-done.8.refs_3_
  24.1 1.4 %collective-permute-done.11.refs_7_ = bf16[320,384]{1,0:T(8,128)(2,1)S(1)} collective-permute-done((bf16[320,384]{1,0:T(8,128)(2,1)S(1)}, bf16[320,384]{1,0:T(8,128)(2,1)S(1)}, u32[]{:S(2)}, u32[]{:S(2)}) %collective-permute-start.11) | collective-permute-done | bytes 245792 | tf_op jit(solution)/shard_map/ppermute | solution.py:23
  25.5 4.8 %attention.1 = (bf16[480,384]{1,0:T(8,128)(2,1)S(1)}, f32[32,2,128]{2,1,0:T(2,128)}) custom-call(s32[1]{0:T(128)} %bitcast.8.distance_ref, f32[2,384]{1,0:T(2,128)S(1)} %pad_maximum_fusion.5.stats_ref, bf16[384,384]{1,0:T(8,128)(2,1)S(1)} %get-tuple-element.60.qk_ref, bf16[384,384]{1,0:T(8,128)(2,1)S(1)} %get-tuple-element.61.vo_ref, ...), custom_call_target="tpu_custom_call" | custom-call | tf_op jit(solution)/shard_map/attention/pallas_call | solution.py:176
  30.3 1.5 %collective-permute-start.12 = (bf16[480,384]{1,0:T(8,128)(2,1)S(1)}, bf16[480,384]{1,0:T(8,128)(2,1)S(1)}, u32[]{:S(2)}, u32[]{:S(2)}) collective-permute-start(bf16[480,384]{1,0:T(8,128)(2,1)S(1)} %get-tuple-element.68.after.current_ref), channel_id=1, source_target_pairs={{0,8},{8,16},{16,24},{24,0},{1,9},{9,17},{17,25},{25,1},{2,10},{10... | collective-permute-start | bytes 1105928 | tf_op jit(solution)/shard_map/ppermute | solution.py:379
  31.8 4.8 %all-to-all-start = ((f32[32,2,128]{2,1,0:T(2,128)}), f32[32,2,128]{2,1,0:T(2,128)S(1)}, u32[]{:S(2)}, u32[]{:S(2)}) async-start(f32[32,2,128]{2,1,0:T(2,128)} %get-tuple-element.69), calls=%async_computation | async-start | bytes 65536 | tf_op jit(solution)/shard_map/all_to_all | solution.py:380
  36.6 0.1 add_convert_fusion.valid_ref
  36.7 1.8 %fetch.1.middle_ref = bf16[3,3,384,384]{3,2,1,0:T(8,128)(2,1)S(1)} custom-call(bf16[480,384]{1,0:T(8,128)(2,1)S(1)} %get-tuple-element.68.after.current_ref, bf16[3,3,3,384,384]{4,3,2,1,0:T(8,128)(2,1)} %weight_hbm.3), custom_call_target="tpu_custom_call" | custom-call | bytes 5308416 | tf_op jit(solution)/shard_map/fetch/pallas_call | solution.py:198
  38.5 5.4 %all-to-all-done.stats_ref = f32[32,2,128]{2,1,0:T(2,128)S(1)} async-done(((f32[32,2,128]{2,1,0:T(2,128)}), f32[32,2,128]{2,1,0:T(2,128)S(1)}, u32[]{:S(2)}, u32[]{:S(2)}) %all-to-all-start) | async-done | bytes 32800 | tf_op jit(solution)/shard_map/all_to_all | solution.py:380
  43.9 6.4 %upsample.1 = bf16[2,2,2,320,384]{4,3,2,1,0:T(8,128)(2,1)} custom-call(s32[2]{0:T(128)S(1)} %add_convert_fusion.valid_ref, bf16[480,384]{1,0:T(8,128)(2,1)S(1)} %get-tuple-element.68.after.current_ref, bf16[480,384]{1,0:T(8,128)(2,1)S(1)} %collective-permute-done.12.earlier_ref, f32[32,2,128]{2,1,0:T(2,128)S(1)} %all-to-all-done.stats_ref, ...), custom_call_target="tpu_custom_call" | custom-call | tf_op jit(solution)/shard_map/upsample/pallas_call | solution.py:291
  (25 shorter events, 0.2 us)
Async XLA Ops:
  0.0 5.6 %collective-permute-start.3 = (bf16[320,384]{1,0:T(8,128)(2,1)}, bf16[320,384]{1,0:T(8,128)(2,1)S(1)}, u32[]{:S(2)}, u32[]{:S(2)}) collective-permute-start(bf16[320,384]{1,0:T(8,128)(2,1)} %bitcast.58), channel_id=1, source_target_pairs={{0,1},{1,0},{2,3},{3,2},{4,5},{5,4},{6,7},{7,6},{8,9},{9,8},{10,11... | collective-permute-start | bytes 737288 | tf_op jit(solution)/shard_map/ppermute | solution.py:23
  0.5 15.0 %collective-permute-start.7 = (bf16[320,384]{1,0:T(8,128)(2,1)}, bf16[320,384]{1,0:T(8,128)(2,1)S(1)}, u32[]{:S(2)}, u32[]{:S(2)}) collective-permute-start(bf16[320,384]{1,0:T(8,128)(2,1)} %bitcast.59), channel_id=1, source_target_pairs={{0,2},{1,3},{2,0},{3,1},{4,6},{5,7},{6,4},{7,5},{8,10},{9,11},{10,... | collective-permute-start | bytes 737288 | tf_op jit(solution)/shard_map/ppermute | solution.py:23
  3.0 14.6 %collective-permute-start.6 = (bf16[320,384]{1,0:T(8,128)(2,1)}, bf16[320,384]{1,0:T(8,128)(2,1)S(1)}, u32[]{:S(2)}, u32[]{:S(2)}) collective-permute-start(bf16[320,384]{1,0:T(8,128)(2,1)} %bitcast.60), channel_id=1, source_target_pairs={{0,4},{1,5},{2,6},{3,7},{4,0},{5,1},{6,2},{7,3},{8,12},{9,13},{10,... | collective-permute-start | bytes 737288 | tf_op jit(solution)/shard_map/ppermute | solution.py:23
  7.4 5.4 %collective-permute-start.2 = (f32[2,384]{1,0:T(2,128)}, f32[2,384]{1,0:T(2,128)S(1)}, u32[]{:S(2)}, u32[]{:S(2)}) collective-permute-start(f32[2,384]{1,0:T(2,128)} %bitcast.62), channel_id=1, source_target_pairs={{0,24},{8,16},{16,8},{24,0},{1,25},{9,17},{17,9},{25,1},{2,26},{10... | collective-permute-start | bytes 9224 | tf_op jit(solution)/shard_map/cond/branch_1_fun/ppermute | solution.py:23
  9.9 3.8 %collective-permute-start.1 = (f32[2,384]{1,0:T(2,128)}, f32[2,384]{1,0:T(2,128)S(1)}, u32[]{:S(2)}, u32[]{:S(2)}) collective-permute-start(f32[2,384]{1,0:T(2,128)} %bitcast.63), channel_id=1, source_target_pairs={{0,16},{8,24},{16,0},{24,8},{1,17},{9,25},{17,1},{25,9},{2,18},{10... | collective-permute-start | bytes 9224 | tf_op jit(solution)/shard_map/cond/branch_1_fun/ppermute | solution.py:23
  10.5 3.8 %collective-permute-start = (f32[2,384]{1,0:T(2,128)}, f32[2,384]{1,0:T(2,128)S(1)}, u32[]{:S(2)}, u32[]{:S(2)}) collective-permute-start(f32[2,384]{1,0:T(2,128)} %bitcast.64), channel_id=1, source_target_pairs={{0,8},{8,0},{16,24},{24,16},{1,9},{9,1},{17,25},{25,17},{2,10},{10... | collective-permute-start | bytes 9224 | tf_op jit(solution)/shard_map/cond/branch_1_fun/ppermute | solution.py:23
  15.1 4.7 %collective-permute-start.4 = (f32[2,384]{1,0:T(2,128)S(1)}, f32[2,384]{1,0:T(2,128)S(1)}, u32[]{:S(2)}, u32[]{:S(2)}) collective-permute-start(f32[2,384]{1,0:T(2,128)S(1)} %get-tuple-element.59), channel_id=1, source_target_pairs={{0,4},{1,5},{2,6},{3,7},{4,0},{5,1},{6,2},{7,3},{8,12},{9,13},{10,... | collective-permute-start | bytes 9224 | tf_op jit(solution)/shard_map/ppermute | solution.py:23
  17.6 6.3 %collective-permute-start.10 = (bf16[320,384]{1,0:T(8,128)(2,1)S(1)}, bf16[320,384]{1,0:T(8,128)(2,1)S(1)}, u32[]{:S(2)}, u32[]{:S(2)}) collective-permute-start(bf16[320,384]{1,0:T(8,128)(2,1)S(1)} %collective-permute-done.6.refs_4_), channel_id=1, source_target_pairs={{0,2},{1,3},{2,0},{3,1},{4,6},{5,7},{6,4},{7,5},{8,10},{9,11},{10,... | collective-permute-start | bytes 737288 | tf_op jit(solution)/shard_map/ppermute | solution.py:23
  19.8 4.1 %collective-permute-start.5 = (f32[2,384]{1,0:T(2,128)S(1)}, f32[2,384]{1,0:T(2,128)S(1)}, u32[]{:S(2)}, u32[]{:S(2)}) collective-permute-start(f32[2,384]{1,0:T(2,128)S(1)} %get-tuple-element.100), channel_id=1, source_target_pairs={{0,2},{1,3},{2,0},{3,1},{4,6},{5,7},{6,4},{7,5},{8,10},{9,11},{10,... | collective-permute-start | bytes 9224 | tf_op jit(solution)/shard_map/ppermute | solution.py:23
  20.2 3.8 %collective-permute-start.9 = (bf16[320,384]{1,0:T(8,128)(2,1)S(1)}, bf16[320,384]{1,0:T(8,128)(2,1)S(1)}, u32[]{:S(2)}, u32[]{:S(2)}) collective-permute-start(bf16[320,384]{1,0:T(8,128)(2,1)S(1)} %collective-permute-done.6.refs_4_), channel_id=1, source_target_pairs={{0,1},{1,0},{2,3},{3,2},{4,5},{5,4},{6,7},{7,6},{8,9},{9,8},{10,11... | collective-permute-start | bytes 737288 | tf_op jit(solution)/shard_map/ppermute | solution.py:23
  20.2 3.8 %collective-permute-start.8 = (bf16[320,384]{1,0:T(8,128)(2,1)S(1)}, bf16[320,384]{1,0:T(8,128)(2,1)S(1)}, u32[]{:S(2)}, u32[]{:S(2)}) collective-permute-start(bf16[320,384]{1,0:T(8,128)(2,1)S(1)} %collective-permute-done.7.refs_2_), channel_id=1, source_target_pairs={{0,1},{1,0},{2,3},{3,2},{4,5},{5,4},{6,7},{7,6},{8,9},{9,8},{10,11... | collective-permute-start | bytes 737288 | tf_op jit(solution)/shard_map/ppermute | solution.py:23
  23.9 1.6 %collective-permute-start.11 = (bf16[320,384]{1,0:T(8,128)(2,1)S(1)}, bf16[320,384]{1,0:T(8,128)(2,1)S(1)}, u32[]{:S(2)}, u32[]{:S(2)}) collective-permute-start(bf16[320,384]{1,0:T(8,128)(2,1)S(1)} %collective-permute-done.10.refs_6_), channel_id=1, source_target_pairs={{0,1},{1,0},{2,3},{3,2},{4,5},{5,4},{6,7},{7,6},{8,9},{9,8},{10,11... | collective-permute-start | bytes 737288 | tf_op jit(solution)/shard_map/ppermute | solution.py:23
  30.3 13.6 %collective-permute-start.12 = (bf16[480,384]{1,0:T(8,128)(2,1)S(1)}, bf16[480,384]{1,0:T(8,128)(2,1)S(1)}, u32[]{:S(2)}, u32[]{:S(2)}) collective-permute-start(bf16[480,384]{1,0:T(8,128)(2,1)S(1)} %get-tuple-element.68.after.current_ref), channel_id=1, source_target_pairs={{0,8},{8,16},{16,24},{24,0},{1,9},{9,17},{17,25},{25,1},{2,10},{10... | collective-permute-start | bytes 1105928 | tf_op jit(solution)/shard_map/ppermute | solution.py:379
  31.8 12.1 %all-to-all-start = ((f32[32,2,128]{2,1,0:T(2,128)}), f32[32,2,128]{2,1,0:T(2,128)S(1)}, u32[]{:S(2)}, u32[]{:S(2)}) async-start(f32[32,2,128]{2,1,0:T(2,128)} %get-tuple-element.69), calls=%async_computation | async-start | bytes 65536 | tf_op jit(solution)/shard_map/all_to_all | solution.py:380

commit v7 on v6

--- a/solution.py
+++ b/solution.py
@@ -265,13 +265,10 @@
                         out[odd_time, row, odd_row, :, lane * 128 : (lane + 1) * 128] = wide[
                             odd_time, row, lane
                         ].astype(BF16)
-            if odd_col == 1:
-                place = (odd_time, slice(None), odd_row)
-                copy = pltpu.make_async_copy(
-                    out.at[*place], out_hbm.at[*place], out_sems.at[odd_time, odd_row]
-                )
-                copy.start()
-                out_copies.append(copy)
+                    place = (odd_time, row, odd_row)
+                    copy = pltpu.make_async_copy(out.at[*place], out_hbm.at[*place], out_sems.at[*place])
+                    copy.start()
+                    out_copies.append(copy)
 
     first = [(phase, multiplied(*phase)) for phase in ((0, 0), (0, 1))]
     stored(*first[0][0], first[0][1])
@@ -302,7 +299,7 @@
             pltpu.VMEM((2, 2, 2, 2 * cols, width), BF16),
             pltpu.VMEM((3, 2, 3, width, width), BF16),
             pltpu.SemaphoreType.DMA((2,)),
-            pltpu.SemaphoreType.DMA((2, 2)),
+            pltpu.SemaphoreType.DMA((2, 2, 2)),
         ],
         compiler_params=pltpu.CompilerParams(vmem_limit_bytes=VMEM_LIMIT),
         name="upsample",

time: 50.5 us -> 50.5 us (level)
  no operation moved by 1% of the time
where the time goes in v7:
time: 50.5 us; the launch traced here: 50.2 us
  starting transfers between devices  17.3 us (34%)
  Pallas kernels  16.6 us (33%)
  waiting for transfers between devices  15.2 us (30%)
  other arithmetic  0.97 us (2%)
    ppermute x12, starting transfers between devices, swapped(): return lax.ppermute(value, axis, [(i, i ^ mask) for i in range(count)])  11 us
    ppermute x12, waiting for transfers between devices, swapped(): return lax.ppermute(value, axis, [(i, i ^ mask) for i in range(count)])  9.82 us
    pallas_call x1, Pallas kernels, upsample(): pl.pallas_call(functools.partial(upsample_kernel, count), out_shape=jax.S...  6.36 us
    all_to_all x1, waiting for transfers between devices, local(): lax.all_to_all(second, ('frames', 'height'), split_axis=0, concat_axis=0,...  5.4 us
    all_to_all x1, starting transfers between devices, local(): lax.all_to_all(second, ('frames', 'height'), split_axis=0, concat_axis=0,...  4.82 us
    pallas_call x1, Pallas kernels, attention(): pl.pallas_call(functools.partial(attention_kernel, count), out_shape=(jax...  4.81 us
    pallas_call x1, Pallas kernels, prepare(): pl.pallas_call(prepare_kernel, out_shape=(square, square, jax.ShapeDtypeS...  1.83 us
    pallas_call x1, Pallas kernels, local_stats(): pl.pallas_call(stats_kernel, out_shape=(jax.ShapeDtypeStruct((copies, 2,...  1.8 us
  transfers between devices with their start and end apart: 14, of which 7 were waited for; matrix products, arithmetic and copies ran while one was open for 2% of the time, Pallas kernels for 11%

profile of v7, /device:TPU:0, one launch (start us, length us, event | category | flops | bytes accessed | tf_op | source)
XLA Modules:
  0.0 50.2 jit_solution(7632075868982493984)
XLA Ops:
  0.0 0.5 collective-permute-start.3
  0.5 2.6 %collective-permute-start.7 = (bf16[320,384]{1,0:T(8,128)(2,1)}, bf16[320,384]{1,0:T(8,128)(2,1)S(1)}, u32[]{:S(2)}, u32[]{:S(2)}) collective-permute-start(bf16[320,384]{1,0:T(8,128)(2,1)} %bitcast.59), channel_id=1, source_target_pairs={{0,2},{1,3},{2,0},{3,1},{4,6},{5,7},{6,4},{7,5},{8,10},{9,11},{10,... | collective-permute-start | bytes 737288 | tf_op jit(solution)/shard_map/ppermute | solution.py:23
  3.0 2.6 %collective-permute-start.6 = (bf16[320,384]{1,0:T(8,128)(2,1)}, bf16[320,384]{1,0:T(8,128)(2,1)S(1)}, u32[]{:S(2)}, u32[]{:S(2)}) collective-permute-start(bf16[320,384]{1,0:T(8,128)(2,1)} %bitcast.60), channel_id=1, source_target_pairs={{0,4},{1,5},{2,6},{3,7},{4,0},{5,1},{6,2},{7,3},{8,12},{9,13},{10,... | collective-permute-start | bytes 737288 | tf_op jit(solution)/shard_map/ppermute | solution.py:23
  5.6 9.4 %conditional.1 = (f32[2,384]{1,0:T(2,128)S(1)}, bf16[320,384]{1,0:T(8,128)(2,1)S(1)}, bf16[384,384]{1,0:T(8,128)(2,1)S(1)}, bf16[384,384]{1,0:T(8,128)(2,1)S(1)}...) conditional(s32[]{:T(128)} %convert_element_type.7, () %tuple.14, ...), branch_computations={%region_0.0_spmd, %region_1.0_spmd} | conditional | flops 227560576 | bytes 1244246 | solution.py:348
  5.6 1.8 %local_stats.1 = (f32[1,2,384]{2,1,0:T(2,128)}, bf16[320,384]{1,0:T(8,128)(2,1)S(1)}) custom-call(bf16[320,384]{1,0:T(8,128)(2,1)} %get-tuple-element.29.own_hbm, bf16[320,384]{1,0:T(8,128)(2,1)S(1)} %get-tuple-element.30.other_ref), custom_call_target="tpu_custom_call" | custom-call | flops 1048576 | tf_op jit(solution)/shard_map/cond/branch_1_fun/local_stats/pallas_call | solution.py:64
  7.4 2.5 %collective-permute-start.2 = (f32[2,384]{1,0:T(2,128)}, f32[2,384]{1,0:T(2,128)S(1)}, u32[]{:S(2)}, u32[]{:S(2)}) collective-permute-start(f32[2,384]{1,0:T(2,128)} %bitcast.62), channel_id=1, source_target_pairs={{0,24},{8,16},{16,8},{24,0},{1,25},{9,17},{17,9},{25,1},{2,26},{10... | collective-permute-start | bytes 9224 | tf_op jit(solution)/shard_map/cond/branch_1_fun/ppermute | solution.py:23
  9.9 0.5 %collective-permute-start.1 = (f32[2,384]{1,0:T(2,128)}, f32[2,384]{1,0:T(2,128)S(1)}, u32[]{:S(2)}, u32[]{:S(2)}) collective-permute-start(f32[2,384]{1,0:T(2,128)} %bitcast.63), channel_id=1, source_target_pairs={{0,16},{8,24},{16,0},{24,8},{1,17},{9,25},{17,1},{25,9},{2,18},{10... | collective-permute-start | bytes 9224 | tf_op jit(solution)/shard_map/cond/branch_1_fun/ppermute | solution.py:23
  10.5 0.5 %collective-permute-start = (f32[2,384]{1,0:T(2,128)}, f32[2,384]{1,0:T(2,128)S(1)}, u32[]{:S(2)}, u32[]{:S(2)}) collective-permute-start(f32[2,384]{1,0:T(2,128)} %bitcast.64), channel_id=1, source_target_pairs={{0,8},{8,0},{16,24},{24,16},{1,9},{9,1},{17,25},{25,17},{2,10},{10... | collective-permute-start | bytes 9224 | tf_op jit(solution)/shard_map/cond/branch_1_fun/ppermute | solution.py:23
  11.0 1.8 %prepare.1 = (bf16[384,384]{1,0:T(8,128)(2,1)S(1)}, bf16[384,384]{1,0:T(8,128)(2,1)S(1)}, f32[6,384]{1,0:T(8,128)S(1)}, bf16[384,384]{1,0:T(8,128)(2,1)S(1)}, bf16[384,128]{1,0:T(8,128)(2,1)S(1)}) custom-call(bf16[384,384]{1,0:T(8,128)(2,1)} %get-tuple-element.81.query_ref, bf16[384,384]{1,0:T(8,128)(2,1)} %get-tuple-element.82.key_ref, ...), custom_call_target="tpu_custom_call" | custom-call | flops 226492416 | tf_op jit(solution)/shard_map/cond/branch_1_fun/prepare/pallas_call | solution.py:100
  12.8 0.0 collective-permute-done.2
  12.8 0.9 %collective-permute-done.1 = f32[2,384]{1,0:T(2,128)S(1)} collective-permute-done((f32[2,384]{1,0:T(2,128)}, f32[2,384]{1,0:T(2,128)S(1)}, u32[]{:S(2)}, u32[]{:S(2)}) %collective-permute-start.1) | collective-permute-done | bytes 3104 | tf_op jit(solution)/shard_map/cond/branch_1_fun/ppermute | solution.py:23
  13.8 0.5 %collective-permute-done = f32[2,384]{1,0:T(2,128)S(1)} collective-permute-done((f32[2,384]{1,0:T(2,128)}, f32[2,384]{1,0:T(2,128)S(1)}, u32[]{:S(2)}, u32[]{:S(2)}) %collective-permute-start) | collective-permute-done | bytes 3104 | tf_op jit(solution)/shard_map/cond/branch_1_fun/ppermute | solution.py:23
  14.3 0.7 %pad_maximum_fusion = f32[4,2,384]{2,1,0:T(2,128)S(1)} fusion(f32[1,2,384]{2,1,0:T(2,128)S(1)} %bitcast.65, f32[1,2,384]{2,1,0:T(2,128)S(1)} %bitcast.66, f32[1,2,384]{2,1,0:T(2,128)S(1)} %bitcast.67, f32[1,2,384]{2,1,0:T(2,128)} %get-tuple-element.31), kind=kLoop, calls=%fused_computation | loop fusion | flops 9216 | bytes 24576 | tf_op jit(solution)/shard_map/cond/branch_1_fun/stack | solution.py:343
  15.1 0.4 collective-permute-start.4
  15.5 2.2 %collective-permute-done.6.refs_4_ = bf16[320,384]{1,0:T(8,128)(2,1)S(1)} collective-permute-done((bf16[320,384]{1,0:T(8,128)(2,1)}, bf16[320,384]{1,0:T(8,128)(2,1)S(1)}, u32[]{:S(2)}, u32[]{:S(2)}) %collective-permute-start.6) | collective-permute-done | bytes 245792 | tf_op jit(solution)/shard_map/ppermute | solution.py:23
  17.6 0.4 collective-permute-start.10
  18.0 1.7 %collective-permute-done.4 = f32[2,384]{1,0:T(2,128)S(1)} collective-permute-done((f32[2,384]{1,0:T(2,128)S(1)}, f32[2,384]{1,0:T(2,128)S(1)}, u32[]{:S(2)}, u32[]{:S(2)}) %collective-permute-start.4) | collective-permute-done | bytes 3104 | tf_op jit(solution)/shard_map/ppermute | solution.py:23
  19.8 0.4 collective-permute-start.5
  20.2 0.0 collective-permute-start.9
  20.2 0.5 %collective-permute-start.8 = (bf16[320,384]{1,0:T(8,128)(2,1)S(1)}, bf16[320,384]{1,0:T(8,128)(2,1)S(1)}, u32[]{:S(2)}, u32[]{:S(2)}) collective-permute-start(bf16[320,384]{1,0:T(8,128)(2,1)S(1)} %collective-permute-done.7.refs_2_), channel_id=1, source_target_pairs={{0,1},{1,0},{2,3},{3,2},{4,5},{5,4},{6,7},{7,6},{8,9},{9,8},{10,11... | collective-permute-start | bytes 737288 | tf_op jit(solution)/shard_map/ppermute | solution.py:23
  20.7 3.1 %collective-permute-done.5 = f32[2,384]{1,0:T(2,128)S(1)} collective-permute-done((f32[2,384]{1,0:T(2,128)S(1)}, f32[2,384]{1,0:T(2,128)S(1)}, u32[]{:S(2)}, u32[]{:S(2)}) %collective-permute-start.5) | collective-permute-done | bytes 3104 | tf_op jit(solution)/shard_map/ppermute | solution.py:23
  23.9 0.0 collective-permute-done.10.refs_6_
  23.9 0.1 collective-permute-start.11
  24.1 0.0 collective-permute-done.8.refs_3_
  24.1 1.4 %collective-permute-done.11.refs_7_ = bf16[320,384]{1,0:T(8,128)(2,1)S(1)} collective-permute-done((bf16[320,384]{1,0:T(8,128)(2,1)S(1)}, bf16[320,384]{1,0:T(8,128)(2,1)S(1)}, u32[]{:S(2)}, u32[]{:S(2)}) %collective-permute-start.11) | collective-permute-done | bytes 245792 | tf_op jit(solution)/shard_map/ppermute | solution.py:23
  25.5 4.8 %attention.1 = (bf16[480,384]{1,0:T(8,128)(2,1)S(1)}, f32[32,2,128]{2,1,0:T(2,128)}) custom-call(s32[1]{0:T(128)} %bitcast.8.distance_ref, f32[2,384]{1,0:T(2,128)S(1)} %pad_maximum_fusion.5.stats_ref, bf16[384,384]{1,0:T(8,128)(2,1)S(1)} %get-tuple-element.60.qk_ref, bf16[384,384]{1,0:T(8,128)(2,1)S(1)} %get-tuple-element.61.vo_ref, ...), custom_call_target="tpu_custom_call" | custom-call | tf_op jit(solution)/shard_map/attention/pallas_call | solution.py:176
  30.3 1.5 %collective-permute-start.12 = (bf16[480,384]{1,0:T(8,128)(2,1)S(1)}, bf16[480,384]{1,0:T(8,128)(2,1)S(1)}, u32[]{:S(2)}, u32[]{:S(2)}) collective-permute-start(bf16[480,384]{1,0:T(8,128)(2,1)S(1)} %get-tuple-element.68.after.current_ref), channel_id=1, source_target_pairs={{0,8},{8,16},{16,24},{24,0},{1,9},{9,17},{17,25},{25,1},{2,10},{10... | collective-permute-start | bytes 1105928 | tf_op jit(solution)/shard_map/ppermute | solution.py:376
  31.8 4.8 %all-to-all-start = ((f32[32,2,128]{2,1,0:T(2,128)}), f32[32,2,128]{2,1,0:T(2,128)S(1)}, u32[]{:S(2)}, u32[]{:S(2)}) async-start(f32[32,2,128]{2,1,0:T(2,128)} %get-tuple-element.69), calls=%async_computation | async-start | bytes 65536 | tf_op jit(solution)/shard_map/all_to_all | solution.py:377
  36.6 0.1 add_convert_fusion.valid_ref
  36.7 1.8 %fetch.1.middle_ref = bf16[3,3,384,384]{3,2,1,0:T(8,128)(2,1)S(1)} custom-call(bf16[480,384]{1,0:T(8,128)(2,1)S(1)} %get-tuple-element.68.after.current_ref, bf16[3,3,3,384,384]{4,3,2,1,0:T(8,128)(2,1)} %weight_hbm.3), custom_call_target="tpu_custom_call" | custom-call | bytes 5308416 | tf_op jit(solution)/shard_map/fetch/pallas_call | solution.py:198
  38.5 5.4 %all-to-all-done.stats_ref = f32[32,2,128]{2,1,0:T(2,128)S(1)} async-done(((f32[32,2,128]{2,1,0:T(2,128)}), f32[32,2,128]{2,1,0:T(2,128)S(1)}, u32[]{:S(2)}, u32[]{:S(2)}) %all-to-all-start) | async-done | bytes 32800 | tf_op jit(solution)/shard_map/all_to_all | solution.py:377
  43.9 6.4 %upsample.1 = bf16[2,2,2,320,384]{4,3,2,1,0:T(8,128)(2,1)} custom-call(s32[2]{0:T(128)S(1)} %add_convert_fusion.valid_ref, bf16[480,384]{1,0:T(8,128)(2,1)S(1)} %get-tuple-element.68.after.current_ref, bf16[480,384]{1,0:T(8,128)(2,1)S(1)} %collective-permute-done.12.earlier_ref, f32[32,2,128]{2,1,0:T(2,128)S(1)} %all-to-all-done.stats_ref, ...), custom_call_target="tpu_custom_call" | custom-call | tf_op jit(solution)/shard_map/upsample/pallas_call | solution.py:288
  (25 shorter events, 0.2 us)
Async XLA Ops:
  0.0 5.6 %collective-permute-start.3 = (bf16[320,384]{1,0:T(8,128)(2,1)}, bf16[320,384]{1,0:T(8,128)(2,1)S(1)}, u32[]{:S(2)}, u32[]{:S(2)}) collective-permute-start(bf16[320,384]{1,0:T(8,128)(2,1)} %bitcast.58), channel_id=1, source_target_pairs={{0,1},{1,0},{2,3},{3,2},{4,5},{5,4},{6,7},{7,6},{8,9},{9,8},{10,11... | collective-permute-start | bytes 737288 | tf_op jit(solution)/shard_map/ppermute | solution.py:23
  0.5 15.0 %collective-permute-start.7 = (bf16[320,384]{1,0:T(8,128)(2,1)}, bf16[320,384]{1,0:T(8,128)(2,1)S(1)}, u32[]{:S(2)}, u32[]{:S(2)}) collective-permute-start(bf16[320,384]{1,0:T(8,128)(2,1)} %bitcast.59), channel_id=1, source_target_pairs={{0,2},{1,3},{2,0},{3,1},{4,6},{5,7},{6,4},{7,5},{8,10},{9,11},{10,... | collective-permute-start | bytes 737288 | tf_op jit(solution)/shard_map/ppermute | solution.py:23
  3.0 14.6 %collective-permute-start.6 = (bf16[320,384]{1,0:T(8,128)(2,1)}, bf16[320,384]{1,0:T(8,128)(2,1)S(1)}, u32[]{:S(2)}, u32[]{:S(2)}) collective-permute-start(bf16[320,384]{1,0:T(8,128)(2,1)} %bitcast.60), channel_id=1, source_target_pairs={{0,4},{1,5},{2,6},{3,7},{4,0},{5,1},{6,2},{7,3},{8,12},{9,13},{10,... | collective-permute-start | bytes 737288 | tf_op jit(solution)/shard_map/ppermute | solution.py:23
  7.4 5.4 %collective-permute-start.2 = (f32[2,384]{1,0:T(2,128)}, f32[2,384]{1,0:T(2,128)S(1)}, u32[]{:S(2)}, u32[]{:S(2)}) collective-permute-start(f32[2,384]{1,0:T(2,128)} %bitcast.62), channel_id=1, source_target_pairs={{0,24},{8,16},{16,8},{24,0},{1,25},{9,17},{17,9},{25,1},{2,26},{10... | collective-permute-start | bytes 9224 | tf_op jit(solution)/shard_map/cond/branch_1_fun/ppermute | solution.py:23
  9.9 3.8 %collective-permute-start.1 = (f32[2,384]{1,0:T(2,128)}, f32[2,384]{1,0:T(2,128)S(1)}, u32[]{:S(2)}, u32[]{:S(2)}) collective-permute-start(f32[2,384]{1,0:T(2,128)} %bitcast.63), channel_id=1, source_target_pairs={{0,16},{8,24},{16,0},{24,8},{1,17},{9,25},{17,1},{25,9},{2,18},{10... | collective-permute-start | bytes 9224 | tf_op jit(solution)/shard_map/cond/branch_1_fun/ppermute | solution.py:23
  10.5 3.8 %collective-permute-start = (f32[2,384]{1,0:T(2,128)}, f32[2,384]{1,0:T(2,128)S(1)}, u32[]{:S(2)}, u32[]{:S(2)}) collective-permute-start(f32[2,384]{1,0:T(2,128)} %bitcast.64), channel_id=1, source_target_pairs={{0,8},{8,0},{16,24},{24,16},{1,9},{9,1},{17,25},{25,17},{2,10},{10... | collective-permute-start | bytes 9224 | tf_op jit(solution)/shard_map/cond/branch_1_fun/ppermute | solution.py:23
  15.1 4.7 %collective-permute-start.4 = (f32[2,384]{1,0:T(2,128)S(1)}, f32[2,384]{1,0:T(2,128)S(1)}, u32[]{:S(2)}, u32[]{:S(2)}) collective-permute-start(f32[2,384]{1,0:T(2,128)S(1)} %get-tuple-element.59), channel_id=1, source_target_pairs={{0,4},{1,5},{2,6},{3,7},{4,0},{5,1},{6,2},{7,3},{8,12},{9,13},{10,... | collective-permute-start | bytes 9224 | tf_op jit(solution)/shard_map/ppermute | solution.py:23
  17.6 6.3 %collective-permute-start.10 = (bf16[320,384]{1,0:T(8,128)(2,1)S(1)}, bf16[320,384]{1,0:T(8,128)(2,1)S(1)}, u32[]{:S(2)}, u32[]{:S(2)}) collective-permute-start(bf16[320,384]{1,0:T(8,128)(2,1)S(1)} %collective-permute-done.6.refs_4_), channel_id=1, source_target_pairs={{0,2},{1,3},{2,0},{3,1},{4,6},{5,7},{6,4},{7,5},{8,10},{9,11},{10,... | collective-permute-start | bytes 737288 | tf_op jit(solution)/shard_map/ppermute | solution.py:23
  19.8 4.1 %collective-permute-start.5 = (f32[2,384]{1,0:T(2,128)S(1)}, f32[2,384]{1,0:T(2,128)S(1)}, u32[]{:S(2)}, u32[]{:S(2)}) collective-permute-start(f32[2,384]{1,0:T(2,128)S(1)} %get-tuple-element.100), channel_id=1, source_target_pairs={{0,2},{1,3},{2,0},{3,1},{4,6},{5,7},{6,4},{7,5},{8,10},{9,11},{10,... | collective-permute-start | bytes 9224 | tf_op jit(solution)/shard_map/ppermute | solution.py:23
  20.2 3.8 %collective-permute-start.9 = (bf16[320,384]{1,0:T(8,128)(2,1)S(1)}, bf16[320,384]{1,0:T(8,128)(2,1)S(1)}, u32[]{:S(2)}, u32[]{:S(2)}) collective-permute-start(bf16[320,384]{1,0:T(8,128)(2,1)S(1)} %collective-permute-done.6.refs_4_), channel_id=1, source_target_pairs={{0,1},{1,0},{2,3},{3,2},{4,5},{5,4},{6,7},{7,6},{8,9},{9,8},{10,11... | collective-permute-start | bytes 737288 | tf_op jit(solution)/shard_map/ppermute | solution.py:23
  20.2 3.8 %collective-permute-start.8 = (bf16[320,384]{1,0:T(8,128)(2,1)S(1)}, bf16[320,384]{1,0:T(8,128)(2,1)S(1)}, u32[]{:S(2)}, u32[]{:S(2)}) collective-permute-start(bf16[320,384]{1,0:T(8,128)(2,1)S(1)} %collective-permute-done.7.refs_2_), channel_id=1, source_target_pairs={{0,1},{1,0},{2,3},{3,2},{4,5},{5,4},{6,7},{7,6},{8,9},{9,8},{10,11... | collective-permute-start | bytes 737288 | tf_op jit(solution)/shard_map/ppermute | solution.py:23
  23.9 1.6 %collective-permute-start.11 = (bf16[320,384]{1,0:T(8,128)(2,1)S(1)}, bf16[320,384]{1,0:T(8,128)(2,1)S(1)}, u32[]{:S(2)}, u32[]{:S(2)}) collective-permute-start(bf16[320,384]{1,0:T(8,128)(2,1)S(1)} %collective-permute-done.10.refs_6_), channel_id=1, source_target_pairs={{0,1},{1,0},{2,3},{3,2},{4,5},{5,4},{6,7},{7,6},{8,9},{9,8},{10,11... | collective-permute-start | bytes 737288 | tf_op jit(solution)/shard_map/ppermute | solution.py:23
  30.3 13.6 %collective-permute-start.12 = (bf16[480,384]{1,0:T(8,128)(2,1)S(1)}, bf16[480,384]{1,0:T(8,128)(2,1)S(1)}, u32[]{:S(2)}, u32[]{:S(2)}) collective-permute-start(bf16[480,384]{1,0:T(8,128)(2,1)S(1)} %get-tuple-element.68.after.current_ref), channel_id=1, source_target_pairs={{0,8},{8,16},{16,24},{24,0},{1,9},{9,17},{17,25},{25,1},{2,10},{10... | collective-permute-start | bytes 1105928 | tf_op jit(solution)/shard_map/ppermute | solution.py:376
  31.8 12.1 %all-to-all-start = ((f32[32,2,128]{2,1,0:T(2,128)}), f32[32,2,128]{2,1,0:T(2,128)S(1)}, u32[]{:S(2)}, u32[]{:S(2)}) async-start(f32[32,2,128]{2,1,0:T(2,128)} %get-tuple-element.69), calls=%async_computation | async-start | bytes 65536 | tf_op jit(solution)/shard_map/all_to_all | solution.py:377
